TPU v7x, 128 devices: a whole 4x4x4 slice. The times are simulated.
128 devices in a mesh: dp: 16 (over z, x), ctx: 8 (over y, core).
Axes of the slice: x: 4, y: 4, z: 4, core: 2. Of those that a mesh axis runs over, the one named last changes fastest.
Arguments:
- tokens: bfloat16 [16, 1, 2048, 2560], P('dp', None, 'ctx'), may hold values from -6 to 6
- target: bfloat16 [16, 1, 2048, 2560], P('dp', None, 'ctx'), may hold values from -6 to 6
- rewards: float32 [16, 1, 2048], P('dp', None, 'ctx'), may hold values from 0.25 to 4
- doc_lengths: int32 [16, 1, 5], P('dp'), may hold values from 1 to 1024, 2048 in all within a row
- norm_gain: float32 [2560], replicated, may hold values from 0.1 to 1.9
- w_query: bfloat16 [2560, 1024], P(('dp', 'ctx')), as said below
- w_key: bfloat16 [2560, 512], P(('dp', 'ctx')), as said below
- w_value: bfloat16 [2560, 512], P(('dp', 'ctx')), may hold values from -0.125 to 0.125
- w_out: bfloat16 [1024, 2560], P(('dp', 'ctx')), may hold values from -0.1875 to 0.1875
- gossip_bit: int32 [16], P('dp'), may hold values from 0 to 3, as said below
Outputs:
- grad_query: float32 [16, 2560, 1024], P('dp', 'ctx')
- grad_key: float32 [16, 2560, 512], P('dp', 'ctx')
- grad_value: float32 [16, 2560, 512], P('dp', 'ctx')
- grad_out: float32 [16, 1024, 2560], P('dp', 'ctx')
Inputs may be any that keep to these rules, and one draw needn't show every extreme that they name: `doc_lengths`: the lengths of one sequence sum to 2048; the longest is exactly 1024. `gossip_bit`: every bit from 0 to 3 is named by some group. `w_query`: a projection's weights. `w_key`: a projection's weights.
All inputs are finite; a program needn't handle non-finite values.
Results may differ from a plain program's by a relative error of at most 0.019.
The roundings to bfloat16 on the way count: a program that leaves them out, or rounds other values in their place, can miss the bound.
Values may be sent and summed in bfloat16 or wider, within the bound.
A program may use at most 128 MiB of HBM per device.

v0:
```python
import jax
import jax.numpy as jnp
from jax import lax
from jax.sharding import PartitionSpec as P

QUERY_HEADS = 4
KEY_VALUE_HEADS = 2
HEAD_DIM = 256
WINDOW = 1024


epsilon = 1e-06
masked_score = -1e30


def partner(value, axis, bit):
    mask = 2**bit
    pairs = [(source, source ^ mask) for source in range(lax.axis_size(axis))]
    return lax.ppermute(value, axis, pairs)


def shifted(block, axis, distance):
    devices = range(lax.axis_size(axis))
    route = [(i - distance, i) for i in devices if i - distance in devices]
    return lax.ppermute(block, axis, route)


def norm_rows(inputs, norm_gain):
    values = inputs.astype(jnp.float32)
    power = jnp.mean(values * values, axis=-1, keepdims=True)
    return (values * lax.rsqrt(power + epsilon) * norm_gain).astype(jnp.bfloat16)


def doc_index(positions, lengths):
    endings = jnp.cumsum(lengths, axis=-1)
    return jnp.sum((endings[:, None, :] <= positions[:, :, None]).astype(jnp.int32), axis=-1)


def allowed(query_pos, key_pos, lengths):
    query_doc = doc_index(query_pos, lengths)
    key_doc = doc_index(key_pos, lengths)
    distance = query_pos[:, :, None] - key_pos[:, None, :]
    same_doc = query_doc[:, :, None] == key_doc[:, None, :]
    return (key_pos[:, None, :] >= 0) & same_doc & (distance >= 0) & (distance < WINDOW)


def split_heads(query_rows, key_tile, value_tile):
    batch_count, query_length, _ = query_rows.shape
    key_length = key_tile.shape[1]
    query_heads = query_rows.reshape(
        batch_count, query_length, KEY_VALUE_HEADS, QUERY_HEADS // KEY_VALUE_HEADS, HEAD_DIM
    )
    key_heads = key_tile.reshape(batch_count, key_length, KEY_VALUE_HEADS, HEAD_DIM)
    value_heads = value_tile.reshape(batch_count, key_length, KEY_VALUE_HEADS, HEAD_DIM)
    return (query_heads, key_heads, value_heads)


def attend(query_rows, key_tile, value_tile, mask):
    query_heads, key_heads, value_heads = split_heads(query_rows, key_tile, value_tile)
    scores = jnp.einsum(
        "btkgd,bskd->bkgts", query_heads, key_heads, preferred_element_type=jnp.float32
    ) * HEAD_DIM ** (-0.5)
    allowed_mask = mask[:, None, None, :, :]
    scores = jnp.where(allowed_mask, scores, masked_score)
    row_max = jnp.max(scores, axis=-1, keepdims=True)
    raised = jnp.where(allowed_mask, jnp.exp(scores - row_max), 0.0)
    attn_probs = (raised / jnp.sum(raised, axis=-1, keepdims=True)).astype(jnp.bfloat16)
    mixed_heads = jnp.einsum(
        "bkgts,bskd->btkgd", attn_probs, value_heads, preferred_element_type=jnp.float32
    )
    return (
        attn_probs,
        mixed_heads.reshape(
            query_rows.shape[0], query_rows.shape[1], QUERY_HEADS * HEAD_DIM
        ).astype(jnp.bfloat16),
    )


def attend_back(query_rows, key_tile, value_tile, attn_probs, blended_block, blended_gradient):
    query_heads, key_heads, value_heads = split_heads(query_rows, key_tile, value_tile)
    batch_count, query_length, _ = query_rows.shape
    key_length = key_tile.shape[1]
    gradient_heads = blended_gradient.reshape(
        batch_count, query_length, KEY_VALUE_HEADS, QUERY_HEADS // KEY_VALUE_HEADS, HEAD_DIM
    )
    output_heads = blended_block.reshape(
        batch_count, query_length, KEY_VALUE_HEADS, QUERY_HEADS // KEY_VALUE_HEADS, HEAD_DIM
    )
    prob_grads = jnp.einsum(
        "btkgd,bskd->bkgts", gradient_heads, value_heads, preferred_element_type=jnp.float32
    )
    row_dots = jnp.sum(
        gradient_heads.astype(jnp.float32) * output_heads.astype(jnp.float32), axis=-1
    )
    row_dots = jnp.transpose(row_dots, (0, 2, 3, 1))[..., None]
    score_grads = (
        attn_probs.astype(jnp.float32) * (prob_grads - row_dots) * HEAD_DIM ** (-0.5)
    ).astype(jnp.bfloat16)
    query_gradients = jnp.einsum(
        "bkgts,bskd->btkgd", score_grads, key_heads, preferred_element_type=jnp.float32
    )
    key_gradients = jnp.einsum(
        "bkgts,btkgd->bskd", score_grads, query_heads, preferred_element_type=jnp.float32
    )
    value_gradients = jnp.einsum(
        "bkgts,btkgd->bskd", attn_probs, gradient_heads, preferred_element_type=jnp.float32
    )
    return (
        query_gradients.reshape(batch_count, query_length, QUERY_HEADS * HEAD_DIM).astype(
            jnp.bfloat16
        ),
        key_gradients.reshape(batch_count, key_length, KEY_VALUE_HEADS * HEAD_DIM).astype(
            jnp.bfloat16
        ),
        value_gradients.reshape(batch_count, key_length, KEY_VALUE_HEADS * HEAD_DIM).astype(
            jnp.bfloat16
        ),
    )


def trade(shard_pair, bit_number):
    return partner((shard_pair[0], shard_pair[1]), "dp", bit_number)


def per_device(
    tokens, target, rewards, doc_lengths, norm_gain, w_query, w_key, w_value, w_out, gossip_bit
):
    seq_count, shard_len, model_width = (tokens.shape[1], tokens.shape[2], tokens.shape[3])
    query_width = w_query.shape[1]
    key_feature_width = w_key.shape[1]
    row_count = seq_count * shard_len
    reach_blocks = WINDOW // shard_len
    span_len = (reach_blocks + 1) * shard_len
    ctx_index = lax.axis_index("ctx")
    lengths = doc_lengths[0]
    normed = norm_rows(tokens[0], norm_gain)
    flat_rows = normed.reshape(row_count, model_width)
    pieces = (
        lax.all_gather(w_query, ("dp", "ctx"), axis=0, tiled=True),
        lax.all_gather(w_key, ("dp", "ctx"), axis=0, tiled=True),
        lax.all_gather(w_value, ("dp", "ctx"), axis=0, tiled=True),
    )
    columns = flat_rows
    query_sum, key_sum, value_sum = tuple(
        (
            jnp.dot(columns, weight_piece, preferred_element_type=jnp.float32)
            for weight_piece in pieces
        )
    )
    query_rows = query_sum.astype(jnp.bfloat16).reshape(seq_count, shard_len, query_width)
    key_own = key_sum.astype(jnp.bfloat16).reshape(seq_count, shard_len, key_feature_width)
    value_own = value_sum.astype(jnp.bfloat16).reshape(seq_count, shard_len, key_feature_width)
    key_parts = []
    value_parts = []
    for offset in range(reach_blocks, 0, -1):
        moved = shifted((key_own, value_own), "ctx", offset)
        key_parts.append(moved[0])
        value_parts.append(moved[1])
    key_tile = jnp.concatenate(key_parts + [key_own], axis=1)
    value_tile = jnp.concatenate(value_parts + [value_own], axis=1)
    query_pos = jnp.broadcast_to(
        ctx_index * shard_len + jnp.arange(shard_len, dtype=jnp.int32), (seq_count, shard_len)
    )
    key_pos = jnp.broadcast_to(
        (ctx_index - reach_blocks) * shard_len + jnp.arange(span_len, dtype=jnp.int32),
        (seq_count, span_len),
    )
    mask = allowed(query_pos, key_pos, lengths)
    attn_probs, mixed_heads = attend(query_rows, key_tile, value_tile, mask)
    mixed_flat = mixed_heads.reshape(row_count, query_width)
    out_whole = lax.all_gather(w_out, ("dp", "ctx"), axis=0, tiled=True)
    update = jnp.dot(mixed_flat, out_whole, preferred_element_type=jnp.float32)
    result = tokens[0].reshape(row_count, model_width).astype(jnp.float32) + update
    delta_rows = (
        rewards[0].reshape(row_count, 1)
        * (result - target[0].reshape(row_count, model_width).astype(jnp.float32))
    ).astype(jnp.bfloat16)
    blended_gradient = lax.dot_general(
        delta_rows, out_whole, (((1,), (1,)), ((), ())), preferred_element_type=jnp.float32
    )
    blended_gradient = blended_gradient.astype(jnp.bfloat16).reshape(
        seq_count, shard_len, query_width
    )
    query_gradients, key_terms, value_terms = attend_back(
        query_rows, key_tile, value_tile, attn_probs, mixed_heads, blended_gradient
    )
    own_start = reach_blocks * shard_len
    key_total = key_terms[:, own_start:].astype(jnp.float32)
    value_total = value_terms[:, own_start:].astype(jnp.float32)
    for offset in range(1, reach_blocks + 1):
        low_row = (reach_blocks - offset) * shard_len
        returned = shifted(
            (
                key_terms[:, low_row : low_row + shard_len],
                value_terms[:, low_row : low_row + shard_len],
            ),
            "ctx",
            -offset,
        )
        key_total = key_total + returned[0].astype(jnp.float32)
        value_total = value_total + returned[1].astype(jnp.float32)
    key_final = key_total.astype(jnp.bfloat16)
    value_final = value_total.astype(jnp.bfloat16)
    joined = jnp.concatenate([query_gradients, key_final, value_final], axis=-1).reshape(
        row_count, query_width + 2 * key_feature_width
    )
    columns = flat_rows
    partial_term = lax.dot_general(
        columns, joined, (((0,), (0,)), ((), ())), preferred_element_type=jnp.float32
    )
    grad_inputs = lax.psum_scatter(
        lax.optimization_barrier(partial_term.astype(jnp.bfloat16))
        .astype(jnp.float32)
        .astype(jnp.bfloat16),
        "ctx",
        scatter_dimension=0,
        tiled=True,
    )
    columns = mixed_flat
    partial_term = lax.dot_general(
        columns, delta_rows, (((0,), (0,)), ((), ())), preferred_element_type=jnp.float32
    )
    grad_outputs = lax.psum_scatter(
        lax.optimization_barrier(partial_term.astype(jnp.bfloat16))
        .astype(jnp.float32)
        .astype(jnp.bfloat16),
        "ctx",
        scatter_dimension=0,
        tiled=True,
    )
    level_count = lax.axis_size("dp").bit_length() - 1
    own_bit = gossip_bit[0]
    partner_inputs = grad_inputs
    partner_outputs = grad_outputs
    for level_number in range(level_count):
        moved_pair = trade((grad_inputs, grad_outputs), level_number)
        picked = own_bit == level_number
        partner_inputs = jnp.where(picked, moved_pair[0], partner_inputs)
        partner_outputs = jnp.where(picked, moved_pair[1], partner_outputs)
    mean_inputs = (grad_inputs.astype(jnp.float32) + partner_inputs.astype(jnp.float32)) * 0.5
    mean_outputs = (grad_outputs.astype(jnp.float32) + partner_outputs.astype(jnp.float32)) * 0.5
    return (
        mean_inputs[None, :, :query_width],
        mean_inputs[None, :, query_width : query_width + key_feature_width],
        mean_inputs[None, :, query_width + key_feature_width :],
        mean_outputs[None],
    )


def solution(mesh):
    placed = (
        P("dp", None, "ctx", None),
        P("dp", None, "ctx", None),
        P("dp", None, "ctx"),
        P("dp", None, None),
        P(),
        P(("dp", "ctx"), None),
        P(("dp", "ctx"), None),
        P(("dp", "ctx"), None),
        P(("dp", "ctx"), None),
        P("dp"),
    )
    return jax.shard_map(
        per_device,
        mesh=mesh,
        in_specs=placed,
        out_specs=(
            P("dp", "ctx", None),
            P("dp", "ctx", None),
            P("dp", "ctx", None),
            P("dp", "ctx", None),
        ),
        check_vma=False,
    )
```

profile of v0, /device:TPU:0, one launch (start us, length us, event | category | flops | bytes accessed | tf_op | source)
XLA Modules:
  0.0 512.9 jit_solution(3897365908669054505)
XLA Ops:
  12.8 66.7 %all-gather.10.cloned.1.call-done = bf16[128,20,512]{2,1,0:T(8,128)(2,1)} async-done(((bf16[1,20,512]{2,1,0:T(8,128)(2,1)}), bf16[128,20,512]{2,1,0:T(8,128)(2,1)}) %all-gather.10.cloned.1.call-update) | async-done | bytes 2621456 | tf_op jit(solution)/shard_map/all_gather | solution.py:140
  79.5 5.2 %reshape.511 = bf16[2560,512]{1,0:T(8,128)(2,1)} reshape(bf16[128,20,512]{2,1,0:T(8,128)(2,1)} %all-gather.10.cloned.1.call-done) | data formatting | bytes 5242880
  84.7 3.3 convolution_convert_fusion.5
  88.0 3.4 collective-permute-start
  93.2 55.6 %all-gather.14.cloned.1.call-done = bf16[128,20,512]{2,1,0:T(8,128)(2,1)} async-done(((bf16[1,20,512]{2,1,0:T(8,128)(2,1)}), bf16[128,20,512]{2,1,0:T(8,128)(2,1)}) %all-gather.14.cloned.1.call-update) | async-done | bytes 2621456 | tf_op jit(solution)/shard_map/all_gather | solution.py:141
  148.8 5.2 %reshape.515 = bf16[2560,512]{1,0:T(8,128)(2,1)} reshape(bf16[128,20,512]{2,1,0:T(8,128)(2,1)} %all-gather.14.cloned.1.call-done) | data formatting | bytes 5242880
  154.0 3.3 convolution_convert_fusion.4
  157.3 3.4 collective-permute-start.4
  161.8 2.9 collective-permute-start.2
  172.0 4.1 collective-permute-start.6
  176.2 3.8 collective-permute-start.7
  196.5 23.2 %all-gather.12.cloned.1.call-done = bf16[128,20,1024]{2,1,0:T(8,128)(2,1)} async-done(((bf16[1,20,1024]{2,1,0:T(8,128)(2,1)}), bf16[128,20,1024]{2,1,0:T(8,128)(2,1)}) %all-gather.12.cloned.1.call-update) | async-done | bytes 5242896 | tf_op jit(solution)/shard_map/all_gather | solution.py:139
  219.6 9.0 %reshape.513 = bf16[2560,1024]{1,0:T(8,128)(2,1)} reshape(bf16[128,20,1024]{2,1,0:T(8,128)(2,1)} %all-gather.12.cloned.1.call-done) | data formatting | bytes 10485760
  228.6 4.1 convolution_convert_fusion.3
  232.9 2.4 fusion.50
  238.5 49.1 %all-gather.8.cloned.1.call-done = bf16[1024,2560]{1,0:T(8,128)(2,1)} async-done(((bf16[8,2560]{1,0:T(8,128)(2,1)}), bf16[1024,2560]{1,0:T(8,128)(2,1)}) %all-gather.8.cloned.1.call-update) | async-done | bytes 5242896 | tf_op jit(solution)/shard_map/all_gather | solution.py:171
  287.6 4.9 fusion.6
  293.7 3.8 convolution_convert_fusion.1
  297.5 5.2 %convolution_convert_fusion.2 = bf16[256,1024]{1,0:T(8,128)(2,1)} fusion(bf16[256,2560]{1,0:T(8,128)(2,1)} %copy-done.2, bf16[1024,2560]{1,0:T(8,128)(2,1)} %all-gather.8.cloned.1.call-done), kind=kOutput, calls=%fused_computation.46 | convolution fusion | flops 1342439424 | bytes 7077888 | tf_op jit(solution)/shard_map/dot_general | solution.py:178
  319.5 4.8 collective-permute-done.15
  328.4 9.9 %collective-permute-done.11 = bf16[1,256,512]{1,2,0:T(8,128)(2,1)S(1)} collective-permute-done((bf16[1,256,512]{1,2,0:T(8,128)(2,1)S(1)}, bf16[1,256,512]{1,2,0:T(8,128)(2,1)S(1)}, u32[]{:S(2)}, u32[]{:S(2)}) %collective-permute-start.11) | collective-permute-done | bytes 262176 | tf_op jit(solution)/shard_map/ppermute | solution.py:25
  339.2 5.3 %collective-permute-done.9 = bf16[1,256,512]{1,2,0:T(8,128)(2,1)S(1)} collective-permute-done((bf16[1,256,512]{1,2,0:T(8,128)(2,1)S(1)}, bf16[1,256,512]{1,2,0:T(8,128)(2,1)S(1)}, u32[]{:S(2)}, u32[]{:S(2)}) %collective-permute-start.9) | collective-permute-done | bytes 262176 | tf_op jit(solution)/shard_map/ppermute | solution.py:25
  344.6 6.9 %convolution_convert_fusion = bf16[2560,2048]{1,0:T(8,128)(2,1)} fusion(bf16[1,1,256,2560]{3,2,1,0:T(8,128)(2,1)S(1)} %copy-done.1, f32[2560]{0:T(1024)S(1)} %copy-done.13, f32[256]{0:T(256)S(1)} %add_rsqrt_fusion, bf16[1,256,512]{1,2,0:T(8,128)(2,1)S(1)} %add_convert_fusion, bf16[1,256,512]{1,2,0:T(8,128)(2,1)S(1)} %add_convert_fusion.1, ...), kind=kOutput, calls=%fused_computation | convolution fusion | flops 2695364608 | bytes 12856320 | tf_op jit(solution)/shard_map/dot_general | solution.py:208
  351.6 3.5 collective-permute-start.20
  355.5 4.8 collective-permute-start.22
  360.6 79.5 %reduce-scatter.3.cloned.1.call-done = bf16[320,2048]{1,0:T(8,128)(2,1)} async-done(((bf16[2560,2048]{1,0:T(8,128)(2,1)}), bf16[320,2048]{1,0:T(8,128)(2,1)}) %reduce-scatter.3.cloned.1.call-update) | async-done | bytes 1310736 | tf_op jit(solution)/shard_map/reduce_scatter | solution.py:211
  440.1 3.2 collective-permute-start.16
  444.0 3.0 collective-permute-start.18
  448.2 2.7 multiply_bitcast_fusion
  450.9 22.7 %collective-permute-done.16 = bf16[320,2048]{1,0:T(8,128)(2,1)S(1)} collective-permute-done((bf16[320,2048]{1,0:T(8,128)(2,1)}, bf16[320,2048]{1,0:T(8,128)(2,1)S(1)}, u32[]{:S(2)}, u32[]{:S(2)}) %collective-permute-start.16) | collective-permute-done | bytes 1310752 | tf_op jit(solution)/shard_map/ppermute | solution.py:19
  473.6 26.6 %collective-permute-done.17 = bf16[320,2048]{1,0:T(8,128)(2,1)S(1)} collective-permute-done((bf16[320,2048]{1,0:T(8,128)(2,1)}, bf16[320,2048]{1,0:T(8,128)(2,1)S(1)}, u32[]{:S(2)}, u32[]{:S(2)}) %collective-permute-start.17) | collective-permute-done | bytes 1310752 | tf_op jit(solution)/shard_map/ppermute | solution.py:19
  500.2 3.0 collective-permute-done.19
  (119 shorter events, 63.0 us)
Async XLA Ops:
  7.2 72.3 %all-gather.10.cloned.1.call-start = ((), (), s32[]{:S(2)}) async-start(), calls=%async_computation.5 | async-start | bytes 3170304 | tf_op jit(solution)/shard_map/all_gather | solution.py:140
  7.9 140.9 %all-gather.14.cloned.1.call-start = ((), (), s32[]{:S(2)}) async-start(), calls=%async_computation.7 | async-start | bytes 3170304 | tf_op jit(solution)/shard_map/all_gather | solution.py:141
  8.6 211.0 %all-gather.12.cloned.1.call-start = ((), (), s32[]{:S(2)}) async-start(), calls=%async_computation.6 | async-start | bytes 6340608 | tf_op jit(solution)/shard_map/all_gather | solution.py:139
  9.4 278.3 %all-gather.8.cloned.1.call-start = ((), (), s32[]{:S(2)}) async-start(), calls=%async_computation.2 | async-start | bytes 5283840 | tf_op jit(solution)/shard_map/all_gather | solution.py:171
  10.0 341.6 %reduce-scatter.5.cloned.1.call-start = ((), (), s32[]{:S(2)}) async-start(), calls=%async_computation.4 | async-start | bytes 5898240 | tf_op jit(solution)/shard_map/reduce_scatter | solution.py:223
  12.7 71.9 %copy-start = (bf16[1,1,256,2560]{3,2,1,0:T(8,128)(2,1)S(1)}, bf16[1,1,256,2560]{3,2,1,0:T(8,128)(2,1)}, u32[]{:S(2)}) copy-start(bf16[1,1,256,2560]{3,2,1,0:T(8,128)(2,1)} %param.10) | copy-start | bytes 3932164
  12.7 71.9 %copy-start.13 = (f32[2560]{0:T(1024)S(1)}, f32[2560]{0:T(1024)}, u32[]{:S(2)}) copy-start(f32[2560]{0:T(1024)} %param.14) | copy-start | bytes 30724
  88.0 84.0 %collective-permute-start = (bf16[1,256,512]{2,1,0:T(8,128)(2,1)}, bf16[1,256,512]{2,1,0:T(8,128)(2,1)S(1)}, u32[]{:S(2)}, u32[]{:S(2)}) collective-permute-start(bf16[1,256,512]{2,1,0:T(8,128)(2,1)} %bitcast.3), channel_id=1, source_target_pairs={{0,4},{1,5},{2,6},{3,7},{8,12},{9,13},{10,14},{11,15},{16,20},{17,... | collective-permute-start | bytes 786440 | tf_op jit(solution)/shard_map/ppermute | solution.py:25
  91.4 84.8 %collective-permute-start.1 = (bf16[1,256,512]{2,1,0:T(8,128)(2,1)}, bf16[1,256,512]{2,1,0:T(8,128)(2,1)S(1)}, u32[]{:S(2)}, u32[]{:S(2)}) collective-permute-start(bf16[1,256,512]{2,1,0:T(8,128)(2,1)} %bitcast.3), channel_id=1, source_target_pairs={{0,3},{1,4},{2,5},{3,6},{4,7},{8,11},{9,12},{10,13},{11,14},{12,15... | collective-permute-start | bytes 786440 | tf_op jit(solution)/shard_map/ppermute | solution.py:25
  157.3 11.8 %collective-permute-start.4 = (bf16[1,256,512]{2,1,0:T(8,128)(2,1)}, bf16[1,256,512]{2,1,0:T(8,128)(2,1)S(1)}, u32[]{:S(2)}, u32[]{:S(2)}) collective-permute-start(bf16[1,256,512]{2,1,0:T(8,128)(2,1)} %bitcast.14), channel_id=1, source_target_pairs={{0,4},{1,5},{2,6},{3,7},{8,12},{9,13},{10,14},{11,15},{16,20},{17,... | collective-permute-start | bytes 786440 | tf_op jit(solution)/shard_map/ppermute | solution.py:25
  161.8 30.3 %collective-permute-start.2 = (bf16[1,256,512]{2,1,0:T(8,128)(2,1)}, bf16[1,256,512]{2,1,0:T(8,128)(2,1)}, u32[]{:S(2)}, u32[]{:S(2)}) collective-permute-start(bf16[1,256,512]{2,1,0:T(8,128)(2,1)} %bitcast.3), channel_id=1, source_target_pairs={{0,2},{1,3},{2,4},{3,5},{4,6},{5,7},{8,10},{9,11},{10,12},{11,13},... | collective-permute-start | bytes 786440 | tf_op jit(solution)/shard_map/ppermute | solution.py:25
  164.7 29.3 %collective-permute-start.3 = (bf16[1,256,512]{2,1,0:T(8,128)(2,1)}, bf16[1,256,512]{2,1,0:T(8,128)(2,1)}, u32[]{:S(2)}, u32[]{:S(2)}) collective-permute-start(bf16[1,256,512]{2,1,0:T(8,128)(2,1)} %bitcast.3), channel_id=1, source_target_pairs={{0,1},{1,2},{2,3},{3,4},{4,5},{5,6},{6,7},{8,9},{9,10},{10,11},{11... | collective-permute-start | bytes 786440 | tf_op jit(solution)/shard_map/ppermute | solution.py:25
  169.1 12.9 %collective-permute-start.5 = (bf16[1,256,512]{2,1,0:T(8,128)(2,1)}, bf16[1,256,512]{2,1,0:T(8,128)(2,1)}, u32[]{:S(2)}, u32[]{:S(2)}) collective-permute-start(bf16[1,256,512]{2,1,0:T(8,128)(2,1)} %bitcast.14), channel_id=1, source_target_pairs={{0,3},{1,4},{2,5},{3,6},{4,7},{8,11},{9,12},{10,13},{11,14},{12,15... | collective-permute-start | bytes 786440 | tf_op jit(solution)/shard_map/ppermute | solution.py:25
  172.0 13.6 %collective-permute-start.6 = (bf16[1,256,512]{2,1,0:T(8,128)(2,1)}, bf16[1,256,512]{2,1,0:T(8,128)(2,1)}, u32[]{:S(2)}, u32[]{:S(2)}) collective-permute-start(bf16[1,256,512]{2,1,0:T(8,128)(2,1)} %bitcast.14), channel_id=1, source_target_pairs={{0,2},{1,3},{2,4},{3,5},{4,6},{5,7},{8,10},{9,11},{10,12},{11,13},... | collective-permute-start | bytes 786440 | tf_op jit(solution)/shard_map/ppermute | solution.py:25
  176.2 13.2 %collective-permute-start.7 = (bf16[1,256,512]{2,1,0:T(8,128)(2,1)}, bf16[1,256,512]{2,1,0:T(8,128)(2,1)}, u32[]{:S(2)}, u32[]{:S(2)}) collective-permute-start(bf16[1,256,512]{2,1,0:T(8,128)(2,1)} %bitcast.14), channel_id=1, source_target_pairs={{0,1},{1,2},{2,3},{3,4},{4,5},{5,6},{6,7},{8,9},{9,10},{10,11},{11... | collective-permute-start | bytes 786440 | tf_op jit(solution)/shard_map/ppermute | solution.py:25
  297.5 142.6 %reduce-scatter.3.cloned.1.call-start = ((), (), s32[]{:S(2)}) async-start(), calls=%async_computation.3 | async-start | bytes 11796480 | tf_op jit(solution)/shard_map/reduce_scatter | solution.py:211
  309.1 15.2 %collective-permute-start.15 = (bf16[1,256,512]{1,2,0:T(8,128)(2,1)S(1)}, bf16[1,256,512]{1,2,0:T(8,128)(2,1)S(1)}, u32[]{:S(2)}, u32[]{:S(2)}) collective-permute-start(bf16[1,256,512]{1,2,0:T(8,128)(2,1)S(1)} %get-tuple-element.11), channel_id=1, source_target_pairs={{4,0},{5,1},{6,2},{7,3},{12,8},{13,9},{14,10},{15,11},{20,16},{21,... | collective-permute-start | bytes 786440 | tf_op jit(solution)/shard_map/ppermute | solution.py:25
  310.7 14.9 %collective-permute-start.14 = (bf16[1,256,512]{1,2,0:T(8,128)(2,1)S(1)}, bf16[1,256,512]{1,2,0:T(8,128)(2,1)S(1)}, u32[]{:S(2)}, u32[]{:S(2)}) collective-permute-start(bf16[1,256,512]{1,2,0:T(8,128)(2,1)S(1)} %get-tuple-element.12), channel_id=1, source_target_pairs={{3,0},{4,1},{5,2},{6,3},{7,4},{11,8},{12,9},{13,10},{14,11},{15,12... | collective-permute-start | bytes 786440 | tf_op jit(solution)/shard_map/ppermute | solution.py:25
  312.0 15.0 %collective-permute-start.13 = (bf16[1,256,512]{1,2,0:T(8,128)(2,1)S(1)}, bf16[1,256,512]{1,2,0:T(8,128)(2,1)S(1)}, u32[]{:S(2)}, u32[]{:S(2)}) collective-permute-start(bf16[1,256,512]{1,2,0:T(8,128)(2,1)S(1)} %get-tuple-element.13), channel_id=1, source_target_pairs={{2,0},{3,1},{4,2},{5,3},{6,4},{7,5},{10,8},{11,9},{12,10},{13,11},... | collective-permute-start | bytes 786440 | tf_op jit(solution)/shard_map/ppermute | solution.py:25
  313.3 15.0 %collective-permute-start.12 = (bf16[1,256,512]{1,2,0:T(8,128)(2,1)S(1)}, bf16[1,256,512]{1,2,0:T(8,128)(2,1)S(1)}, u32[]{:S(2)}, u32[]{:S(2)}) collective-permute-start(bf16[1,256,512]{1,2,0:T(8,128)(2,1)S(1)} %get-tuple-element.10), channel_id=1, source_target_pairs={{1,0},{2,1},{3,2},{4,3},{5,4},{6,5},{7,6},{9,8},{10,9},{11,10},{12... | collective-permute-start | bytes 786440 | tf_op jit(solution)/shard_map/ppermute | solution.py:25
  317.2 21.2 %collective-permute-start.11 = (bf16[1,256,512]{1,2,0:T(8,128)(2,1)S(1)}, bf16[1,256,512]{1,2,0:T(8,128)(2,1)S(1)}, u32[]{:S(2)}, u32[]{:S(2)}) collective-permute-start(bf16[1,256,512]{1,2,0:T(8,128)(2,1)S(1)} %get-tuple-element.7), channel_id=1, source_target_pairs={{4,0},{5,1},{6,2},{7,3},{12,8},{13,9},{14,10},{15,11},{20,16},{21,... | collective-permute-start | bytes 786440 | tf_op jit(solution)/shard_map/ppermute | solution.py:25
  324.3 14.8 %collective-permute-start.10 = (bf16[1,256,512]{1,2,0:T(8,128)(2,1)S(1)}, bf16[1,256,512]{1,2,0:T(8,128)(2,1)S(1)}, u32[]{:S(2)}, u32[]{:S(2)}) collective-permute-start(bf16[1,256,512]{1,2,0:T(8,128)(2,1)S(1)} %get-tuple-element.8), channel_id=1, source_target_pairs={{3,0},{4,1},{5,2},{6,3},{7,4},{11,8},{12,9},{13,10},{14,11},{15,12... | collective-permute-start | bytes 786440 | tf_op jit(solution)/shard_map/ppermute | solution.py:25
  325.6 18.8 %collective-permute-start.9 = (bf16[1,256,512]{1,2,0:T(8,128)(2,1)S(1)}, bf16[1,256,512]{1,2,0:T(8,128)(2,1)S(1)}, u32[]{:S(2)}, u32[]{:S(2)}) collective-permute-start(bf16[1,256,512]{1,2,0:T(8,128)(2,1)S(1)} %get-tuple-element.9), channel_id=1, source_target_pairs={{2,0},{3,1},{4,2},{5,3},{6,4},{7,5},{10,8},{11,9},{12,10},{13,11},... | collective-permute-start | bytes 786440 | tf_op jit(solution)/shard_map/ppermute | solution.py:25
  326.9 17.5 %collective-permute-start.8 = (bf16[1,256,512]{1,2,0:T(8,128)(2,1)S(1)}, bf16[1,256,512]{1,2,0:T(8,128)(2,1)S(1)}, u32[]{:S(2)}, u32[]{:S(2)}) collective-permute-start(bf16[1,256,512]{1,2,0:T(8,128)(2,1)S(1)} %get-tuple-element.6), channel_id=1, source_target_pairs={{1,0},{2,1},{3,2},{4,3},{5,4},{6,5},{7,6},{9,8},{10,9},{11,10},{12... | collective-permute-start | bytes 786440 | tf_op jit(solution)/shard_map/ppermute | solution.py:25
  351.6 91.7 %collective-permute-start.20 = (bf16[128,2560]{1,0:T(8,128)(2,1)}, bf16[128,2560]{1,0:T(8,128)(2,1)S(1)}, u32[]{:S(2)}, u32[]{:S(2)}) collective-permute-start(bf16[128,2560]{1,0:T(8,128)(2,1)} %reduce-scatter.5.cloned.1.call-done), channel_id=1, source_target_pairs={{0,64},{8,72},{16,80},{24,88},{32,96},{40,104},{48,112},{56,120},{... | collective-permute-start | bytes 1966088 | tf_op jit(solution)/shard_map/ppermute | solution.py:19
  355.1 88.9 %collective-permute-start.21 = (bf16[128,2560]{1,0:T(8,128)(2,1)}, bf16[128,2560]{1,0:T(8,128)(2,1)S(1)}, u32[]{:S(2)}, u32[]{:S(2)}) collective-permute-start(bf16[128,2560]{1,0:T(8,128)(2,1)} %reduce-scatter.5.cloned.1.call-done), channel_id=1, source_target_pairs={{0,32},{8,40},{16,48},{24,56},{32,0},{40,8},{48,16},{56,24},{64,96... | collective-permute-start | bytes 1966088 | tf_op jit(solution)/shard_map/ppermute | solution.py:19
  355.5 91.4 %collective-permute-start.22 = (bf16[128,2560]{1,0:T(8,128)(2,1)}, bf16[128,2560]{1,0:T(8,128)(2,1)S(1)}, u32[]{:S(2)}, u32[]{:S(2)}) collective-permute-start(bf16[128,2560]{1,0:T(8,128)(2,1)} %reduce-scatter.5.cloned.1.call-done), channel_id=1, source_target_pairs={{0,16},{8,24},{16,0},{24,8},{32,48},{40,56},{48,32},{56,40},{64,80... | collective-permute-start | bytes 1966088 | tf_op jit(solution)/shard_map/ppermute | solution.py:19
  360.3 87.9 %collective-permute-start.23 = (bf16[128,2560]{1,0:T(8,128)(2,1)}, bf16[128,2560]{1,0:T(8,128)(2,1)S(1)}, u32[]{:S(2)}, u32[]{:S(2)}) collective-permute-start(bf16[128,2560]{1,0:T(8,128)(2,1)} %reduce-scatter.5.cloned.1.call-done), channel_id=1, source_target_pairs={{0,8},{8,0},{16,24},{24,16},{32,40},{40,32},{48,56},{56,48},{64,72... | collective-permute-start | bytes 1966088 | tf_op jit(solution)/shard_map/ppermute | solution.py:19
  440.1 33.4 %collective-permute-start.16 = (bf16[320,2048]{1,0:T(8,128)(2,1)}, bf16[320,2048]{1,0:T(8,128)(2,1)S(1)}, u32[]{:S(2)}, u32[]{:S(2)}) collective-permute-start(bf16[320,2048]{1,0:T(8,128)(2,1)} %reduce-scatter.3.cloned.1.call-done), channel_id=1, source_target_pairs={{0,64},{8,72},{16,80},{24,88},{32,96},{40,104},{48,112},{56,120},{... | collective-permute-start | bytes 3932168 | tf_op jit(solution)/shard_map/ppermute | solution.py:19
  443.3 56.9 %collective-permute-start.17 = (bf16[320,2048]{1,0:T(8,128)(2,1)}, bf16[320,2048]{1,0:T(8,128)(2,1)S(1)}, u32[]{:S(2)}, u32[]{:S(2)}) collective-permute-start(bf16[320,2048]{1,0:T(8,128)(2,1)} %reduce-scatter.3.cloned.1.call-done), channel_id=1, source_target_pairs={{0,32},{8,40},{16,48},{24,56},{32,0},{40,8},{48,16},{56,24},{64,96... | collective-permute-start | bytes 3932168 | tf_op jit(solution)/shard_map/ppermute | solution.py:19
  444.0 56.2 %collective-permute-start.18 = (bf16[320,2048]{1,0:T(8,128)(2,1)}, bf16[320,2048]{1,0:T(8,128)(2,1)S(1)}, u32[]{:S(2)}, u32[]{:S(2)}) collective-permute-start(bf16[320,2048]{1,0:T(8,128)(2,1)} %reduce-scatter.3.cloned.1.call-done), channel_id=1, source_target_pairs={{0,16},{8,24},{16,0},{24,8},{32,48},{40,56},{48,32},{56,40},{64,80... | collective-permute-start | bytes 3932168 | tf_op jit(solution)/shard_map/ppermute | solution.py:19
  446.9 56.2 %collective-permute-start.19 = (bf16[320,2048]{1,0:T(8,128)(2,1)}, bf16[320,2048]{1,0:T(8,128)(2,1)S(1)}, u32[]{:S(2)}, u32[]{:S(2)}) collective-permute-start(bf16[320,2048]{1,0:T(8,128)(2,1)} %reduce-scatter.3.cloned.1.call-done), channel_id=1, source_target_pairs={{0,8},{8,0},{16,24},{24,16},{32,40},{40,32},{48,56},{56,48},{64,72... | collective-permute-start | bytes 3932168 | tf_op jit(solution)/shard_map/ppermute | solution.py:19
  (13 other events, 192.9 us)
Sparse Core Ops, SparseCore 0:
  11.1 68.3 all-gather.9
  82.6 66.1 all-gather.13
  151.9 67.6 all-gather.11
  222.5 65.1 all-gather.7
  297.6 52.8 reduce-scatter.4
  352.7 87.3 reduce-scatter.2
where the time goes:
time: 515 us; the launch traced here: 513 us
  waiting for transfers between devices  352 us (68%)
  starting transfers between devices  51.2 us (10%)
  local copies, waits for them, and re-layouts  45.3 us (9%)
  matrix products  39.8 us (8%)
  between operations  15.3 us (3%)
  other arithmetic  9.58 us (2%)
    reduce_scatter x2, waiting for transfers between devices, per_device(): lax.psum_scatter(lax.optimization_barrier(partial_term.astype(jnp.bfloat1...  79.5 us
    all_gather x1, waiting for transfers between devices, per_device(): lax.all_gather(w_key, ('dp', 'ctx'), axis=0, tiled=True)  66.7 us
    all_gather x1, waiting for transfers between devices, per_device(): lax.all_gather(w_value, ('dp', 'ctx'), axis=0, tiled=True)  55.6 us
    ppermute x8, waiting for transfers between devices, partner(): return lax.ppermute(value, axis, pairs)  52.3 us
    all_gather x1, waiting for transfers between devices, per_device(): out_whole = lax.all_gather(w_out, ('dp', 'ctx'), axis=0, tiled=True)  49.1 us
    ppermute x16, starting transfers between devices, shifted(): return lax.ppermute(block, axis, route)  34.6 us
    unnamed x41, local copies, waits for them, and re-layouts  29.2 us
    all_gather x1, waiting for transfers between devices, per_device(): lax.all_gather(w_query, ('dp', 'ctx'), axis=0, tiled=True)  23.2 us
  transfers between devices with their start and end apart: 30, of which 13 were waited for; matrix products, arithmetic and copies ran while one was open for 16% of the time, Pallas kernels for 0%

commit v1 on v0

--- a/solution.py
+++ b/solution.py
@@ -1,7 +1,381 @@
+import functools
 import jax
 import jax.numpy as jnp
 from jax import lax
+from jax.experimental import pallas as pl
+from jax.experimental.pallas import tpu as pltpu
 from jax.sharding import PartitionSpec as P
+
+MESH = pl.DeviceIdType.MESH
+BF16 = jnp.bfloat16
+F32 = jnp.float32
+SIDE = 4
+
+
+def place():
+    dp, ctx = lax.axis_index("dp"), lax.axis_index("ctx")
+    return {"x": lax.rem(dp, SIDE), "z": lax.div(dp, SIDE), "y": lax.div(ctx, 2), "c": lax.rem(ctx, 2)}
+
+
+def device(at):
+    return (at["z"] * SIDE + at["x"], at["y"] * 2 + at["c"])
+
+
+def beside(at, axis, step):
+    return {**at, axis: lax.rem(at[axis] + step + SIDE, SIDE)}
+
+
+def sibling(at):
+    return {**at, "c": 1 - at["c"]}
+
+
+def greet(peers):
+    barrier = pltpu.get_barrier_semaphore()
+    for peer in peers:
+        pl.semaphore_signal(barrier, inc=1, device_id=device(peer), device_id_type=MESH)
+    pl.semaphore_wait(barrier, len(peers))
+
+
+def gather_kernel(rows_in, rows_out, in_ref, out_ref, w_in, w_out, slots_in, slots_out, wide, block_in, block_out,
+                  swap_send, swap_recv, pair_sem, local_sem, ring_send, ring_recv, twin_send, twin_recv):
+    at = place()
+    c = at["c"]
+    ctx = at["y"] * 2 + c
+    twin = sibling(at)
+    others = [lax.rem(ctx + k, 8) for k in range(1, 8)]
+    group = [{**at, "y": lax.div(j, 2), "c": lax.rem(j, 2)} for j in others]
+    greet([beside(at, "x", 1), beside(at, "x", -1), beside(at, "z", 1), beside(at, "z", -1)] + group)
+
+    copies = []
+    for k in range(7):
+        copies.append(pltpu.make_async_remote_copy(
+            in_ref.at[others[k]], slots_in.at[ctx], swap_send.at[k], swap_recv.at[k],
+            device_id=device(group[k]), device_id_type=MESH))
+    pair = pltpu.make_async_remote_copy(
+        out_ref.at[1 - c], slots_out.at[c], pair_sem.at[0], pair_sem.at[1], device_id=device(twin), device_id_type=MESH)
+    pair.start()
+    for copy in copies:
+        copy.start()
+    slots_in[ctx] = in_ref[ctx]
+    slots_out[c] = out_ref[c]
+    pair.wait()
+    block_out[0, 0, 0] = jnp.concatenate(
+        [slots_out[0].astype(F32)[:rows_out], slots_out[1].astype(F32)[:rows_out]], axis=0).astype(BF16)
+    for copy in copies:
+        copy.wait()
+    for j in range(8):
+        wide[rows_in * j:rows_in * (j + 1)] = slots_in[j].astype(F32)[:rows_in]
+    block_in[0, 0, 0] = wide[...].astype(BF16)
+
+    half_rows = rows_in * 4
+    one = {a: pl.ds(at[a], 1) for a in "xyz"}
+    whole = pl.ds(0, SIDE)
+
+    def view(part, where, core):
+        if part == 2:
+            return w_out.at[where["z"], where["x"], where["y"], :, pl.ds(pl.multiple_of(core * 1280, 128), 1280)]
+        rows = pl.ds(half_rows * part, half_rows)
+        return w_in.at[where["y"], where["z"], where["x"], rows, pl.ds(pl.multiple_of(core * 256, 128), 256)]
+
+    def rest(part):
+        return [
+            pltpu.make_async_copy(block_in.at[:, :, :, pl.ds(half_rows * p, half_rows), :] if p < 2 else block_out,
+                                  view(p, one, c), local_sem.at[p])
+            for p in part]
+
+    stores = rest(range(3))
+    for copy in stores:
+        copy.start()
+    for copy in stores:
+        copy.wait()
+
+    orders = ("xyz", "yzx", "zxy")
+    twins, sends = [], []
+
+    def to_twin(part, where, slot):
+        copy = pltpu.make_async_remote_copy(
+            view(part, where, c), view(part, where, c), twin_send.at[part, slot], twin_recv.at[part, slot],
+            device_id=device(twin), device_id_type=MESH)
+        copy.start()
+        twins.append(copy)
+
+    def ring(part, phase, slot, where, step):
+        axis = orders[part][phase]
+        copy = pltpu.make_async_remote_copy(
+            view(part, where, c), view(part, where, c), ring_send.at[part, phase, slot], ring_recv.at[part, phase, slot],
+            device_id=device(beside(at, axis, step)), device_id_type=MESH)
+        copy.start()
+        sends.append(copy)
+        return copy
+
+    for phase in range(3):
+        def known(part, shift, half):
+            order = orders[part]
+            where = dict(one)
+            for a in order[:phase]:
+                where[a] = whole
+            if phase and half is not None:
+                where[order[0]] = pl.ds(2 * half, 2)
+            axis = order[phase]
+            where[axis] = pl.ds(lax.rem(at[axis] + shift + SIDE, SIDE), 1)
+            return where
+
+        first, last = {}, {}
+        halves = (0, 1) if phase else (None,)
+        for part in range(3):
+            if phase:
+                first[part] = (ring(part, phase, 0, known(part, 0, 0), 1), ring(part, phase, 1, known(part, 0, 1), -1))
+                last[part] = [ring(part, phase, 2, known(part, 0, 1), 1), ring(part, phase, 3, known(part, 0, 0), -1)]
+            else:
+                first[part] = (ring(part, 0, 0, known(part, 0, None), 1),)
+                last[part] = [ring(part, 0, 1, known(part, 0, None), -1)]
+        if phase == 2:
+            for part in range(3):
+                to_twin(part, known(part, 0, None), 0)
+        for part in range(3):
+            if phase:
+                first[part][0].wait_recv()
+                last[part].append(ring(part, phase, 4, known(part, -1, 0), 1))
+                first[part][1].wait_recv()
+                last[part].append(ring(part, phase, 5, known(part, 1, 1), -1))
+                if phase == 2:
+                    to_twin(part, known(part, -1, 0), 1)
+                    to_twin(part, known(part, 1, 1), 2)
+            else:
+                first[part][0].wait_recv()
+                last[part].append(ring(part, 0, 4, known(part, -1, None), 1))
+        for n in range(4):
+            for part in range(3):
+                if n < len(last[part]):
+                    last[part][n].wait_recv()
+                    if phase == 2:
+                        shift, half = ((-1, 1), (1, 0), (-2, 0), (2, 1))[n]
+                        to_twin(part, known(part, shift, half), 3 + n)
+    for copy in sends:
+        copy.wait_send()
+    for copy in twins:
+        copy.wait()
+
+
+def gather_weights(w_query, w_key, w_value, w_out):
+    rows_in, rows_out = w_query.shape[0], w_out.shape[0]
+    joined = jnp.concatenate([w_query, w_key, w_value], axis=1)
+    pieces_in = jnp.pad(joined.reshape(rows_in, 8, 256).transpose(1, 0, 2), ((0, 0), (0, 32 - rows_in), (0, 0)))
+    pieces_out = jnp.pad(w_out.reshape(rows_out, 2, 1280).transpose(1, 0, 2), ((0, 0), (0, 16 - rows_out), (0, 0)))
+    vmem = pl.BlockSpec(memory_space=pltpu.VMEM)
+    hbm = pl.BlockSpec(memory_space=pl.ANY)
+    dma = pltpu.SemaphoreType.DMA
+    whole_in, whole_out = pl.pallas_call(
+        functools.partial(gather_kernel, rows_in, rows_out),
+        out_shape=(
+            jax.ShapeDtypeStruct((SIDE, SIDE, SIDE, 8 * rows_in, 512), BF16),
+            jax.ShapeDtypeStruct((SIDE, SIDE, SIDE, 2 * rows_out, 2560), BF16),
+        ),
+        in_specs=[vmem, vmem],
+        out_specs=(hbm, hbm),
+        scratch_shapes=[
+            pltpu.VMEM((8, 32, 256), BF16),
+            pltpu.VMEM((2, 16, 1280), BF16),
+            pltpu.VMEM((8 * rows_in, 256), F32),
+            pltpu.VMEM((1, 1, 1, 8 * rows_in, 256), BF16),
+            pltpu.VMEM((1, 1, 1, 2 * rows_out, 1280), BF16),
+            dma((7,)), dma((7,)), dma((2,)), dma((3,)),
+            dma((3, 3, 6)), dma((3, 3, 6)), dma((3, 7)), dma((3, 7)),
+        ],
+        compiler_params=pltpu.CompilerParams(collective_id=0, has_side_effects=True),
+        name="gather_weights",
+    )(pieces_in, pieces_out)
+    return whole_in.reshape(4, 128 * rows_in, 512), whole_out.reshape(128 * rows_out, 2560)
+
+
+def add_rows(count, step, body):
+    def at(i, carry):
+        body(pl.ds(pl.multiple_of(i * step, step), step))
+        return carry
+    lax.fori_loop(0, count // step, at, 0)
+
+
+N_IN, N_OUT = 4, 2
+
+
+def reduce_kernel(in_ref, out_ref, own_in, own_out, mate_in, mate_out, *scratch):
+    (sum_in, sum_out, twin_in, twin_out, far_in, far_out, near_in, near_out, load_sem, twin_send, twin_recv,
+     far_send, far_recv, near_send, near_recv, mate_send, mate_recv, keep_sem, stage_in, stage_out, done_in, done_out) = scratch
+    at = place()
+    c, y = at["c"], at["y"]
+    twin = sibling(at)
+    up, down = beside(at, "y", 1), beside(at, "y", -1)
+    x_flip = {**at, "x": at["x"] + 1 - 2 * lax.rem(at["x"], 2)}
+    x_turn = {**at, "x": SIDE - 1 - at["x"]}
+    z_flip = {**at, "z": at["z"] + 1 - 2 * lax.rem(at["z"], 2)}
+    z_turn = {**at, "z": SIDE - 1 - at["z"]}
+    greet([twin, up, down, x_flip, x_turn, z_flip, z_turn])
+
+    chunks = [(1, n) for n in range(N_OUT)] + [(0, n) for n in range(N_IN)]
+    total = len(chunks)
+
+    def pick(kind, n, inside, outside):
+        return (inside if kind == 0 else outside).at[n]
+
+    def columns(kind, n):
+        return pl.ds(512 * n, 512) if kind == 0 else pl.ds(1280 * n, 1280)
+
+    def source(kind, n, core):
+        ref = in_ref if kind == 0 else out_ref
+        return ref.at[:, core, :, columns(kind, n)]
+
+    loads, swaps = [], []
+    for k, (kind, n) in enumerate(chunks):
+        load = pltpu.make_async_copy(source(kind, n, c), pick(kind, n, sum_in, sum_out), load_sem.at[k])
+        swap = pltpu.make_async_remote_copy(
+            source(kind, n, 1 - c), pick(kind, n, twin_in, twin_out), twin_send.at[k], twin_recv.at[k],
+            device_id=device(twin), device_id_type=MESH)
+        swap.start()
+        load.start()
+        loads.append(load)
+        swaps.append(swap)
+
+    y_far, y_up, y_down = lax.rem(y + 2, SIDE), up["y"], down["y"]
+    height = {0: in_ref.shape[2], 1: out_ref.shape[2]}
+    far, near_own, near_sum, flips, turns, keeps = {}, {}, {}, {}, {}, {}
+
+    def remote(src, dst, send, recv, to):
+        copy = pltpu.make_async_remote_copy(src, dst, send, recv, device_id=device(to), device_id_type=MESH)
+        copy.start()
+        return copy
+
+    def stage_a(k):
+        kind, n = chunks[k]
+        rows = height[kind]
+        sums, extra = pick(kind, n, sum_in, sum_out), pick(kind, n, twin_in, twin_out)
+        fars, nears = pick(kind, n, far_in, far_out), pick(kind, n, near_in, near_out)
+        h0, h1 = pl.ds(0, rows // 2), pl.ds(rows // 2, rows // 2)
+        loads[k].wait()
+        swaps[k].wait_recv()
+
+        def add(block):
+            def body(r):
+                sums[block, r, :] = (sums[block, r, :].astype(F32) + extra[block, r, :].astype(F32)).astype(BF16)
+            add_rows(rows, 32, body)
+        add(y_far)
+        far[k] = (remote(sums.at[y_far, h0], fars.at[0], far_send.at[k, 0], far_recv.at[k, 0], up),
+                  remote(sums.at[y_far, h1], fars.at[1], far_send.at[k, 1], far_recv.at[k, 1], down))
+        add(y_up)
+        add(y_down)
+        near_own[k] = (remote(sums.at[y_up, h1], nears.at[0, h1], near_send.at[k, 0], near_recv.at[k, 0], up),
+                       remote(sums.at[y_down, h0], nears.at[1, h0], near_send.at[k, 1], near_recv.at[k, 1], down))
+        add(y)
+
+    def stage_b(k):
+        kind, n = chunks[k]
+        rows = height[kind]
+        half = rows // 2
+        sums = pick(kind, n, sum_in, sum_out)
+        fars, nears = pick(kind, n, far_in, far_out), pick(kind, n, near_in, near_out)
+        h0, h1 = pl.ds(0, half), pl.ds(half, half)
+        far[k][0].wait_recv()
+
+        def low(r):
+            sums[y_up, r, :] = (sums[y_up, r, :].astype(F32) + fars[0, r, :].astype(F32)).astype(BF16)
+        add_rows(half, 32, low)
+        first = remote(sums.at[y_up, h0], nears.at[0, h0], near_send.at[k, 2], near_recv.at[k, 2], up)
+        far[k][1].wait_recv()
+
+        def high(i, carry):
+            r = pl.ds(pl.multiple_of(i * 32, 32), 32)
+            s = pl.ds(pl.multiple_of(i * 32 + half, 32), 32)
+            sums[y_down, s, :] = (sums[y_down, s, :].astype(F32) + fars[1, r, :].astype(F32)).astype(BF16)
+            return carry
+        lax.fori_loop(0, half // 32, high, 0)
+        near_sum[k] = (first, remote(sums.at[y_down, h1], nears.at[1, h1], near_send.at[k, 3], near_recv.at[k, 3], down))
+
+    def stage_c(k):
+        kind, n = chunks[k]
+        rows = height[kind]
+        sums = pick(kind, n, sum_in, sum_out)
+        nears = pick(kind, n, near_in, near_out)
+        done = pick(kind, n, done_in, done_out)
+        for copy in near_own[k] + near_sum[k]:
+            copy.wait_recv()
+
+        def body(r):
+            done[r, :] = (sums[y, r, :].astype(F32) + nears[0, r, :].astype(F32) + nears[1, r, :].astype(F32)).astype(BF16)
+        add_rows(rows, 32, body)
+        mates = stage_in if kind == 0 else stage_out
+        flips[k] = (remote(done, mates.at[0, n], mate_send.at[k, 0], mate_recv.at[k, 0], x_flip),
+                    remote(done, mates.at[2, n], mate_send.at[k, 2], mate_recv.at[k, 2], z_flip))
+        result = own_in if kind == 0 else own_out
+        keeps[k] = [pltpu.make_async_copy(done, result.at[:, columns(kind, n)], keep_sem.at[k, 4])]
+        keeps[k][0].start()
+
+    def keep(k, level):
+        kind, n = chunks[k]
+        mates, result = (stage_in, mate_in) if kind == 0 else (stage_out, mate_out)
+        copy = pltpu.make_async_copy(mates.at[level, n], result.at[level, :, columns(kind, n)], keep_sem.at[k, level])
+        copy.start()
+        keeps[k].append(copy)
+
+    def stage_d(k):
+        kind, n = chunks[k]
+        mates = stage_in if kind == 0 else stage_out
+        flips[k][0].wait_recv()
+        first = remote(mates.at[0, n], mates.at[1, n], mate_send.at[k, 1], mate_recv.at[k, 1], x_turn)
+        flips[k][1].wait_recv()
+        turns[k] = (first, remote(mates.at[2, n], mates.at[3, n], mate_send.at[k, 3], mate_recv.at[k, 3], z_turn))
+        keep(k, 0)
+        keep(k, 2)
+
+    for t in range(total + 3):
+        if t < total:
+            stage_a(t)
+        if 0 <= t - 1 < total:
+            stage_b(t - 1)
+        if 0 <= t - 2 < total:
+            stage_c(t - 2)
+        if 0 <= t - 3 < total:
+            stage_d(t - 3)
+    for k in range(total):
+        turns[k][0].wait_recv()
+        keep(k, 1)
+        turns[k][1].wait_recv()
+        keep(k, 3)
+    for k in range(total):
+        swaps[k].wait_send()
+        for copy in far[k] + near_own[k] + near_sum[k] + flips[k] + turns[k]:
+            copy.wait_send()
+        for copy in keeps[k]:
+            copy.wait()
+
+
+def reduce_and_trade(term_in, term_out):
+    ri, ro = term_in.shape[0] // 8, term_out.shape[0] // 8
+    ci, co = term_in.shape[1], term_out.shape[1]
+    wi, wo = ci // N_IN, co // N_OUT
+    hbm = pl.BlockSpec(memory_space=pl.ANY)
+    dma = pltpu.SemaphoreType.DMA
+    n = N_IN + N_OUT
+    return pl.pallas_call(
+        reduce_kernel,
+        out_shape=(
+            jax.ShapeDtypeStruct((ri, ci), BF16), jax.ShapeDtypeStruct((ro, co), BF16),
+            jax.ShapeDtypeStruct((4, ri, ci), BF16), jax.ShapeDtypeStruct((4, ro, co), BF16),
+        ),
+        in_specs=[hbm, hbm],
+        out_specs=(hbm,) * 4,
+        scratch_shapes=[
+            pltpu.VMEM((N_IN, 4, ri, wi), BF16), pltpu.VMEM((N_OUT, 4, ro, wo), BF16),
+            pltpu.VMEM((N_IN, 4, ri, wi), BF16), pltpu.VMEM((N_OUT, 4, ro, wo), BF16),
+            pltpu.VMEM((N_IN, 2, ri // 2, wi), BF16), pltpu.VMEM((N_OUT, 2, ro // 2, wo), BF16),
+            pltpu.VMEM((N_IN, 2, ri, wi), BF16), pltpu.VMEM((N_OUT, 2, ro, wo), BF16),
+            dma((n,)), dma((n,)), dma((n,)),
+            dma((n, 2)), dma((n, 2)), dma((n, 4)), dma((n, 4)), dma((n, 4)), dma((n, 4)), dma((n, 5)),
+            pltpu.VMEM((4, N_IN, ri, wi), BF16), pltpu.VMEM((4, N_OUT, ro, wo), BF16),
+            pltpu.VMEM((N_IN, ri, wi), BF16), pltpu.VMEM((N_OUT, ro, wo), BF16),
+        ],
+        compiler_params=pltpu.CompilerParams(collective_id=1, has_side_effects=True, vmem_limit_bytes=56 * 2**20),
+        name="reduce_and_trade",
+    )(term_in.reshape(4, 2, ri, ci), term_out.reshape(4, 2, ro, co))
+
 
 QUERY_HEADS = 4
 KEY_VALUE_HEADS = 2
@@ -13,12 +387,6 @@
 masked_score = -1e30
 
 
-def partner(value, axis, bit):
-    mask = 2**bit
-    pairs = [(source, source ^ mask) for source in range(lax.axis_size(axis))]
-    return lax.ppermute(value, axis, pairs)
-
-
 def shifted(block, axis, distance):
     devices = range(lax.axis_size(axis))
     route = [(i - distance, i) for i in devices if i - distance in devices]
@@ -32,7 +400,9 @@
 
 
 def doc_index(positions, lengths):
-    endings = jnp.cumsum(lengths, axis=-1)
+    count = lengths.shape[-1]
+    upto = jnp.arange(count)[:, None] >= jnp.arange(count)[None, :]
+    endings = jnp.sum(jnp.where(upto[None], lengths[:, None, :], 0), axis=-1)
     return jnp.sum((endings[:, None, :] <= positions[:, :, None]).astype(jnp.int32), axis=-1)
 
 
@@ -116,10 +486,6 @@
             jnp.bfloat16
         ),
     )
-
-
-def trade(shard_pair, bit_number):
-    return partner((shard_pair[0], shard_pair[1]), "dp", bit_number)
 
 
 def per_device(
@@ -135,18 +501,9 @@
     lengths = doc_lengths[0]
     normed = norm_rows(tokens[0], norm_gain)
     flat_rows = normed.reshape(row_count, model_width)
-    pieces = (
-        lax.all_gather(w_query, ("dp", "ctx"), axis=0, tiled=True),
-        lax.all_gather(w_key, ("dp", "ctx"), axis=0, tiled=True),
-        lax.all_gather(w_value, ("dp", "ctx"), axis=0, tiled=True),
-    )
-    columns = flat_rows
-    query_sum, key_sum, value_sum = tuple(
-        (
-            jnp.dot(columns, weight_piece, preferred_element_type=jnp.float32)
-            for weight_piece in pieces
-        )
-    )
+    weights_in, out_whole = gather_weights(w_query, w_key, w_value, w_out)
+    sums = [jnp.dot(flat_rows, weights_in[n], preferred_element_type=jnp.float32) for n in range(4)]
+    query_sum, key_sum, value_sum = jnp.concatenate(sums[:2], axis=1), sums[2], sums[3]
     query_rows = query_sum.astype(jnp.bfloat16).reshape(seq_count, shard_len, query_width)
     key_own = key_sum.astype(jnp.bfloat16).reshape(seq_count, shard_len, key_feature_width)
     value_own = value_sum.astype(jnp.bfloat16).reshape(seq_count, shard_len, key_feature_width)
@@ -168,7 +525,6 @@
     mask = allowed(query_pos, key_pos, lengths)
     attn_probs, mixed_heads = attend(query_rows, key_tile, value_tile, mask)
     mixed_flat = mixed_heads.reshape(row_count, query_width)
-    out_whole = lax.all_gather(w_out, ("dp", "ctx"), axis=0, tiled=True)
     update = jnp.dot(mixed_flat, out_whole, preferred_element_type=jnp.float32)
     result = tokens[0].reshape(row_count, model_width).astype(jnp.float32) + update
     delta_rows = (
@@ -204,39 +560,18 @@
     joined = jnp.concatenate([query_gradients, key_final, value_final], axis=-1).reshape(
         row_count, query_width + 2 * key_feature_width
     )
-    columns = flat_rows
-    partial_term = lax.dot_general(
-        columns, joined, (((0,), (0,)), ((), ())), preferred_element_type=jnp.float32
-    )
-    grad_inputs = lax.psum_scatter(
-        lax.optimization_barrier(partial_term.astype(jnp.bfloat16))
-        .astype(jnp.float32)
-        .astype(jnp.bfloat16),
-        "ctx",
-        scatter_dimension=0,
-        tiled=True,
-    )
-    columns = mixed_flat
-    partial_term = lax.dot_general(
-        columns, delta_rows, (((0,), (0,)), ((), ())), preferred_element_type=jnp.float32
-    )
-    grad_outputs = lax.psum_scatter(
-        lax.optimization_barrier(partial_term.astype(jnp.bfloat16))
-        .astype(jnp.float32)
-        .astype(jnp.bfloat16),
-        "ctx",
-        scatter_dimension=0,
-        tiled=True,
-    )
-    level_count = lax.axis_size("dp").bit_length() - 1
+    term_in = lax.dot_general(
+        flat_rows, joined, (((0,), (0,)), ((), ())), preferred_element_type=jnp.float32
+    ).astype(jnp.bfloat16)
+    term_out = lax.dot_general(
+        mixed_flat, delta_rows, (((0,), (0,)), ((), ())), preferred_element_type=jnp.float32
+    ).astype(jnp.bfloat16)
+    grad_inputs, grad_outputs, mates_in, mates_out = reduce_and_trade(term_in, term_out)
     own_bit = gossip_bit[0]
-    partner_inputs = grad_inputs
-    partner_outputs = grad_outputs
-    for level_number in range(level_count):
-        moved_pair = trade((grad_inputs, grad_outputs), level_number)
-        picked = own_bit == level_number
-        partner_inputs = jnp.where(picked, moved_pair[0], partner_inputs)
-        partner_outputs = jnp.where(picked, moved_pair[1], partner_outputs)
+    partner_inputs, partner_outputs = mates_in[0], mates_out[0]
+    for level in range(1, 4):
+        partner_inputs = jnp.where(own_bit == level, mates_in[level], partner_inputs)
+        partner_outputs = jnp.where(own_bit == level, mates_out[level], partner_outputs)
     mean_inputs = (grad_inputs.astype(jnp.float32) + partner_inputs.astype(jnp.float32)) * 0.5
     mean_outputs = (grad_outputs.astype(jnp.float32) + partner_outputs.astype(jnp.float32)) * 0.5
     return (

time: 515 us -> 293 us (0.57)
  waiting for transfers between devices: 352 us -> 33 us
  Pallas kernels: 0 us -> 158 us
  starting transfers between devices: 51.2 us -> 29.7 us
  local copies, waits for them, and re-layouts: 45.3 us -> 24 us
  between operations: 15.3 us -> 1.95 us
  matrix products: 39.8 us -> 31.8 us
    all_gather x4 -> x0, waiting for transfers between devices: 195 us -> none  [the longest x1 66.7 us: per_device(): lax.all_gather(w_key, ('dp', 'ctx'), axis=0, tiled=True)]
    pallas_call x0 -> x2, Pallas kernels: none -> 158 us  [the longest x1 103 us: reduce_and_trade(): pl.pallas_call(reduce_kernel, out_shape=(jax.ShapeDtypeStruct((ri, ci), B...]
    reduce_scatter x2 -> x0, waiting for transfers between devices: 79.5 us -> none  [per_device(): lax.psum_scatter(lax.optimization_barrier(partial_term.astype(jnp.bfloat1...]
    ppermute x8 -> x0, waiting for transfers between devices: 52.3 us -> none  [partner(): return lax.ppermute(value, axis, pairs)]
    unnamed x41 -> x45, local copies, waits for them, and re-layouts: 29.2 us -> 3.37 us
    ppermute x8 -> x0, starting transfers between devices: 16.4 us -> none  [partner(): return lax.ppermute(value, axis, pairs)]
    ppermute x16, waiting for transfers between devices: 22.6 us -> 33 us  [shifted(): return lax.ppermute(block, axis, route)]
    slice x0 -> x1, local copies, waits for them, and re-layouts: none -> 6.22 us  [per_device(): weights_in[n]]
  transfers between devices with their start and end apart: 30 -> 16, of which waited for: 13 -> 7; matrix products, arithmetic and copies ran while one was open for 16% -> 6% of each run, Pallas kernels for 0% -> 0%
where the time goes in v1:
time: 293 us; the launch traced here: 291 us
  Pallas kernels  158 us (54%)
  waiting for transfers between devices  33 us (11%)
  matrix products  31.8 us (11%)
  starting transfers between devices  29.7 us (10%)
  local copies, waits for them, and re-layouts  24 us (8%)
  other arithmetic  12.1 us (4%)
    pallas_call x1, Pallas kernels, reduce_and_trade(): pl.pallas_call(reduce_kernel, out_shape=(jax.ShapeDtypeStruct((ri, ci), B...  103 us
    pallas_call x1, Pallas kernels, gather_weights(): pl.pallas_call(functools.partial(gather_kernel, rows_in, rows_out), out_s...  55.4 us
    ppermute x16, waiting for transfers between devices, shifted(): return lax.ppermute(block, axis, route)  33 us
    ppermute x16, starting transfers between devices, shifted(): return lax.ppermute(block, axis, route)  29.7 us
    dot_general x1, matrix products, per_device(): lax.dot_general(flat_rows, joined, (((0,), (0,)), ((), ())), preferred_el...  6.91 us
    slice x1, local copies, waits for them, and re-layouts, per_device(): weights_in[n]  6.22 us
    dot_general x4, matrix products, per_device(): jnp.dot(flat_rows, weights_in[n], preferred_element_type=jnp.float32)  6.14 us
  transfers between devices with their start and end apart: 16, of which 7 were waited for; matrix products, arithmetic and copies ran while one was open for 6% of the time, Pallas kernels for 0%

profile of v1, /device:TPU:0, one launch (start us, length us, event | category | flops | bytes accessed | tf_op | source)
XLA Modules:
  0.0 291.0 jit_solution(16266283264035186170)
XLA Ops:
  2.2 1.4 pad.9.out_ref
  3.6 55.4 %gather_weights.1 = (bf16[4,4,4,160,512]{4,3,2,1,0:T(8,128)(2,1)}, bf16[4,4,4,16,2560]{4,3,2,1,0:T(8,128)(2,1)}) custom-call(bf16[8,32,256]{2,1,0:T(8,128)(2,1)} %pad.8.in_ref, bf16[2,16,1280]{2,1,0:T(8,128)(2,1)} %pad.9.out_ref), custom_call_target="tpu_custom_call" | custom-call | tf_op jit(solution)/shard_map/gather_weights/pallas_call | solution.py:168
  59.1 6.2 %fusion.48 = (bf16[1,4,4,160,512]{4,3,2,1,0:T(8,128)(2,1)S(1)}, bf16[1,4,4,160,512]{4,3,2,1,0:T(8,128)(2,1)}, bf16[1,4,4,160,512]{4,3,2,1,0:T(8,128)(2,1)}, bf16[1,4,4,160,512]{4,3,2,1,0:T(8,128)(2,1)S(1)}) fusion(bf16[4,4,4,160,512]{4,3,2,1,0:T(8,128)(2,1)} %get-tuple-element.10), kind=kLoop, calls=%fused_computation.85 | loop fusion | bytes 20971520 | tf_op jit(solution)/shard_map/slice | solution.py:505
  66.5 4.0 %collective-permute-start = (bf16[1,256,512]{2,1,0:T(8,128)(2,1)S(1)}, bf16[1,256,512]{2,1,0:T(8,128)(2,1)S(1)}, u32[]{:S(2)}, u32[]{:S(2)}) collective-permute-start(bf16[1,256,512]{2,1,0:T(8,128)(2,1)S(1)} %bitcast.211), channel_id=1, source_target_pairs={{0,4},{1,5},{2,6},{3,7},{8,12},{9,13},{10,14},{11,15},{16,20},{17,... | collective-permute-start | bytes 786440 | tf_op jit(solution)/shard_map/ppermute | solution.py:393
  70.5 2.4 collective-permute-start.1
  72.9 1.6 collective-permute-start.2
  74.5 2.3 collective-permute-start.3
  76.9 1.6 convolution_convert_fusion.3
  78.4 2.0 collective-permute-start.4
  80.5 2.8 convolution_convert_fusion.4
  87.9 2.0 collective-permute-start.5
  89.9 2.1 collective-permute-start.6
  92.1 2.6 collective-permute-start.7
  100.9 4.5 %collective-permute-done.6 = bf16[1,256,512]{2,1,0:T(8,128)(2,1)} collective-permute-done((bf16[1,256,512]{2,1,0:T(8,128)(2,1)}, bf16[1,256,512]{2,1,0:T(8,128)(2,1)}, u32[]{:S(2)}, u32[]{:S(2)}) %collective-permute-start.6) | collective-permute-done | bytes 262176 | tf_op jit(solution)/shard_map/ppermute | solution.py:393
  110.5 2.3 fusion.30
  112.9 4.4 %fusion.6 = bf16[256,2560]{1,0:T(8,128)(2,1)S(1)} fusion(bf16[256,1024]{0,1:T(8,128)(2,1)S(1)} %bitcast.187, bf16[1024,2560]{1,0:T(8,128)(2,1)} %bitcast.183, bf16[1,1,256,2560]{3,2,1,0:T(8,128)(2,1)S(1)} %copy-done.1, bf16[1,1,256,2560]{3,2,1,0:T(8,128)(2,1)S(1)} %copy-done.9, f32[256]{0:T(256)S(1)} %bitcast.221), kind=kOutput, calls=%fused_computation.16 | convolution fusion | flops 1346109440 | bytes 9700352 | tf_op jit(solution)/shard_map/dot_general | solution.py:528
  117.3 3.8 %convolution_convert_fusion.1 = bf16[1024,2560]{1,0:T(8,128)(2,1)} fusion(bf16[256,1024]{0,1:T(8,128)(2,1)S(1)} %bitcast.188, bf16[256,2560]{1,0:T(8,128)(2,1)S(1)} %fusion.6), kind=kOutput, calls=%fused_computation.1 | convolution fusion | flops 1344798720 | bytes 7077888 | tf_op jit(solution)/shard_map/dot_general | solution.py:566
  121.0 2.3 convolution_convert_fusion.2
  123.4 2.2 copy.72
  125.6 2.0 copy.99
  127.7 1.3 multiply_reduce_fusion
  129.0 2.0 fusion.9
  133.3 1.4 collective-permute-start.10
  138.7 1.5 collective-permute-start.12
  141.2 2.4 collective-permute-done.10
  144.9 9.3 %collective-permute-done.11 = bf16[1,256,512]{1,2,0:T(8,128)(2,1)S(1)} collective-permute-done((bf16[1,256,512]{1,2,0:T(8,128)(2,1)S(1)}, bf16[1,256,512]{1,2,0:T(8,128)(2,1)S(1)}, u32[]{:S(2)}, u32[]{:S(2)}) %collective-permute-start.11) | collective-permute-done | bytes 262176 | tf_op jit(solution)/shard_map/ppermute | solution.py:393
  157.0 8.7 %collective-permute-done.13 = bf16[1,256,512]{1,2,0:T(8,128)(2,1)S(1)} collective-permute-done((bf16[1,256,512]{1,2,0:T(8,128)(2,1)S(1)}, bf16[1,256,512]{1,2,0:T(8,128)(2,1)S(1)}, u32[]{:S(2)}, u32[]{:S(2)}) %collective-permute-start.13) | collective-permute-done | bytes 262176 | tf_op jit(solution)/shard_map/ppermute | solution.py:393
  165.9 6.8 %collective-permute-done.15 = bf16[1,256,512]{1,2,0:T(8,128)(2,1)S(1)} collective-permute-done((bf16[1,256,512]{1,2,0:T(8,128)(2,1)S(1)}, bf16[1,256,512]{1,2,0:T(8,128)(2,1)S(1)}, u32[]{:S(2)}, u32[]{:S(2)}) %collective-permute-start.15) | collective-permute-done | bytes 262176 | tf_op jit(solution)/shard_map/ppermute | solution.py:393
  172.9 6.9 %convolution_convert_fusion = bf16[2560,2048]{1,0:T(8,128)(2,1)} fusion(bf16[1,256,512]{1,2,0:T(8,128)(2,1)S(1)} %add_convert_fusion, bf16[1,256,512]{1,2,0:T(8,128)(2,1)S(1)} %add_convert_fusion.1, bf16[1,256,1024]{1,2,0:T(8,128)(2,1)S(1)} %bitcast.207, bf16[1,1,256,2560]{3,2,1,0:T(8,128)(2,1)S(1)} %copy-done.2, f32[2560]{0:T(1024)S(1)} %copy-done.13, ...), kind=kOutput, calls=%fused_computation | convolution fusion | flops 2695364608 | bytes 12856320 | tf_op jit(solution)/shard_map/dot_general | solution.py:563
  179.8 103.0 %reduce_and_trade.1 = (bf16[320,2048]{1,0:T(8,128)(2,1)}, bf16[128,2560]{1,0:T(8,128)(2,1)}, bf16[4,320,2048]{2,1,0:T(8,128)(2,1)}, bf16[4,128,2560]{2,1,0:T(8,128)(2,1)}) custom-call(bf16[4,2,320,2048]{3,2,1,0:T(8,128)(2,1)} %bitcast.181, bf16[4,2,128,2560]{3,2,1,0:T(8,128)(2,1)} %bitcast.182), custom_call_target="tpu_custom_call" | custom-call | tf_op jit(solution)/shard_map/reduce_and_trade/pallas_call | solution.py:357
  282.7 4.1 %fusion.13 = f32[320,2048]{1,0:T(8,128)S(1)} fusion(bf16[320,2048]{1,0:T(8,128)(2,1)} %get-tuple-element.12, bf16[4,320,2048]{2,1,0:T(8,128)(2,1)} %get-tuple-element.13, pred[]{:T(512)} %bitcast.65, pred[]{:T(512)} %bitcast.64, pred[]{:T(512)} %bitcast.63), kind=kLoop, calls=%fused_computation.26 | loop fusion | flops 4587520 | bytes 9175043 | tf_op jit(solution)/shard_map/mul | solution.py:575
  289.5 1.5 fusion.24
  (100 shorter events, 31.9 us)
Async XLA Ops:
  59.0 6.2 %copy-start = (bf16[1,1,256,2560]{3,2,1,0:T(8,128)(2,1)S(1)}, bf16[1,1,256,2560]{3,2,1,0:T(8,128)(2,1)}, u32[]{:S(2)}) copy-start(bf16[1,1,256,2560]{3,2,1,0:T(8,128)(2,1)} %param.10) | copy-start | bytes 3932164
  59.1 6.6 %copy-start.13 = (f32[2560]{0:T(1024)S(1)}, f32[2560]{0:T(1024)}, u32[]{:S(2)}) copy-start(f32[2560]{0:T(1024)} %param.14) | copy-start | bytes 30724
  66.5 21.3 %collective-permute-start = (bf16[1,256,512]{2,1,0:T(8,128)(2,1)S(1)}, bf16[1,256,512]{2,1,0:T(8,128)(2,1)S(1)}, u32[]{:S(2)}, u32[]{:S(2)}) collective-permute-start(bf16[1,256,512]{2,1,0:T(8,128)(2,1)S(1)} %bitcast.211), channel_id=1, source_target_pairs={{0,4},{1,5},{2,6},{3,7},{8,12},{9,13},{10,14},{11,15},{16,20},{17,... | collective-permute-start | bytes 786440 | tf_op jit(solution)/shard_map/ppermute | solution.py:393
  70.5 19.4 %collective-permute-start.1 = (bf16[1,256,512]{2,1,0:T(8,128)(2,1)S(1)}, bf16[1,256,512]{2,1,0:T(8,128)(2,1)S(1)}, u32[]{:S(2)}, u32[]{:S(2)}) collective-permute-start(bf16[1,256,512]{2,1,0:T(8,128)(2,1)S(1)} %bitcast.212), channel_id=1, source_target_pairs={{0,3},{1,4},{2,5},{3,6},{4,7},{8,11},{9,12},{10,13},{11,14},{12,15... | collective-permute-start | bytes 786440 | tf_op jit(solution)/shard_map/ppermute | solution.py:393
  72.9 19.2 %collective-permute-start.2 = (bf16[1,256,512]{2,1,0:T(8,128)(2,1)S(1)}, bf16[1,256,512]{2,1,0:T(8,128)(2,1)S(1)}, u32[]{:S(2)}, u32[]{:S(2)}) collective-permute-start(bf16[1,256,512]{2,1,0:T(8,128)(2,1)S(1)} %bitcast.213), channel_id=1, source_target_pairs={{0,2},{1,3},{2,4},{3,5},{4,6},{5,7},{8,10},{9,11},{10,12},{11,13},... | collective-permute-start | bytes 786440 | tf_op jit(solution)/shard_map/ppermute | solution.py:393
  74.5 20.1 %collective-permute-start.3 = (bf16[1,256,512]{2,1,0:T(8,128)(2,1)S(1)}, bf16[1,256,512]{2,1,0:T(8,128)(2,1)S(1)}, u32[]{:S(2)}, u32[]{:S(2)}) collective-permute-start(bf16[1,256,512]{2,1,0:T(8,128)(2,1)S(1)} %bitcast.214), channel_id=1, source_target_pairs={{0,1},{1,2},{2,3},{3,4},{4,5},{5,6},{6,7},{8,9},{9,10},{10,11},{11... | collective-permute-start | bytes 786440 | tf_op jit(solution)/shard_map/ppermute | solution.py:393
  78.4 19.4 %collective-permute-start.4 = (bf16[1,256,512]{2,1,0:T(8,128)(2,1)}, bf16[1,256,512]{2,1,0:T(8,128)(2,1)S(1)}, u32[]{:S(2)}, u32[]{:S(2)}) collective-permute-start(bf16[1,256,512]{2,1,0:T(8,128)(2,1)} %bitcast.16), channel_id=1, source_target_pairs={{0,4},{1,5},{2,6},{3,7},{8,12},{9,13},{10,14},{11,15},{16,20},{17,... | collective-permute-start | bytes 786440 | tf_op jit(solution)/shard_map/ppermute | solution.py:393
  80.5 2.8 copy-start.15
  80.5 4.3 %copy-start.4 = (bf16[1,4,4,160,512]{4,3,2,1,0:T(8,128)(2,1)S(1)}, bf16[1,4,4,160,512]{4,3,2,1,0:T(8,128)(2,1)}, u32[]{:S(2)}) copy-start(bf16[1,4,4,160,512]{4,3,2,1,0:T(8,128)(2,1)} %get-tuple-element.18) | copy-start | bytes 7864324
  87.2 8.5 %copy-start.6 = (bf16[256,1024]{0,1:T(8,128)(2,1)}, bf16[256,1024]{0,1:T(8,128)(2,1)S(1)}, u32[]{:S(2)}) copy-start(bf16[256,1024]{0,1:T(8,128)(2,1)S(1)} %copy.98) | copy-start | bytes 1572868
  87.9 11.9 %collective-permute-start.5 = (bf16[1,256,512]{2,1,0:T(8,128)(2,1)}, bf16[1,256,512]{2,1,0:T(8,128)(2,1)}, u32[]{:S(2)}, u32[]{:S(2)}) collective-permute-start(bf16[1,256,512]{2,1,0:T(8,128)(2,1)} %bitcast.16), channel_id=1, source_target_pairs={{0,3},{1,4},{2,5},{3,6},{4,7},{8,11},{9,12},{10,13},{11,14},{12,15... | collective-permute-start | bytes 786440 | tf_op jit(solution)/shard_map/ppermute | solution.py:393
  89.9 15.5 %collective-permute-start.6 = (bf16[1,256,512]{2,1,0:T(8,128)(2,1)}, bf16[1,256,512]{2,1,0:T(8,128)(2,1)}, u32[]{:S(2)}, u32[]{:S(2)}) collective-permute-start(bf16[1,256,512]{2,1,0:T(8,128)(2,1)} %bitcast.16), channel_id=1, source_target_pairs={{0,2},{1,3},{2,4},{3,5},{4,6},{5,7},{8,10},{9,11},{10,12},{11,13},... | collective-permute-start | bytes 786440 | tf_op jit(solution)/shard_map/ppermute | solution.py:393
  92.1 15.9 %collective-permute-start.7 = (bf16[1,256,512]{2,1,0:T(8,128)(2,1)}, bf16[1,256,512]{2,1,0:T(8,128)(2,1)}, u32[]{:S(2)}, u32[]{:S(2)}) collective-permute-start(bf16[1,256,512]{2,1,0:T(8,128)(2,1)} %bitcast.16), channel_id=1, source_target_pairs={{0,1},{1,2},{2,3},{3,4},{4,5},{5,6},{6,7},{8,9},{9,10},{10,11},{11... | collective-permute-start | bytes 786440 | tf_op jit(solution)/shard_map/ppermute | solution.py:393
  109.8 3.1 %copy-start.1 = (bf16[1,1,256,2560]{3,2,1,0:T(8,128)(2,1)S(1)}, bf16[1,1,256,2560]{3,2,1,0:T(8,128)(2,1)}, u32[]{:S(2)}) copy-start(bf16[1,1,256,2560]{3,2,1,0:T(8,128)(2,1)} %param.10) | copy-start | bytes 3932164
  109.8 3.1 %copy-start.9 = (bf16[1,1,256,2560]{3,2,1,0:T(8,128)(2,1)S(1)}, bf16[1,1,256,2560]{3,2,1,0:T(8,128)(2,1)}, u32[]{:S(2)}) copy-start(bf16[1,1,256,2560]{3,2,1,0:T(8,128)(2,1)} %param.11) | copy-start | bytes 3932164
  109.8 3.1 %copy-start.14 = (f32[1,1,256]{2,1,0:T(1,128)S(1)}, f32[1,1,256]{2,1,0:T(1,128)}, u32[]{:S(2)}) copy-start(f32[1,1,256]{2,1,0:T(1,128)} %param.12) | copy-start | bytes 3076
  110.5 10.6 %slice-start = ((s8[5242880]{0:T(1024)(128)(4,1)}), s8[4194304]{0:T(1024)(128)(4,1)S(1)}, s32[]{:S(2)}) async-start(s8[5242880]{0:T(1024)(128)(4,1)} %bitcast.184), calls=%async_computation | async-start | bytes 8388608
  112.9 8.2 %slice-start.1 = ((s8[5242880]{0:T(1024)(128)(4,1)}), s8[1048576]{0:T(1024)(128)(4,1)S(1)}, s32[]{:S(2)}) async-start(s8[5242880]{0:T(1024)(128)(4,1)} %bitcast.184), calls=%async_computation.1 | async-start | bytes 2097152
  129.0 2.1 copy-start.3
  129.0 2.1 copy-start.8
  133.2 7.0 %copy-start.12 = (bf16[1,1280,2,256]{3,1,2,0:T(8,128)(2,1)S(1)}, bf16[1,1280,2,256]{3,1,2,0:T(8,128)(2,1)}, u32[]{:S(2)}) copy-start(bf16[1,1280,2,256]{3,1,2,0:T(8,128)(2,1)} %copy-done.11) | copy-start | bytes 3932164
  133.3 10.3 %collective-permute-start.10 = (bf16[1,256,512]{1,2,0:T(8,128)(2,1)S(1)}, bf16[1,256,512]{1,2,0:T(8,128)(2,1)S(1)}, u32[]{:S(2)}, u32[]{:S(2)}) collective-permute-start(bf16[1,256,512]{1,2,0:T(8,128)(2,1)S(1)} %get-tuple-element.24), channel_id=1, source_target_pairs={{3,0},{4,1},{5,2},{6,3},{7,4},{11,8},{12,9},{13,10},{14,11},{15,12... | collective-permute-start | bytes 786440 | tf_op jit(solution)/shard_map/ppermute | solution.py:393
  134.7 19.4 %collective-permute-start.11 = (bf16[1,256,512]{1,2,0:T(8,128)(2,1)S(1)}, bf16[1,256,512]{1,2,0:T(8,128)(2,1)S(1)}, u32[]{:S(2)}, u32[]{:S(2)}) collective-permute-start(bf16[1,256,512]{1,2,0:T(8,128)(2,1)S(1)} %get-tuple-element.23), channel_id=1, source_target_pairs={{4,0},{5,1},{6,2},{7,3},{12,8},{13,9},{14,10},{15,11},{20,16},{21,... | collective-permute-start | bytes 786440 | tf_op jit(solution)/shard_map/ppermute | solution.py:393
  136.0 19.4 %collective-permute-start.8 = (bf16[1,256,512]{1,2,0:T(8,128)(2,1)S(1)}, bf16[1,256,512]{1,2,0:T(8,128)(2,1)S(1)}, u32[]{:S(2)}, u32[]{:S(2)}) collective-permute-start(bf16[1,256,512]{1,2,0:T(8,128)(2,1)S(1)} %get-tuple-element.22), channel_id=1, source_target_pairs={{1,0},{2,1},{3,2},{4,3},{5,4},{6,5},{7,6},{9,8},{10,9},{11,10},{12... | collective-permute-start | bytes 786440 | tf_op jit(solution)/shard_map/ppermute | solution.py:393
  137.3 19.4 %collective-permute-start.9 = (bf16[1,256,512]{1,2,0:T(8,128)(2,1)S(1)}, bf16[1,256,512]{1,2,0:T(8,128)(2,1)S(1)}, u32[]{:S(2)}, u32[]{:S(2)}) collective-permute-start(bf16[1,256,512]{1,2,0:T(8,128)(2,1)S(1)} %get-tuple-element.25), channel_id=1, source_target_pairs={{2,0},{3,1},{4,2},{5,3},{6,4},{7,5},{10,8},{11,9},{12,10},{13,11},... | collective-permute-start | bytes 786440 | tf_op jit(solution)/shard_map/ppermute | solution.py:393
  138.7 18.2 %collective-permute-start.12 = (bf16[1,256,512]{1,2,0:T(8,128)(2,1)S(1)}, bf16[1,256,512]{1,2,0:T(8,128)(2,1)S(1)}, u32[]{:S(2)}, u32[]{:S(2)}) collective-permute-start(bf16[1,256,512]{1,2,0:T(8,128)(2,1)S(1)} %get-tuple-element.26), channel_id=1, source_target_pairs={{1,0},{2,1},{3,2},{4,3},{5,4},{6,5},{7,6},{9,8},{10,9},{11,10},{12... | collective-permute-start | bytes 786440 | tf_op jit(solution)/shard_map/ppermute | solution.py:393
  141.1 31.7 %copy-start.2 = (bf16[1,1,256,2560]{3,2,1,0:T(8,128)(2,1)S(1)}, bf16[1,1,256,2560]{3,2,1,0:T(8,128)(2,1)}, u32[]{:S(2)}) copy-start(bf16[1,1,256,2560]{3,2,1,0:T(8,128)(2,1)} %param.10) | copy-start | bytes 3932164
  143.6 22.1 %collective-permute-start.13 = (bf16[1,256,512]{1,2,0:T(8,128)(2,1)S(1)}, bf16[1,256,512]{1,2,0:T(8,128)(2,1)S(1)}, u32[]{:S(2)}, u32[]{:S(2)}) collective-permute-start(bf16[1,256,512]{1,2,0:T(8,128)(2,1)S(1)} %get-tuple-element.29), channel_id=1, source_target_pairs={{2,0},{3,1},{4,2},{5,3},{6,4},{7,5},{10,8},{11,9},{12,10},{13,11},... | collective-permute-start | bytes 786440 | tf_op jit(solution)/shard_map/ppermute | solution.py:393
  154.2 11.7 %collective-permute-start.14 = (bf16[1,256,512]{1,2,0:T(8,128)(2,1)S(1)}, bf16[1,256,512]{1,2,0:T(8,128)(2,1)S(1)}, u32[]{:S(2)}, u32[]{:S(2)}) collective-permute-start(bf16[1,256,512]{1,2,0:T(8,128)(2,1)S(1)} %get-tuple-element.28), channel_id=1, source_target_pairs={{3,0},{4,1},{5,2},{6,3},{7,4},{11,8},{12,9},{13,10},{14,11},{15,12... | collective-permute-start | bytes 786440 | tf_op jit(solution)/shard_map/ppermute | solution.py:393
  155.5 17.2 %collective-permute-start.15 = (bf16[1,256,512]{1,2,0:T(8,128)(2,1)S(1)}, bf16[1,256,512]{1,2,0:T(8,128)(2,1)S(1)}, u32[]{:S(2)}, u32[]{:S(2)}) collective-permute-start(bf16[1,256,512]{1,2,0:T(8,128)(2,1)S(1)} %get-tuple-element.27), channel_id=1, source_target_pairs={{4,0},{5,1},{6,2},{7,3},{12,8},{13,9},{14,10},{15,11},{20,16},{21,... | collective-permute-start | bytes 786440 | tf_op jit(solution)/shard_map/ppermute | solution.py:393
  286.9 2.4 copy-start.5
  286.9 2.6 copy-start.10
  (2 other events, 2.3 us)

commit v2 on v1

v2 whole, which is shorter than its diff:
```python
import functools
import jax
import jax.numpy as jnp
from jax import lax
from jax.experimental import pallas as pl
from jax.experimental.pallas import tpu as pltpu
from jax.sharding import PartitionSpec as P

MESH = pl.DeviceIdType.MESH
BF16 = jnp.bfloat16
F32 = jnp.float32
WINDOW = 1024

epsilon = 1e-06
masked_score = -1e30

SIDE = 4


def place():
    dp, ctx = lax.axis_index("dp"), lax.axis_index("ctx")
    return {"x": lax.rem(dp, SIDE), "z": lax.div(dp, SIDE), "y": lax.div(ctx, 2), "c": lax.rem(ctx, 2)}


def device(at):
    return (at["z"] * SIDE + at["x"], at["y"] * 2 + at["c"])


def beside(at, axis, step):
    return {**at, axis: lax.rem(at[axis] + step + SIDE, SIDE)}


def sibling(at):
    return {**at, "c": 1 - at["c"]}


def greet(peers):
    barrier = pltpu.get_barrier_semaphore()
    for peer in peers:
        pl.semaphore_signal(barrier, inc=1, device_id=device(peer), device_id_type=MESH)
    pl.semaphore_wait(barrier, len(peers))


def gather_kernel(rows_in, rows_out, in_ref, out_ref, x_ref, p_ref, w_out, w_in, slots_in, slots_out, wide, block_in,
                  block_out, swap_send, swap_recv, pair_sem, local_sem, ring_send, ring_recv, twin_send, twin_recv):
    at = place()
    c = at["c"]
    ctx = at["y"] * 2 + c
    twin = sibling(at)
    others = [lax.rem(ctx + k, 8) for k in range(1, 8)]
    group = [{**at, "y": lax.div(j, 2), "c": lax.rem(j, 2)} for j in others]
    greet([beside(at, "x", 1), beside(at, "x", -1), beside(at, "z", 1), beside(at, "z", -1)] + group)

    copies = []
    for k in range(7):
        copies.append(pltpu.make_async_remote_copy(
            in_ref.at[others[k]], slots_in.at[ctx], swap_send.at[k], swap_recv.at[k],
            device_id=device(group[k]), device_id_type=MESH))
    pair = pltpu.make_async_remote_copy(
        out_ref.at[1 - c], slots_out.at[c], pair_sem.at[0], pair_sem.at[1], device_id=device(twin), device_id_type=MESH)
    pair.start()
    for copy in copies:
        copy.start()
    slots_in[ctx] = in_ref[ctx]
    slots_out[c] = out_ref[c]
    pair.wait()
    block_out[0, 0, 0] = jnp.concatenate(
        [slots_out[0].astype(F32)[:rows_out], slots_out[1].astype(F32)[:rows_out]], axis=0).astype(BF16)
    for copy in copies:
        copy.wait()
    for j in range(8):
        wide[rows_in * j:rows_in * (j + 1)] = slots_in[j].astype(F32)[:rows_in]
    block_in[0, 0, 0] = wide[...].astype(BF16)

    half_rows = rows_in * 4
    one = {a: pl.ds(at[a], 1) for a in "xyz"}
    whole = pl.ds(0, SIDE)

    def view(part, where, core):
        if part == 2:
            return w_out.at[where["z"], where["x"], where["y"], :, pl.ds(pl.multiple_of(core * 1280, 128), 1280)]
        rows = pl.ds(half_rows * part, half_rows)
        return w_in.at[where["y"], where["z"], where["x"], rows, pl.ds(pl.multiple_of(core * 256, 128), 256)]

    def rest(part):
        return [
            pltpu.make_async_copy(block_in.at[:, :, :, pl.ds(half_rows * p, half_rows), :] if p < 2 else block_out,
                                  view(p, one, c), local_sem.at[p])
            for p in part]

    stores = rest(range(3))
    for copy in stores:
        copy.start()
    for copy in stores:
        copy.wait()

    orders = ("xyz", "yzx", "zxy")
    twins, sends = [], []

    def to_twin(part, where, slot):
        copy = pltpu.make_async_remote_copy(
            view(part, where, c), view(part, where, c), twin_send.at[part, slot], twin_recv.at[part, slot],
            device_id=device(twin), device_id_type=MESH)
        copy.start()
        twins.append(copy)

    def ring(part, phase, slot, where, step):
        axis = orders[part][phase]
        copy = pltpu.make_async_remote_copy(
            view(part, where, c), view(part, where, c), ring_send.at[part, phase, slot], ring_recv.at[part, phase, slot],
            device_id=device(beside(at, axis, step)), device_id_type=MESH)
        copy.start()
        sends.append(copy)
        return copy

    for phase in range(3):
        def known(part, shift, half):
            order = orders[part]
            where = dict(one)
            for a in order[:phase]:
                where[a] = whole
            if phase and half is not None:
                where[order[0]] = pl.ds(2 * half, 2)
            axis = order[phase]
            where[axis] = pl.ds(lax.rem(at[axis] + shift + SIDE, SIDE), 1)
            return where

        first, last = {}, {}
        halves = (0, 1) if phase else (None,)
        for part in range(3):
            if phase:
                first[part] = (ring(part, phase, 0, known(part, 0, 0), 1), ring(part, phase, 1, known(part, 0, 1), -1))
                last[part] = [ring(part, phase, 2, known(part, 0, 1), 1), ring(part, phase, 3, known(part, 0, 0), -1)]
            else:
                first[part] = (ring(part, 0, 0, known(part, 0, None), 1),)
                last[part] = [ring(part, 0, 1, known(part, 0, None), -1)]
        if phase == 2:
            for part in range(3):
                to_twin(part, known(part, 0, None), 0)
        for part in range(3):
            if phase:
                first[part][0].wait_recv()
                last[part].append(ring(part, phase, 4, known(part, -1, 0), 1))
                first[part][1].wait_recv()
                last[part].append(ring(part, phase, 5, known(part, 1, 1), -1))
                if phase == 2:
                    to_twin(part, known(part, -1, 0), 1)
                    to_twin(part, known(part, 1, 1), 2)
            else:
                first[part][0].wait_recv()
                last[part].append(ring(part, 0, 4, known(part, -1, None), 1))
        for n in range(4):
            for part in range(3):
                if n < len(last[part]):
                    last[part][n].wait_recv()
                    if phase == 2:
                        shift, half = ((-1, 1), (1, 0), (-2, 0), (2, 1))[n]
                        to_twin(part, known(part, shift, half), 3 + n)
    for copy in twins:
        copy.wait_recv()

    def project(n, carry):
        weights = w_in[n].reshape(128 * rows_in, 512)
        p_ref[n] = jnp.dot(x_ref[...], weights, preferred_element_type=F32).astype(BF16)
        return carry
    lax.fori_loop(0, 4, project, 0)
    for copy in sends + twins:
        copy.wait_send()


def gather_and_project(normed, w_query, w_key, w_value, w_out):
    rows_in, rows_out = w_query.shape[0], w_out.shape[0]
    joined = jnp.concatenate([w_query, w_key, w_value], axis=1)
    pieces_in = jnp.pad(joined.reshape(rows_in, 8, 256).transpose(1, 0, 2), ((0, 0), (0, 32 - rows_in), (0, 0)))
    pieces_out = jnp.pad(w_out.reshape(rows_out, 2, 1280).transpose(1, 0, 2), ((0, 0), (0, 16 - rows_out), (0, 0)))
    vmem = pl.BlockSpec(memory_space=pltpu.VMEM)
    hbm = pl.BlockSpec(memory_space=pl.ANY)
    dma = pltpu.SemaphoreType.DMA
    projected, whole_out = pl.pallas_call(
        functools.partial(gather_kernel, rows_in, rows_out),
        out_shape=(
            jax.ShapeDtypeStruct((4, normed.shape[0], 512), BF16),
            jax.ShapeDtypeStruct((SIDE, SIDE, SIDE, 2 * rows_out, 2560), BF16),
        ),
        in_specs=[vmem, vmem, vmem],
        out_specs=(vmem, hbm),
        scratch_shapes=[
            pltpu.VMEM((SIDE, SIDE, SIDE, 8 * rows_in, 512), BF16),
            pltpu.VMEM((8, 32, 256), BF16),
            pltpu.VMEM((2, 16, 1280), BF16),
            pltpu.VMEM((8 * rows_in, 256), F32),
            pltpu.VMEM((1, 1, 1, 8 * rows_in, 256), BF16),
            pltpu.VMEM((1, 1, 1, 2 * rows_out, 1280), BF16),
            dma((7,)), dma((7,)), dma((2,)), dma((3,)),
            dma((3, 3, 6)), dma((3, 3, 6)), dma((3, 7)), dma((3, 7)),
        ],
        compiler_params=pltpu.CompilerParams(
            collective_id=0, has_side_effects=True, vmem_limit_bytes=40 * 2**20),
        name="gather_and_project",
    )(pieces_in, pieces_out, normed)
    return projected, whole_out.reshape(128 * rows_out, 2560)


def add_rows(count, step, body):
    def at(i, carry):
        body(pl.ds(pl.multiple_of(i * step, step), step))
        return carry
    lax.fori_loop(0, count // step, at, 0)


HEADS, GROUPS, ROWS, WIDE = 4, 2, 256, 2560
NEAR_UP = 64
NEAR_MID = 160
FAR_DOWN = 80
FAR_MID = 160
CHUNKS = ((1, 0), (1, 1), (0, 0), (0, 1), (0, 2), (0, 3))


def dot(a, b, contract=((1,), (0,))):
    return lax.dot_general(a, b, (contract, ((), ())), preferred_element_type=F32)


def layer_kernel(p_ref, mask_ref, rewards_ref, normed_ref, tokens_ref, target_ref, weight_ref,
                 own_in, own_out, mate_in, mate_out, *scratch):
    (queries, kv, kv_relay, probs, scores, terms, term_mate, term_next, term_far, term_relay, term_end, x_one, x_two,
     weight, turned, mixed, mixed_turned, mixed_grad, joined,
     give_in, give_out, sum_in, sum_out, twin_in, twin_out, far_in, far_out, near_in, near_out, done_in, done_out,
     read_sem, kv_send, kv_recv, term_send, term_recv, twin_send, twin_recv,
     far_send, far_recv, near_send, near_recv, mate_send, mate_recv, keep_sem) = scratch
    at = place()
    c, y = at["c"], at["y"]
    twin = sibling(at)
    up, down = beside(at, "y", 1), beside(at, "y", -1)
    x_flip = {**at, "x": at["x"] + 1 - 2 * lax.rem(at["x"], 2)}
    x_turn = {**at, "x": SIDE - 1 - at["x"]}
    z_flip = {**at, "z": at["z"] + 1 - 2 * lax.rem(at["z"], 2)}
    z_turn = {**at, "z": SIDE - 1 - at["z"]}
    sent = []

    def remote(src, dst, send, recv, to):
        copy = pltpu.make_async_remote_copy(src, dst, send, recv, device_id=device(to), device_id_type=MESH)
        copy.start()
        sent.append(copy)
        return copy

    def read(src, dst, n):
        copy = pltpu.make_async_copy(src, dst, read_sem.at[n])
        copy.start()
        return copy

    read_normed = read(normed_ref, x_one, 0)
    for n in range(2):
        for g in range(2):
            queries[2 * n + g] = p_ref[n, :, 256 * g:256 * g + 256]
            kv[4 + c, 2 * n + g] = p_ref[2 + n, :, 256 * g:256 * g + 256]
    greet([twin, up, down, x_flip, x_turn, z_flip, z_turn])

    def rows_of(slot, low, high):
        return kv.at[slot, :, pl.ds(low, high - low), :]

    def kv_move(src, dst, n, to):
        return remote(src, dst, kv_send.at[n], kv_recv.at[n], to)

    here, before, first = 4 + c, 2 + c, c
    a0 = kv_move(rows_of(here, 0, NEAR_UP), rows_of(before, 0, NEAR_UP), 0, up)
    b0 = kv_move(rows_of(here, NEAR_UP, NEAR_MID), kv_relay.at[:, pl.ds(0, NEAR_MID - NEAR_UP), :], 1, down)
    a1 = kv_move(rows_of(here, NEAR_UP, ROWS), rows_of(before, NEAR_UP, ROWS), 2, up)
    b1 = kv_move(rows_of(here, NEAR_MID, ROWS), kv_relay.at[:, pl.ds(NEAR_MID - NEAR_UP, ROWS - NEAR_MID), :], 3, down)
    t0 = kv_move(kv.at[here], kv.at[here], 4, twin)
    read_weight = read(weight_ref, weight, 1)
    read_tokens = read(tokens_ref, x_two, 2)

    read_normed.wait()

    def turn(i, carry):
        cols = pl.ds(pl.multiple_of(i * 128, 128), 128)
        turned[cols, :] = x_one[:, cols].astype(F32).T.astype(BF16)
        return carry

    a0.wait_recv()
    a2 = kv_move(rows_of(before, 0, NEAR_UP), rows_of(first, 0, NEAR_UP), 5, up)
    lax.fori_loop(0, 10, turn, 0)
    b0.wait_recv()
    b2 = kv_move(kv_relay.at[:, pl.ds(0, NEAR_MID - NEAR_UP), :], rows_of(first, NEAR_UP, NEAR_MID), 6, down)
    lax.fori_loop(10, WIDE // 128, turn, 0)
    read_target = read(target_ref, x_one, 3)
    b1.wait_recv()
    b3 = kv_move(kv_relay.at[:, pl.ds(NEAR_MID - NEAR_UP, ROWS - NEAR_MID), :], rows_of(first, NEAR_MID, ROWS), 7, down)
    a1.wait_recv()
    t1 = kv_move(kv.at[before], kv.at[before], 8, twin)
    a2.wait_recv()
    b2.wait_recv()
    t2 = kv_move(rows_of(first, 0, NEAR_MID), rows_of(first, 0, NEAR_MID), 9, twin)
    b3.wait_recv()
    t3 = kv_move(rows_of(first, NEAR_MID, ROWS), rows_of(first, NEAR_MID, ROWS), 10, twin)
    for copy in (t0, t1, t2, t3):
        copy.wait_recv()

    def tile(n):
        return kv[pl.ds(c, 5), n].reshape(5 * ROWS, 256)

    def attend(h, carry):
        g = h // 2
        seen = mask_ref[...] > 0.5
        score = dot(queries[h], tile(g), ((1,), (1,))) * 256 ** -0.5
        score = jnp.where(seen, score, masked_score)
        raised = jnp.where(seen, jnp.exp(score - jnp.max(score, axis=1, keepdims=True)), 0.0)
        prob = (raised / jnp.sum(raised, axis=1, keepdims=True)).astype(BF16)
        probs[h] = prob
        out = dot(prob, tile(2 + g))
        mixed[h] = out.astype(BF16)
        rounded = out.astype(BF16).astype(F32).T.astype(BF16)
        mixed_turned[2 * h] = rounded[:128]
        mixed_turned[2 * h + 1] = rounded[128:]
        return carry
    lax.fori_loop(0, HEADS, attend, 0)

    for copy in (read_weight, read_tokens, read_target):
        copy.wait()

    def error(i, carry):
        cols = pl.ds(pl.multiple_of(i * 512, 512), 512)
        update = sum(dot(mixed[h], weight[256 * h:256 * h + 256, cols]) for h in range(HEADS))
        result = x_two[:, cols].astype(F32) + update
        x_two[:, cols] = (rewards_ref[...] * (result - x_one[:, cols].astype(F32))).astype(BF16)
        return carry
    lax.fori_loop(0, WIDE // 512, error, 0)
    delta = x_two

    y_far, y_up, y_down = lax.rem(y + 2, SIDE), up["y"], down["y"]
    height = {0: WIDE // 8, 1: HEADS * 256 // 8}
    swaps, far, near_own, near_sum, flips, turns, keeps = {}, {}, {}, {}, {}, {}, {}

    def pick(k, inside, outside):
        kind, n = CHUNKS[k]
        return (outside if kind else inside).at[n]

    def columns(k):
        kind, n = CHUNKS[k]
        return pl.ds(1280 * n, 1280) if kind else pl.ds(512 * n, 512)

    def term(k, dst, core):
        kind, n = CHUNKS[k]

        def body(i, carry):
            j = 2 * i + core
            if kind:
                dst[i] = dot(mixed_turned[j], delta[:, 1280 * n:1280 * n + 1280]).astype(BF16)
            else:
                rows = pl.ds(pl.multiple_of(j * 320, 64), 320)
                dst[i] = dot(turned[rows, :], joined[n]).astype(BF16)
            return carry
        lax.fori_loop(0, 4, body, 0)

    def stage_1(k):
        kind, n = CHUNKS[k]
        give = give_out.at[n] if kind else give_in.at[n % 2]
        if k >= 4:
            swaps[k - 2].wait_send()
        term(k, give, 1 - c)
        swaps[k] = pltpu.make_async_remote_copy(
            give, pick(k, twin_in, twin_out), twin_send.at[k], twin_recv.at[k], device_id=device(twin), device_id_type=MESH)
        swaps[k].start()
        term(k, pick(k, sum_in, sum_out), c)

    def stage_2(k):
        rows = height[CHUNKS[k][0]]
        sums, extra = pick(k, sum_in, sum_out), pick(k, twin_in, twin_out)
        fars, nears = pick(k, far_in, far_out), pick(k, near_in, near_out)
        h0, h1 = pl.ds(0, rows // 2), pl.ds(rows // 2, rows // 2)
        swaps[k].wait_recv()

        def add(block):
            def body(r):
                sums[block, r, :] = (sums[block, r, :].astype(F32) + extra[block, r, :].astype(F32)).astype(BF16)
            add_rows(rows, 32, body)
        add(y_far)
        far[k] = (remote(sums.at[y_far, h0], fars.at[0], far_send.at[k, 0], far_recv.at[k, 0], up),
                  remote(sums.at[y_far, h1], fars.at[1], far_send.at[k, 1], far_recv.at[k, 1], down))
        add(y_up)
        add(y_down)
        near_own[k] = (remote(sums.at[y_up, h1], nears.at[0, h1], near_send.at[k, 0], near_recv.at[k, 0], up),
                       remote(sums.at[y_down, h0], nears.at[1, h0], near_send.at[k, 1], near_recv.at[k, 1], down))
        add(y)

    def stage_3(k):
        rows = height[CHUNKS[k][0]]
        half = rows // 2
        sums = pick(k, sum_in, sum_out)
        fars, nears = pick(k, far_in, far_out), pick(k, near_in, near_out)
        h0, h1 = pl.ds(0, half), pl.ds(half, half)
        far[k][0].wait_recv()

        def low(r):
            sums[y_up, r, :] = (sums[y_up, r, :].astype(F32) + fars[0, r, :].astype(F32)).astype(BF16)
        add_rows(half, 32, low)
        one = remote(sums.at[y_up, h0], nears.at[0, h0], near_send.at[k, 2], near_recv.at[k, 2], up)
        far[k][1].wait_recv()

        def high(i, carry):
            r = pl.ds(pl.multiple_of(i * 32, 32), 32)
            s = pl.ds(pl.multiple_of(i * 32 + half, 32), 32)
            sums[y_down, s, :] = (sums[y_down, s, :].astype(F32) + fars[1, r, :].astype(F32)).astype(BF16)
            return carry
        lax.fori_loop(0, half // 32, high, 0)
        near_sum[k] = (one, remote(sums.at[y_down, h1], nears.at[1, h1], near_send.at[k, 3], near_recv.at[k, 3], down))

    def mates(k, level):
        return (mate_out if CHUNKS[k][0] else mate_in).at[level, :, columns(k)]

    def stage_4(k):
        kind, n = CHUNKS[k]
        sums, nears, done = pick(k, sum_in, sum_out), pick(k, near_in, near_out), pick(k, done_in, done_out)
        for copy in near_own[k] + near_sum[k]:
            copy.wait_recv()

        def body(r):
            done[r, :] = (sums[y, r, :].astype(F32) + nears[0, r, :].astype(F32) + nears[1, r, :].astype(F32)).astype(BF16)
        add_rows(height[kind], 32, body)
        flips[k] = (remote(done, mates(k, 0), mate_send.at[k, 0], mate_recv.at[k, 0], x_flip),
                    remote(done, mates(k, 2), mate_send.at[k, 2], mate_recv.at[k, 2], z_flip))
        keeps[k] = pltpu.make_async_copy(done, (own_out if kind else own_in).at[:, columns(k)], keep_sem.at[k])
        keeps[k].start()

    def stage_5(k):
        flips[k][0].wait_recv()
        one = remote(mates(k, 0), mates(k, 1), mate_send.at[k, 1], mate_recv.at[k, 1], x_turn)
        flips[k][1].wait_recv()
        turns[k] = (one, remote(mates(k, 2), mates(k, 3), mate_send.at[k, 3], mate_recv.at[k, 3], z_turn))

    stage_1(0)
    stage_1(1)
    stage_2(0)

    def spread(h, carry):
        rows = pl.ds(pl.multiple_of(h * 256, 256), 256)
        mixed_grad[h] = dot(delta[...], weight[rows, :], ((1,), (1,))).astype(BF16)
        return carry
    lax.fori_loop(0, HEADS, spread, 0)
    stage_2(1)

    terms[5 * (1 - c)] = jnp.zeros((4, ROWS, 256), BF16)

    def back(g):
        for r in range(2):
            h = 2 * g + r
            grad = mixed_grad[h]
            row_dots = jnp.sum(grad.astype(F32) * mixed[h].astype(F32), axis=1, keepdims=True)
            prob_grads = dot(grad, tile(2 + g), ((1,), (1,)))
            score = (probs[h].astype(F32) * (prob_grads - row_dots) * 256 ** -0.5).astype(BF16)
            scores[r] = score
            joined[g, :, 256 * r:256 * r + 256] = dot(score, tile(g)).astype(BF16)
        key_terms = dot(scores[0], queries[2 * g], ((0,), (0,))) + dot(scores[1], queries[2 * g + 1], ((0,), (0,)))
        terms[pl.ds(c, 5), g] = key_terms.astype(BF16).reshape(5, ROWS, 256)
        value_terms = (dot(probs[2 * g], mixed_grad[2 * g], ((0,), (0,)))
                       + dot(probs[2 * g + 1], mixed_grad[2 * g + 1], ((0,), (0,))))
        terms[pl.ds(c, 5), 2 + g] = value_terms.astype(BF16).reshape(5, ROWS, 256)

    back(0)
    stage_3(0)
    back(1)
    stage_3(1)

    def move(src, dst, n, to):
        return remote(src, dst, term_send.at[n], term_recv.at[n], to)

    to_mate = [move(terms.at[2 * n + 1 - c], term_mate.at[n], n, twin) for n in range(3)]
    stage_4(0)
    stage_1(2)

    def fold(n):
        to_mate[n].wait_recv()
        for q in range(4):
            def body(r):
                terms[2 * n + c, q, r, :] = (
                    terms[2 * n + c, q, r, :].astype(F32) + term_mate[n, q, r, :].astype(F32)).astype(BF16)
            add_rows(ROWS, 64, body)

    def part(ref, low, high, start=0):
        return ref.at[:, pl.ds(low - start, high - low), :]

    fold(0)
    s2 = terms.at[c]
    e0 = move(part(s2, 0, FAR_DOWN), term_far, 3, down)
    f0 = move(part(s2, FAR_DOWN, FAR_MID), part(term_relay, FAR_DOWN, FAR_MID, FAR_DOWN), 4, up)
    f1 = move(part(s2, FAR_MID, ROWS), part(term_relay, FAR_MID, ROWS, FAR_DOWN), 5, up)
    fold(1)
    s1 = terms.at[2 + c]
    e1 = move(part(s1, FAR_DOWN, ROWS), part(term_next, FAR_DOWN, ROWS), 6, down)
    fold(2)
    stage_1(3)
    stage_2(2)
    e0.wait_recv()
    for q in range(4):
        def join(r):
            terms[2 + c, q, r, :] = (terms[2 + c, q, r, :].astype(F32) + term_far[q, r, :].astype(F32)).astype(BF16)
        add_rows(FAR_DOWN, 16, join)
    e2 = move(part(s1, 0, FAR_DOWN), part(term_next, 0, FAR_DOWN), 7, down)
    f0.wait_recv()
    f2 = move(part(term_relay, FAR_DOWN, FAR_MID, FAR_DOWN), part(term_end, FAR_DOWN, FAR_MID, FAR_DOWN), 8, up)
    f1.wait_recv()
    f3 = move(part(term_relay, FAR_MID, ROWS, FAR_DOWN), part(term_end, FAR_MID, ROWS, FAR_DOWN), 9, up)
    stage_4(1)
    stage_2(3)
    stage_5(0)
    stage_3(2)
    for copy in (e1, e2, f2, f3):
        copy.wait_recv()
    for q in range(4):
        n, g = 2 + q // 2, q % 2
        joined[n, 0:FAR_DOWN, 256 * g:256 * g + 256] = (
            terms[4 + c, q, 0:FAR_DOWN, :].astype(F32) + term_next[q, 0:FAR_DOWN, :].astype(F32)).astype(BF16)
        joined[n, FAR_DOWN:ROWS, 256 * g:256 * g + 256] = (
            terms[4 + c, q, FAR_DOWN:ROWS, :].astype(F32) + term_next[q, FAR_DOWN:ROWS, :].astype(F32)
            + term_end[q].astype(F32)).astype(BF16)
    stage_1(4)
    stage_1(5)
    stage_2(4)
    stage_3(3)
    stage_4(2)
    stage_5(1)
    stage_2(5)
    stage_3(4)
    stage_4(3)
    stage_5(2)
    stage_3(5)
    stage_4(4)
    stage_5(3)
    stage_4(5)
    stage_5(4)
    stage_5(5)
    for k in range(6):
        turns[k][0].wait_recv()
        turns[k][1].wait_recv()
        keeps[k].wait()
    for k in (0, 1, 4, 5):
        swaps[k].wait_send()
    for copy in sent:
        copy.wait_send()


def layer_grads(projected, mask, rewards, normed, tokens, target, weight):
    vmem = pl.BlockSpec(memory_space=pltpu.VMEM)
    hbm = pl.BlockSpec(memory_space=pl.ANY)
    dma = pltpu.SemaphoreType.DMA
    ri, ro = WIDE // 8, HEADS * 256 // 8

    def held(*shape):
        return pltpu.VMEM(shape, BF16)

    return pl.pallas_call(
        layer_kernel,
        out_shape=(
            jax.ShapeDtypeStruct((ri, 2048), BF16), jax.ShapeDtypeStruct((ro, WIDE), BF16),
            jax.ShapeDtypeStruct((4, ri, 2048), BF16), jax.ShapeDtypeStruct((4, ro, WIDE), BF16),
        ),
        in_specs=[vmem, vmem, vmem, hbm, hbm, hbm, hbm],
        out_specs=(hbm,) * 4,
        scratch_shapes=[
            held(HEADS, ROWS, 256), held(6, 4, ROWS, 256), held(4, ROWS - NEAR_UP, 256),
            held(HEADS, ROWS, 5 * ROWS), held(2, ROWS, 5 * ROWS),
            held(6, 4, ROWS, 256), held(3, 4, ROWS, 256), held(4, ROWS, 256), held(4, FAR_DOWN, 256),
            held(4, ROWS - FAR_DOWN, 256), held(4, ROWS - FAR_DOWN, 256),
            held(ROWS, WIDE), held(ROWS, WIDE), held(HEADS * 256, WIDE), held(WIDE, ROWS),
            held(HEADS, ROWS, 256), held(8, 128, ROWS), held(HEADS, ROWS, 256), held(4, ROWS, 512),
            held(2, 4, ri, 512), held(2, 4, ro, 1280),
            held(4, 4, ri, 512), held(2, 4, ro, 1280), held(4, 4, ri, 512), held(2, 4, ro, 1280),
            held(4, 2, ri // 2, 512), held(2, 2, ro // 2, 1280), held(4, 2, ri, 512), held(2, 2, ro, 1280),
            held(4, ri, 512), held(2, ro, 1280),
            dma((4,)), dma((11,)), dma((11,)), dma((10,)), dma((10,)), dma((6,)), dma((6,)),
            dma((6, 2)), dma((6, 2)), dma((6, 4)), dma((6, 4)), dma((6, 4)), dma((6, 4)), dma((6,)),
        ],
        compiler_params=pltpu.CompilerParams(
            collective_id=1, has_side_effects=True, vmem_limit_bytes=62 * 2**20),
        name="layer_grads",
    )(projected, mask, rewards, normed, tokens, target, weight)


def norm_rows(inputs, norm_gain):
    values = inputs.astype(jnp.float32)
    power = jnp.mean(values * values, axis=-1, keepdims=True)
    return (values * lax.rsqrt(power + epsilon) * norm_gain).astype(jnp.bfloat16)


def doc_index(positions, lengths):
    count = lengths.shape[-1]
    upto = jnp.arange(count)[:, None] >= jnp.arange(count)[None, :]
    endings = jnp.sum(jnp.where(upto[None], lengths[:, None, :], 0), axis=-1)
    return jnp.sum((endings[:, None, :] <= positions[:, :, None]).astype(jnp.int32), axis=-1)


def allowed(query_pos, key_pos, lengths):
    query_doc = doc_index(query_pos, lengths)
    key_doc = doc_index(key_pos, lengths)
    distance = query_pos[:, :, None] - key_pos[:, None, :]
    same_doc = query_doc[:, :, None] == key_doc[:, None, :]
    return (key_pos[:, None, :] >= 0) & same_doc & (distance >= 0) & (distance < WINDOW)


def per_device(
    tokens, target, rewards, doc_lengths, norm_gain, w_query, w_key, w_value, w_out, gossip_bit
):
    shard_len = tokens.shape[2]
    query_width, key_width = w_query.shape[1], w_key.shape[1]
    reach_blocks = WINDOW // shard_len
    span_len = (reach_blocks + 1) * shard_len
    ctx_index = lax.axis_index("ctx")
    token_rows, target_rows = tokens[0, 0], target[0, 0]
    normed = norm_rows(token_rows, norm_gain)
    projected, out_whole = gather_and_project(normed, w_query, w_key, w_value, w_out)
    query_pos = (ctx_index * shard_len + jnp.arange(shard_len, dtype=jnp.int32))[None]
    key_pos = ((ctx_index - reach_blocks) * shard_len + jnp.arange(span_len, dtype=jnp.int32))[None]
    mask = allowed(query_pos, key_pos, doc_lengths[0])[0].astype(jnp.float32)
    grad_inputs, grad_outputs, mates_in, mates_out = layer_grads(
        projected, mask, rewards.reshape(shard_len, 1), normed, token_rows, target_rows, out_whole
    )
    own_bit = gossip_bit[0]
    partner_inputs, partner_outputs = mates_in[0], mates_out[0]
    for level in range(1, 4):
        partner_inputs = jnp.where(own_bit == level, mates_in[level], partner_inputs)
        partner_outputs = jnp.where(own_bit == level, mates_out[level], partner_outputs)
    mean_inputs = (grad_inputs.astype(jnp.float32) + partner_inputs.astype(jnp.float32)) * 0.5
    mean_outputs = (grad_outputs.astype(jnp.float32) + partner_outputs.astype(jnp.float32)) * 0.5
    return (
        mean_inputs[None, :, :query_width],
        mean_inputs[None, :, query_width : query_width + key_width],
        mean_inputs[None, :, query_width + key_width :],
        mean_outputs[None],
    )


def solution(mesh):
    placed = (
        P("dp", None, "ctx", None),
        P("dp", None, "ctx", None),
        P("dp", None, "ctx"),
        P("dp", None, None),
        P(),
        P(("dp", "ctx"), None),
        P(("dp", "ctx"), None),
        P(("dp", "ctx"), None),
        P(("dp", "ctx"), None),
        P("dp"),
    )
    return jax.shard_map(
        per_device,
        mesh=mesh,
        in_specs=placed,
        out_specs=(
            P("dp", "ctx", None),
            P("dp", "ctx", None),
            P("dp", "ctx", None),
            P("dp", "ctx", None),
        ),
        check_vma=False,
    )
```

time: 293 us -> 214 us (0.73)
  Pallas kernels: 158 us -> 196 us
  waiting for transfers between devices: 33 us -> 0 us
  matrix products: 31.8 us -> 0 us
  starting transfers between devices: 29.7 us -> 0 us
  local copies, waits for them, and re-layouts: 24 us -> 7.96 us
  other arithmetic: 12.1 us -> 9.13 us
    pallas_call x2, Pallas kernels: 158 us -> 196 us  [the longest x1 143 us: layer_grads(): pl.pallas_call(layer_kernel, out_shape=(jax.ShapeDtypeStruct((ri, 2048),...]
    ppermute x16 -> x0, waiting for transfers between devices: 33 us -> none  [shifted(): return lax.ppermute(block, axis, route)]
    dot_general x14 -> x0, matrix products: 31.8 us -> none  [the longest x1 6.91 us: per_device(): lax.dot_general(flat_rows, joined, (((0,), (0,)), ((), ())), preferred_el...]
    ppermute x16 -> x0, starting transfers between devices: 29.7 us -> none  [shifted(): return lax.ppermute(block, axis, route)]
    slice x3 -> x0, local copies, waits for them, and re-layouts: 6.36 us -> none  [the longest x1 6.22 us: per_device(): weights_in[n]]
    concatenate x8 -> x0, local copies, waits for them, and re-layouts: 5.27 us -> none  [the longest x6 5.18 us: per_device(): value_tile = jnp.concatenate(value_parts + [value_own], axis=1)]
  transfers between devices with their start and end apart: 16 -> 0, of which waited for: 7 -> 0; matrix products, arithmetic and copies ran while one was open for 6% -> 0% of each run, Pallas kernels for 0% -> 0%
where the time goes in v2:
time: 214 us
  Pallas kernels  196 us (92%)
  other arithmetic  9.13 us (4%)
  local copies, waits for them, and re-layouts  7.96 us (4%)
    pallas_call x1, Pallas kernels, layer_grads(): pl.pallas_call(layer_kernel, out_shape=(jax.ShapeDtypeStruct((ri, 2048),...  143 us
    pallas_call x1, Pallas kernels, gather_and_project(): pl.pallas_call(functools.partial(gather_kernel, rows_in, rows_out), out_s...  52.3 us
    unnamed x25, local copies, waits for them, and re-layouts  4.74 us

profile of v2, /device:TPU:0, one launch (start us, length us, event | category | flops | bytes accessed | tf_op | source)
XLA Modules:
  0.0 214.2 jit_solution(9285641309197059362)
XLA Ops:
  0.6 0.0 copy-start.3
  0.7 0.9 fusion.11
  1.6 0.1 fusion.9
  1.7 0.1 fusion.10
  1.8 0.0 copy-start.10
  1.9 1.6 fusion.8.mask_ref
  3.5 0.0 copy-done.3
  3.5 0.3 fusion
  3.8 0.0 copy-done.10
  3.8 0.0 copy-start.6
  3.8 0.0 copy-start.8
  3.8 0.0 copy-start.9
  3.8 0.0 copy-start.7
  3.9 0.4 fusion.2.x_ref.normed_ref
  4.2 0.4 copy-done.6
  4.6 0.0 copy-done.8
  4.6 0.0 copy-done.9
  4.7 0.0 copy-done.7
  4.8 52.3 %gather_and_project.1 = (bf16[4,256,512]{2,1,0:T(8,128)(2,1)S(1)}, bf16[4,4,4,16,2560]{4,3,2,1,0:T(8,128)(2,1)S(1)}) custom-call(bf16[8,32,256]{2,1,0:T(8,128)(2,1)S(1)} %pad.8.in_ref, bf16[2,16,1280]{2,1,0:T(8,128)(2,1)S(1)} %pad.9.out_ref, bf16[256,2560]{1,0:T(8,128)(2,1)S(1)} %fusion.2.x_ref.normed_ref), custom_call_target="tpu_custom_call" | custom-call | tf_op jit(solution)/shard_map/gather_and_project/pallas_call | solution.py:179
  57.0 0.0 copy-done
  57.0 0.0 copy-start.1
  57.1 2.3 %copy-done.1 = bf16[4,4,4,16,2560]{4,3,2,1,0:T(8,128)(2,1)} copy-done((bf16[4,4,4,16,2560]{4,3,2,1,0:T(8,128)(2,1)}, bf16[4,4,4,16,2560]{4,3,2,1,0:T(8,128)(2,1)S(1)}, u32[]{:S(2)}) %copy-start.1) | copy-done | bytes 5242904
  59.4 1.0 copy-done.2
  60.3 0.0 copy-done.11
  60.3 0.8 copy.17.rewards_ref
  61.1 143.3 %layer_grads.1 = (bf16[320,2048]{1,0:T(8,128)(2,1)}, bf16[128,2560]{1,0:T(8,128)(2,1)}, bf16[4,320,2048]{2,1,0:T(8,128)(2,1)}, bf16[4,128,2560]{2,1,0:T(8,128)(2,1)}) custom-call(bf16[4,256,512]{2,1,0:T(8,128)(2,1)} %copy-done.2, f32[256,1280]{1,0:T(8,128)} %fusion.8.mask_ref, f32[256,1]{1,0:T(8,128)} %copy.17.rewards_ref, bf16[256,2560]{1,0:T(8,128)(2,1)} %copy-done, ...), custom_call_target="tpu_custom_call" | custom-call | tf_op jit(solution)/shard_map/layer_grads/pallas_call | solution.py:551
  205.1 4.1 %fusion.3 = f32[320,2048]{1,0:T(8,128)S(1)} fusion(bf16[320,2048]{1,0:T(8,128)(2,1)} %get-tuple-element.12, bf16[4,320,2048]{2,1,0:T(8,128)(2,1)} %get-tuple-element.13, pred[]{:T(512)} %bitcast.10, pred[]{:T(512)} %bitcast.9, pred[]{:T(512)} %bitcast.8), kind=kLoop, calls=%fused_computation.6 | loop fusion | flops 4587520 | bytes 9175043 | tf_op jit(solution)/shard_map/mul | solution.py:622
  209.3 1.2 slice_bitcast_fusion.1
  210.5 1.2 slice_bitcast_fusion
  211.7 0.0 copy-done.5
  211.7 1.0 copy-done.4
  212.7 1.5 fusion.5
  (15 shorter events, 0.1 us)
Async XLA Ops:
  0.6 2.8 %copy-start.3 = (bf16[1,1,256,2560]{3,2,1,0:T(8,128)(2,1)S(1)}, bf16[1,1,256,2560]{3,2,1,0:T(8,128)(2,1)}, u32[]{:S(2)}) copy-start(bf16[1,1,256,2560]{3,2,1,0:T(8,128)(2,1)} %param.10) | copy-start | bytes 3932164
  1.8 2.0 copy-start.10
  3.8 0.8 copy-start.6
  3.8 0.8 copy-start.8
  3.8 0.8 copy-start.9
  3.8 0.9 copy-start.7
  4.6 52.4 %copy-start = (bf16[256,2560]{1,0:T(8,128)(2,1)}, bf16[256,2560]{1,0:T(8,128)(2,1)S(1)}, u32[]{:S(2)}) copy-start(bf16[256,2560]{1,0:T(8,128)(2,1)S(1)} %fusion.2.x_ref.normed_ref) | copy-start | bytes 3932164
  4.6 55.7 %copy-start.11 = (f32[1,1,256]{2,1,0:T(1,128)S(1)}, f32[1,1,256]{2,1,0:T(1,128)}, u32[]{:S(2)}) copy-start(f32[1,1,256]{2,1,0:T(1,128)} %param.12) | copy-start | bytes 3076
  57.0 2.3 %copy-start.1 = (bf16[4,4,4,16,2560]{4,3,2,1,0:T(8,128)(2,1)}, bf16[4,4,4,16,2560]{4,3,2,1,0:T(8,128)(2,1)S(1)}, u32[]{:S(2)}) copy-start(bf16[4,4,4,16,2560]{4,3,2,1,0:T(8,128)(2,1)S(1)} %get-tuple-element.11) | copy-start | bytes 15728644
  59.4 1.0 copy-start.2
  209.3 2.4 %copy-start.5 = (bf16[128,2560]{1,0:T(8,128)(2,1)S(1)}, bf16[128,2560]{1,0:T(8,128)(2,1)}, u32[]{:S(2)}) copy-start(bf16[128,2560]{1,0:T(8,128)(2,1)} %get-tuple-element.14) | copy-start | bytes 1966084
  210.4 2.2 %copy-start.4 = (bf16[4,128,2560]{2,1,0:T(8,128)(2,1)S(1)}, bf16[4,128,2560]{2,1,0:T(8,128)(2,1)}, u32[]{:S(2)}) copy-start(bf16[4,128,2560]{2,1,0:T(8,128)(2,1)} %get-tuple-element.15) | copy-start | bytes 7864324

commit v3 on v2

v3 whole, which is shorter than its diff:
```python
import functools
import jax
import jax.numpy as jnp
from jax import lax
from jax.experimental import pallas as pl
from jax.experimental.pallas import tpu as pltpu
from jax.sharding import PartitionSpec as P

MESH = pl.DeviceIdType.MESH
BF16 = jnp.bfloat16
F32 = jnp.float32
WINDOW = 1024

epsilon = 1e-06
masked_score = -1e30

SIDE = 4


def place():
    dp, ctx = lax.axis_index("dp"), lax.axis_index("ctx")
    return {"x": lax.rem(dp, SIDE), "z": lax.div(dp, SIDE), "y": lax.div(ctx, 2), "c": lax.rem(ctx, 2)}


def device(at):
    return (at["z"] * SIDE + at["x"], at["y"] * 2 + at["c"])


def beside(at, axis, step):
    return {**at, axis: lax.rem(at[axis] + step + SIDE, SIDE)}


def sibling(at):
    return {**at, "c": 1 - at["c"]}


def greet(peers):
    barrier = pltpu.get_barrier_semaphore()
    for peer in peers:
        pl.semaphore_signal(barrier, inc=1, device_id=device(peer), device_id_type=MESH)
    pl.semaphore_wait(barrier, len(peers))


HEADS, GROUPS, ROWS, WIDE = 4, 2, 256, 2560
NEAR_UP = 64
NEAR_MID = 160
FAR_DOWN = 80
FAR_MID = 160
CHUNKS = ((1, 0, 0, 1280), (1, 1, 0, 1280), (0, 0, 0, 512), (0, 1, 0, 512), (0, 2, 0, 512), (0, 3, 0, 256), (0, 3, 256, 256))


def dot(a, b, contract=((1,), (0,))):
    return lax.dot_general(a, b, (contract, ((), ())), preferred_element_type=F32)


def add_rows(count, step, body):
    def at(i, carry):
        body(pl.ds(pl.multiple_of(i * step, step), step))
        return carry
    lax.fori_loop(0, count // step, at, 0)


PARTS = (
    ("kv", 0, 64, "xyz"), ("kv", 64, 48, "yzx"), ("kv", 112, 48, "zxy"),
    ("query", 0, 80, "yxz"), ("query", 80, 80, "yzx"),
    ("out", 0, 640, "yxz"), ("out", 640, 640, "yzx"),
)
KV_PARTS, QUERY_PARTS, OUT_PARTS = range(3), range(3, 5), range(5, 7)


def front_kernel(rows_in, rows_out, in_ref, out_ref, tokens_ref, gain_ref, lengths_ref,
                 queries_out, kv_out, turned_out, mask_out, w_out, *scratch):
    (w_kv, w_query, slots_in, slots_out, wide, block_out, x_ref, queries, kv, kv_relay, turned, mask,
     swap_send, swap_recv, pair_sem, local_sem, ring_send, ring_recv, twin_send, twin_recv, kv_send, kv_recv, keep_sem) = scratch
    at = place()
    c = at["c"]
    ctx = at["y"] * 2 + c
    twin = sibling(at)
    up, down = beside(at, "y", 1), beside(at, "y", -1)
    others = [lax.rem(ctx + k, 8) for k in range(1, 8)]
    group = [{**at, "y": lax.div(j, 2), "c": lax.rem(j, 2)} for j in others]
    greet([beside(at, "x", 1), beside(at, "x", -1), beside(at, "z", 1), beside(at, "z", -1)] + group)
    sent = []

    def remote(src, dst, send, recv, to):
        copy = pltpu.make_async_remote_copy(src, dst, send, recv, device_id=device(to), device_id_type=MESH)
        copy.start()
        sent.append(copy)
        return copy

    copies = [remote(in_ref.at[others[k]], slots_in.at[ctx], swap_send.at[k], swap_recv.at[k], group[k]) for k in range(7)]
    pair = remote(out_ref.at[1 - c], slots_out.at[c], pair_sem.at[0], pair_sem.at[1], twin)
    slots_in[ctx] = in_ref[ctx]
    slots_out[c] = out_ref[c]

    def norm(r):
        values = tokens_ref[r, :].astype(F32)
        power = jnp.mean(values * values, axis=1, keepdims=True)
        x_ref[r, :] = (values * lax.rsqrt(power + epsilon) * gain_ref[...]).astype(BF16)

    lane = pl.ds(pl.multiple_of(c * 128, 128), 128)
    for k, copy in enumerate(copies):
        copy.wait_recv()
    for j in range(8):
        wide[rows_in * j:rows_in * (j + 1)] = slots_in[j].astype(F32)[:rows_in]
    w_kv[at["y"], at["z"], at["x"], :, lane] = wide[:, :128].astype(BF16)
    w_query[at["y"], at["z"], at["x"], :, lane] = wide[:, 128:].astype(BF16)

    one = {a: pl.ds(at[a], 1) for a in "xyz"}
    whole = pl.ds(0, SIDE)

    def view(part, where):
        name, start, size, _ = PARTS[part]
        if name == "out":
            cols = pl.ds(pl.multiple_of(c * 1280 + start, 128), size)
            return w_out.at[where["z"], where["x"], where["y"], :, cols]
        ref = w_kv if name == "kv" else w_query
        return ref.at[where["y"], where["z"], where["x"], pl.ds(start, size), lane]

    first, last, twins = {}, {}, {}

    def known(part, phase, shift, half):
        order = PARTS[part][3]
        where = dict(one)
        for a in order[:phase]:
            where[a] = whole
        if phase:
            where[order[0]] = pl.ds(2 * half, 2)
        if half is None and phase:
            where[order[0]] = whole
        axis = order[phase]
        where[axis] = pl.ds(lax.rem(at[axis] + shift + SIDE, SIDE), 1)
        return where

    def ring(part, phase, slot, where, step):
        return remote(view(part, where), view(part, where), ring_send.at[part, phase, slot],
                      ring_recv.at[part, phase, slot], beside(at, PARTS[part][3][phase], step))

    def to_twin(part, where, slot):
        twins.setdefault(part, []).append(
            remote(view(part, where), view(part, where), twin_send.at[part, slot], twin_recv.at[part, slot], twin))

    def begin(part, phase):
        if phase:
            first[part] = (ring(part, phase, 0, known(part, phase, 0, 0), 1), ring(part, phase, 1, known(part, phase, 0, 1), -1))
            last[part] = [ring(part, phase, 2, known(part, phase, 0, 1), 1), ring(part, phase, 3, known(part, phase, 0, 0), -1)]
        else:
            first[part] = (ring(part, 0, 0, known(part, 0, 0, None), 1),)
            last[part] = [ring(part, 0, 1, known(part, 0, 0, None), -1)]

    def share(part):
        where = dict(one)
        for a in PARTS[part][3][:2]:
            where[a] = whole
        to_twin(part, where, 0)

    def relay(part, phase):
        first[part][0].wait_recv()
        if not phase:
            last[part].append(ring(part, 0, 4, known(part, 0, -1, None), 1))
            return
        last[part].append(ring(part, phase, 4, known(part, phase, -1, 0), 1))
        first[part][1].wait_recv()
        last[part].append(ring(part, phase, 5, known(part, phase, 1, 1), -1))
        if phase == 2:
            to_twin(part, known(part, phase, -1, 0), 1)
            to_twin(part, known(part, phase, 1, 1), 2)

    def finish(parts, phase):
        for n in range(4):
            for part in parts:
                if n < len(last[part]):
                    last[part][n].wait_recv()
                    if phase == 2:
                        shift, half = ((-1, 1), (1, 0), (-2, 0), (2, 1))[n]
                        to_twin(part, known(part, phase, shift, half), 3 + n)

    def arrived(parts):
        for part in parts:
            for copy in twins[part]:
                copy.wait_recv()

    later = list(QUERY_PARTS) + list(OUT_PARTS)
    for part in KV_PARTS:
        begin(part, 0)
    for part in QUERY_PARTS:
        begin(part, 0)
    pair.wait_recv()
    block_out[0, 0, 0] = jnp.concatenate(
        [slots_out[0].astype(F32)[:rows_out], slots_out[1].astype(F32)[:rows_out]], axis=0).astype(BF16)
    own_cols = pl.ds(pl.multiple_of(c * 1280, 128), 1280)
    store = pltpu.make_async_copy(block_out, w_out.at[one["z"], one["x"], one["y"], :, own_cols], local_sem)
    store.start()
    for part in KV_PARTS:
        relay(part, 0)
    store.wait()
    for part in OUT_PARTS:
        begin(part, 0)
    finish(KV_PARTS, 0)
    for part in KV_PARTS:
        begin(part, 1)
    add_rows(ROWS // 2, 32, norm)
    for part in later:
        relay(part, 0)
    for part in KV_PARTS:
        relay(part, 1)
    finish(later, 0)
    for part in later:
        begin(part, 1)
    finish(KV_PARTS, 1)
    for part in KV_PARTS:
        begin(part, 2)
        share(part)

    def norm_more(i, carry):
        norm(pl.ds(pl.multiple_of(i * 32, 32), 32))
        return carry
    lax.fori_loop(4, ROWS // 32, norm_more, 0)
    for part in later:
        relay(part, 1)
    finish(later, 1)
    for part in KV_PARTS:
        relay(part, 2)
    for part in QUERY_PARTS:
        begin(part, 2)
    finish(KV_PARTS, 2)
    for part in QUERY_PARTS:
        share(part)
    arrived(KV_PARTS)

    here, before, old = 4 + c, 2 + c, c

    def project_kv(n, carry):
        kv[here, n] = dot(x_ref[...], w_kv[n].reshape(128 * rows_in, 256)).astype(BF16)
        return carry
    lax.fori_loop(0, 4, project_kv, 0)

    def rows_of(slot, low, high):
        return kv.at[slot, :, pl.ds(low, high - low), :]

    def kv_move(src, dst, n, to):
        return remote(src, dst, kv_send.at[n], kv_recv.at[n], to)

    mid = NEAR_MID - NEAR_UP
    a0 = kv_move(rows_of(here, 0, NEAR_UP), rows_of(before, 0, NEAR_UP), 0, up)
    b0 = kv_move(rows_of(here, NEAR_UP, NEAR_MID), kv_relay.at[:, pl.ds(0, mid), :], 1, down)
    a1 = kv_move(rows_of(here, NEAR_UP, ROWS), rows_of(before, NEAR_UP, ROWS), 2, up)
    b1 = kv_move(rows_of(here, NEAR_MID, ROWS), kv_relay.at[:, pl.ds(mid, ROWS - NEAR_MID), :], 3, down)
    t0 = kv_move(kv.at[here], kv.at[here], 4, twin)
    for part in QUERY_PARTS:
        relay(part, 2)
    for part in OUT_PARTS:
        begin(part, 2)

    def turn(i, carry):
        cols = pl.ds(pl.multiple_of(i * 128, 128), 128)
        turned[cols, :] = x_ref[:, cols].astype(F32).T.astype(BF16)
        return carry
    a0.wait_recv()
    a2 = kv_move(rows_of(before, 0, NEAR_UP), rows_of(old, 0, NEAR_UP), 5, up)
    lax.fori_loop(0, 10, turn, 0)
    b0.wait_recv()
    b2 = kv_move(kv_relay.at[:, pl.ds(0, mid), :], rows_of(old, NEAR_UP, NEAR_MID), 6, down)
    finish(QUERY_PARTS, 2)
    for part in OUT_PARTS:
        share(part)
    lax.fori_loop(10, WIDE // 128, turn, 0)
    keep_turned = pltpu.make_async_copy(turned, turned_out, keep_sem.at[0])
    keep_turned.start()
    b1.wait_recv()
    b3 = kv_move(kv_relay.at[:, pl.ds(mid, ROWS - NEAR_MID), :], rows_of(old, NEAR_MID, ROWS), 7, down)
    for part in OUT_PARTS:
        relay(part, 2)

    query_pos = ctx * ROWS + lax.broadcasted_iota(jnp.int32, (ROWS, 1), 0)
    key_pos = (ctx - 4) * ROWS + lax.broadcasted_iota(jnp.int32, (1, 5 * ROWS), 1)
    query_doc, key_doc, ending = 0 * query_pos, 0 * key_pos, 0
    for n in range(lengths_ref.shape[1]):
        ending = ending + lengths_ref[0, n]
        query_doc = query_doc + jnp.where(query_pos >= ending, 1, 0)
        key_doc = key_doc + jnp.where(key_pos >= ending, 1, 0)
    gap = query_pos - key_pos
    seen = (query_doc == key_doc) & (key_pos >= 0) & (gap >= 0) & (gap < WINDOW)
    mask[...] = jnp.where(seen, 1.0, 0.0)
    keep_mask = pltpu.make_async_copy(mask, mask_out, keep_sem.at[1])
    keep_mask.start()

    arrived(QUERY_PARTS)

    def project_query(n, carry):
        queries[n] = dot(x_ref[...], w_query[n].reshape(128 * rows_in, 256)).astype(BF16)
        return carry
    lax.fori_loop(0, 4, project_query, 0)
    keep_queries = pltpu.make_async_copy(queries, queries_out, keep_sem.at[2])
    keep_queries.start()
    a1.wait_recv()
    t1 = kv_move(kv.at[before], kv.at[before], 8, twin)
    a2.wait_recv()
    b2.wait_recv()
    t2 = kv_move(rows_of(old, 0, NEAR_MID), rows_of(old, 0, NEAR_MID), 9, twin)
    finish(OUT_PARTS, 2)
    b3.wait_recv()
    t3 = kv_move(rows_of(old, NEAR_MID, ROWS), rows_of(old, NEAR_MID, ROWS), 10, twin)
    for copy in (t0, t1, t2, t3):
        copy.wait_recv()
    keep_kv = pltpu.make_async_copy(kv, kv_out, keep_sem.at[3])
    keep_kv.start()
    arrived(OUT_PARTS)
    for copy in sent:
        copy.wait_send()
    for copy in (keep_turned, keep_mask, keep_queries, keep_kv):
        copy.wait()


def front(tokens, norm_gain, lengths, w_query, w_key, w_value, w_out):
    rows_in, rows_out = w_query.shape[0], w_out.shape[0]
    cut = [w.reshape(rows_in, 8, 128) for w in (jnp.concatenate([w_key, w_value], axis=1), w_query)]
    pieces_in = jnp.pad(jnp.concatenate(cut, axis=2).transpose(1, 0, 2), ((0, 0), (0, 32 - rows_in), (0, 0)))
    pieces_out = jnp.pad(w_out.reshape(rows_out, 2, 1280).transpose(1, 0, 2), ((0, 0), (0, 16 - rows_out), (0, 0)))
    vmem = pl.BlockSpec(memory_space=pltpu.VMEM)
    hbm = pl.BlockSpec(memory_space=pl.ANY)
    smem = pl.BlockSpec(memory_space=pltpu.SMEM)
    dma = pltpu.SemaphoreType.DMA

    def held(*shape):
        return pltpu.VMEM(shape, BF16)

    *rest, whole_out = pl.pallas_call(
        functools.partial(front_kernel, rows_in, rows_out),
        out_shape=(
            jax.ShapeDtypeStruct((HEADS, ROWS, 256), BF16),
            jax.ShapeDtypeStruct((6, 4, ROWS, 256), BF16),
            jax.ShapeDtypeStruct((WIDE, ROWS), BF16),
            jax.ShapeDtypeStruct((ROWS, 5 * ROWS), F32),
            jax.ShapeDtypeStruct((SIDE, SIDE, SIDE, 2 * rows_out, WIDE), BF16),
        ),
        in_specs=[vmem, vmem, vmem, vmem, smem],
        out_specs=(hbm,) * 5,
        scratch_shapes=[
            held(SIDE, SIDE, SIDE, 8 * rows_in, 256), held(SIDE, SIDE, SIDE, 8 * rows_in, 256),
            held(8, 32, 256), held(2, 16, 1280), pltpu.VMEM((8 * rows_in, 256), F32), held(1, 1, 1, 2 * rows_out, 1280),
            held(ROWS, WIDE), held(HEADS, ROWS, 256), held(6, 4, ROWS, 256), held(4, ROWS - NEAR_UP, 256),
            held(WIDE, ROWS), pltpu.VMEM((ROWS, 5 * ROWS), F32),
            dma((7,)), dma((7,)), dma((2,)), dma,
            dma((7, 3, 6)), dma((7, 3, 6)), dma((7, 7)), dma((7, 7)), dma((11,)), dma((11,)), dma((4,)),
        ],
        compiler_params=pltpu.CompilerParams(
            collective_id=0, has_side_effects=True, vmem_limit_bytes=62 * 2**20),
        name="front",
    )(pieces_in, pieces_out, tokens, norm_gain.reshape(1, -1), lengths)
    return (*rest, whole_out.reshape(128 * rows_out, WIDE))


def layer_kernel(queries, kv, mask_ref, rewards_ref, turned_ref, tokens_ref, target_ref, weight_ref,
                 own_query, own_key, own_value, own_out, mate_query, mate_key, mate_value, mate_out, *scratch):
    (probs, scores, terms, term_mate, term_next, term_far, term_relay, term_end, x_one, x_two,
     weight, turned, mixed, mixed_turned, mixed_grad, joined,
     give_in, give_out, sum_in, sum_out, twin_in, twin_out, far_in, far_out, near_in, near_out, done_in, done_out,
     read_sem, term_send, term_recv, twin_send, twin_recv,
     far_send, far_recv, near_send, near_recv, mate_send, mate_recv, keep_sem) = scratch
    at = place()
    c, y = at["c"], at["y"]
    twin = sibling(at)
    up, down = beside(at, "y", 1), beside(at, "y", -1)
    x_flip = {**at, "x": at["x"] + 1 - 2 * lax.rem(at["x"], 2)}
    x_turn = {**at, "x": SIDE - 1 - at["x"]}
    z_flip = {**at, "z": at["z"] + 1 - 2 * lax.rem(at["z"], 2)}
    z_turn = {**at, "z": SIDE - 1 - at["z"]}
    sent = []

    def remote(src, dst, send, recv, to):
        copy = pltpu.make_async_remote_copy(src, dst, send, recv, device_id=device(to), device_id_type=MESH)
        copy.start()
        sent.append(copy)
        return copy

    def read(src, dst, n):
        copy = pltpu.make_async_copy(src, dst, read_sem.at[n])
        copy.start()
        return copy

    read_weight = read(weight_ref, weight, 1)
    read_tokens = read(tokens_ref, x_two, 2)
    read_target = read(target_ref, x_one, 3)
    read_turned = read(turned_ref, turned, 0)
    greet([twin, up, down, x_flip, x_turn, z_flip, z_turn])

    def tile(n):
        return kv[pl.ds(c, 5), n].reshape(5 * ROWS, 256)

    def attend(h, carry):
        g = h // 2
        seen = mask_ref[...] > 0.5
        score = dot(queries[h], tile(g), ((1,), (1,))) * 256 ** -0.5
        score = jnp.where(seen, score, masked_score)
        raised = jnp.where(seen, jnp.exp(score - jnp.max(score, axis=1, keepdims=True)), 0.0)
        prob = (raised / jnp.sum(raised, axis=1, keepdims=True)).astype(BF16)
        probs[h] = prob
        out = dot(prob, tile(2 + g))
        mixed[h] = out.astype(BF16)
        rounded = out.astype(BF16).astype(F32).T.astype(BF16)
        mixed_turned[2 * h] = rounded[:128]
        mixed_turned[2 * h + 1] = rounded[128:]
        return carry
    lax.fori_loop(0, HEADS, attend, 0)

    for copy in (read_weight, read_tokens, read_target):
        copy.wait()

    def error(i, carry):
        cols = pl.ds(pl.multiple_of(i * 512, 512), 512)
        update = sum(dot(mixed[h], weight[256 * h:256 * h + 256, cols]) for h in range(HEADS))
        result = x_two[:, cols].astype(F32) + update
        x_two[:, cols] = (rewards_ref[...] * (result - x_one[:, cols].astype(F32))).astype(BF16)
        return carry
    lax.fori_loop(0, WIDE // 512, error, 0)
    delta = x_two

    y_far, y_up, y_down = lax.rem(y + 2, SIDE), up["y"], down["y"]
    height = {0: WIDE // 8, 1: HEADS * 256 // 8}
    swaps, far, near_own, near_sum, flips, turns, keeps = {}, {}, {}, {}, {}, {}, {}

    def pick(k, inside, outside):
        kind, n, start, width = CHUNKS[k]
        if kind:
            return outside.at[n]
        if start == 0 and width == 512:
            return inside.at[n]
        return inside.at[n, :, pl.ds(start, width)] if len(inside.shape) == 3 else inside.at[n, :, :, pl.ds(start, width)]

    def term(k, dst, core):
        kind, n, start, width = CHUNKS[k]

        def body(i, carry):
            j = 2 * i + core
            if kind:
                dst[i] = dot(mixed_turned[j], delta[:, 1280 * n:1280 * n + 1280]).astype(BF16)
            else:
                rows = pl.ds(pl.multiple_of(j * 320, 64), 320)
                dst[i] = dot(turned[rows, :], joined[n, :, start:start + width]).astype(BF16)
            return carry
        lax.fori_loop(0, 4, body, 0)

    def stage_1(k):
        kind, n, start, width = CHUNKS[k]
        give = give_out.at[n] if kind else give_in.at[n % 2, :, :, pl.ds(start, width)]
        if k in (4, 5):
            swaps[k - 2].wait_send()
        term(k, give, 1 - c)
        swaps[k] = pltpu.make_async_remote_copy(
            give, pick(k, twin_in, twin_out), twin_send.at[k], twin_recv.at[k], device_id=device(twin), device_id_type=MESH)
        swaps[k].start()
        term(k, pick(k, sum_in, sum_out), c)

    def stage_2(k):
        rows = height[CHUNKS[k][0]]
        sums, extra = pick(k, sum_in, sum_out), pick(k, twin_in, twin_out)
        fars, nears = pick(k, far_in, far_out), pick(k, near_in, near_out)
        h0, h1 = pl.ds(0, rows // 2), pl.ds(rows // 2, rows // 2)
        swaps[k].wait_recv()

        def add(block):
            def body(r):
                sums[block, r, :] = (sums[block, r, :].astype(F32) + extra[block, r, :].astype(F32)).astype(BF16)
            add_rows(rows, 32, body)
        add(y_far)
        far[k] = (remote(sums.at[y_far, h0], fars.at[0], far_send.at[k, 0], far_recv.at[k, 0], up),
                  remote(sums.at[y_far, h1], fars.at[1], far_send.at[k, 1], far_recv.at[k, 1], down))
        add(y_up)
        add(y_down)
        near_own[k] = (remote(sums.at[y_up, h1], nears.at[0, h1], near_send.at[k, 0], near_recv.at[k, 0], up),
                       remote(sums.at[y_down, h0], nears.at[1, h0], near_send.at[k, 1], near_recv.at[k, 1], down))
        add(y)

    def stage_3(k):
        rows = height[CHUNKS[k][0]]
        half = rows // 2
        sums = pick(k, sum_in, sum_out)
        fars, nears = pick(k, far_in, far_out), pick(k, near_in, near_out)
        h0, h1 = pl.ds(0, half), pl.ds(half, half)
        far[k][0].wait_recv()

        def low(r):
            sums[y_up, r, :] = (sums[y_up, r, :].astype(F32) + fars[0, r, :].astype(F32)).astype(BF16)
        add_rows(half, 32, low)
        one = remote(sums.at[y_up, h0], nears.at[0, h0], near_send.at[k, 2], near_recv.at[k, 2], up)
        far[k][1].wait_recv()

        def high(i, carry):
            r = pl.ds(pl.multiple_of(i * 32, 32), 32)
            s = pl.ds(pl.multiple_of(i * 32 + half, 32), 32)
            sums[y_down, s, :] = (sums[y_down, s, :].astype(F32) + fars[1, r, :].astype(F32)).astype(BF16)
            return carry
        lax.fori_loop(0, half // 32, high, 0)
        near_sum[k] = (one, remote(sums.at[y_down, h1], nears.at[1, h1], near_send.at[k, 3], near_recv.at[k, 3], down))

    def result(k, query, key, value, out):
        kind, n, start, width = CHUNKS[k]
        ref = out if kind else (query, query, key, value)[n]
        begin = 1280 * n if kind else start if n > 1 else 512 * n
        return ref, pl.ds(begin, width)

    def mates(k, level):
        ref, cols = result(k, mate_query, mate_key, mate_value, mate_out)
        return ref.at[level, :, cols]

    def stage_4(k):
        kind = CHUNKS[k][0]
        sums, nears, done = pick(k, sum_in, sum_out), pick(k, near_in, near_out), pick(k, done_in, done_out)
        for copy in near_own[k] + near_sum[k]:
            copy.wait_recv()

        def body(r):
            done[r, :] = (sums[y, r, :].astype(F32) + nears[0, r, :].astype(F32) + nears[1, r, :].astype(F32)).astype(BF16)
        add_rows(height[kind], 32, body)
        flips[k] = (remote(done, mates(k, 0), mate_send.at[k, 0], mate_recv.at[k, 0], x_flip),
                    remote(done, mates(k, 2), mate_send.at[k, 2], mate_recv.at[k, 2], z_flip))
        own, cols = result(k, own_query, own_key, own_value, own_out)
        keeps[k] = pltpu.make_async_copy(done, own.at[:, cols], keep_sem.at[k])
        keeps[k].start()

    def stage_5(k):
        flips[k][0].wait_recv()
        one = remote(mates(k, 0), mates(k, 1), mate_send.at[k, 1], mate_recv.at[k, 1], x_turn)
        flips[k][1].wait_recv()
        turns[k] = (one, remote(mates(k, 2), mates(k, 3), mate_send.at[k, 3], mate_recv.at[k, 3], z_turn))

    stage_1(0)
    stage_1(1)
    stage_2(0)

    def spread(h, carry):
        rows = pl.ds(pl.multiple_of(h * 256, 256), 256)
        mixed_grad[h] = dot(delta[...], weight[rows, :], ((1,), (1,))).astype(BF16)
        return carry
    lax.fori_loop(0, HEADS, spread, 0)
    stage_2(1)

    terms[5 * (1 - c)] = jnp.zeros((4, ROWS, 256), BF16)

    def back(g):
        for r in range(2):
            h = 2 * g + r
            grad = mixed_grad[h]
            row_dots = jnp.sum(grad.astype(F32) * mixed[h].astype(F32), axis=1, keepdims=True)
            prob_grads = dot(grad, tile(2 + g), ((1,), (1,)))
            score = (probs[h].astype(F32) * (prob_grads - row_dots) * 256 ** -0.5).astype(BF16)
            scores[r] = score
            joined[g, :, 256 * r:256 * r + 256] = dot(score, tile(g)).astype(BF16)
        key_terms = dot(scores[0], queries[2 * g], ((0,), (0,))) + dot(scores[1], queries[2 * g + 1], ((0,), (0,)))
        terms[pl.ds(c, 5), g] = key_terms.astype(BF16).reshape(5, ROWS, 256)
        value_terms = (dot(probs[2 * g], mixed_grad[2 * g], ((0,), (0,)))
                       + dot(probs[2 * g + 1], mixed_grad[2 * g + 1], ((0,), (0,))))
        terms[pl.ds(c, 5), 2 + g] = value_terms.astype(BF16).reshape(5, ROWS, 256)

    back(0)
    stage_3(0)
    back(1)
    stage_3(1)

    def move(src, dst, n, to):
        return remote(src, dst, term_send.at[n], term_recv.at[n], to)

    to_mate = [move(terms.at[2 * n + 1 - c], term_mate.at[n], n, twin) for n in range(3)]
    stage_4(0)
    read_turned.wait()
    stage_1(2)

    def fold(n):
        to_mate[n].wait_recv()
        for q in range(4):
            def body(r):
                terms[2 * n + c, q, r, :] = (
                    terms[2 * n + c, q, r, :].astype(F32) + term_mate[n, q, r, :].astype(F32)).astype(BF16)
            add_rows(ROWS, 64, body)

    def part(ref, low, high, start=0):
        return ref.at[:, pl.ds(low - start, high - low), :]

    fold(0)
    s2 = terms.at[c]
    e0 = move(part(s2, 0, FAR_DOWN), term_far, 3, down)
    f0 = move(part(s2, FAR_DOWN, FAR_MID), part(term_relay, FAR_DOWN, FAR_MID, FAR_DOWN), 4, up)
    f1 = move(part(s2, FAR_MID, ROWS), part(term_relay, FAR_MID, ROWS, FAR_DOWN), 5, up)
    fold(1)
    s1 = terms.at[2 + c]
    e1 = move(part(s1, FAR_DOWN, ROWS), part(term_next, FAR_DOWN, ROWS), 6, down)
    fold(2)
    stage_1(3)
    stage_2(2)
    e0.wait_recv()
    for q in range(4):
        def join(r):
            terms[2 + c, q, r, :] = (terms[2 + c, q, r, :].astype(F32) + term_far[q, r, :].astype(F32)).astype(BF16)
        add_rows(FAR_DOWN, 16, join)
    e2 = move(part(s1, 0, FAR_DOWN), part(term_next, 0, FAR_DOWN), 7, down)
    f0.wait_recv()
    f2 = move(part(term_relay, FAR_DOWN, FAR_MID, FAR_DOWN), part(term_end, FAR_DOWN, FAR_MID, FAR_DOWN), 8, up)
    f1.wait_recv()
    f3 = move(part(term_relay, FAR_MID, ROWS, FAR_DOWN), part(term_end, FAR_MID, ROWS, FAR_DOWN), 9, up)
    stage_4(1)
    stage_2(3)
    stage_5(0)
    stage_3(2)
    for copy in (e1, e2, f2, f3):
        copy.wait_recv()
    for q in range(4):
        n, g = 2 + q // 2, q % 2
        joined[n, 0:FAR_DOWN, 256 * g:256 * g + 256] = (
            terms[4 + c, q, 0:FAR_DOWN, :].astype(F32) + term_next[q, 0:FAR_DOWN, :].astype(F32)).astype(BF16)
        joined[n, FAR_DOWN:ROWS, 256 * g:256 * g + 256] = (
            terms[4 + c, q, FAR_DOWN:ROWS, :].astype(F32) + term_next[q, FAR_DOWN:ROWS, :].astype(F32)
            + term_end[q].astype(F32)).astype(BF16)
    order = ((1, 4), (1, 5), (2, 4), (1, 6), (3, 3), (2, 5), (4, 2), (5, 1), (2, 6), (3, 4), (4, 3), (5, 2), (3, 5),
             (3, 6), (4, 4), (5, 3), (4, 5), (5, 4), (4, 6), (5, 5), (5, 6))
    for stage, k in order:
        (stage_1, stage_2, stage_3, stage_4, stage_5)[stage - 1](k)
    for k in range(len(CHUNKS)):
        turns[k][0].wait_recv()
        turns[k][1].wait_recv()
        keeps[k].wait()
    for k in (0, 1, 4, 5, 6):
        swaps[k].wait_send()
    for copy in sent:
        copy.wait_send()


def layer_grads(queries, kv, mask, rewards, turned, tokens, target, weight):
    vmem = pl.BlockSpec(memory_space=pltpu.VMEM)
    hbm = pl.BlockSpec(memory_space=pl.ANY)
    dma = pltpu.SemaphoreType.DMA
    ri, ro, n = WIDE // 8, HEADS * 256 // 8, len(CHUNKS)
    results = ((ri, 1024), (ri, 512), (ri, 512), (ro, WIDE))

    def held(*shape):
        return pltpu.VMEM(shape, BF16)

    return pl.pallas_call(
        layer_kernel,
        out_shape=tuple(jax.ShapeDtypeStruct(shape, BF16) for shape in results)
        + tuple(jax.ShapeDtypeStruct((4, *shape), BF16) for shape in results),
        in_specs=[vmem, vmem, vmem, vmem, hbm, hbm, hbm, hbm],
        out_specs=(hbm,) * 8,
        scratch_shapes=[
            held(HEADS, ROWS, 5 * ROWS), held(2, ROWS, 5 * ROWS),
            held(6, 4, ROWS, 256), held(3, 4, ROWS, 256), held(4, ROWS, 256), held(4, FAR_DOWN, 256),
            held(4, ROWS - FAR_DOWN, 256), held(4, ROWS - FAR_DOWN, 256),
            held(ROWS, WIDE), held(ROWS, WIDE), held(HEADS * 256, WIDE), held(WIDE, ROWS),
            held(HEADS, ROWS, 256), held(8, 128, ROWS), held(HEADS, ROWS, 256), held(4, ROWS, 512),
            held(2, 4, ri, 512), held(2, 4, ro, 1280),
            held(4, 4, ri, 512), held(2, 4, ro, 1280), held(4, 4, ri, 512), held(2, 4, ro, 1280),
            held(4, 2, ri // 2, 512), held(2, 2, ro // 2, 1280), held(4, 2, ri, 512), held(2, 2, ro, 1280),
            held(4, ri, 512), held(2, ro, 1280),
            dma((4,)), dma((10,)), dma((10,)), dma((n,)), dma((n,)),
            dma((n, 2)), dma((n, 2)), dma((n, 4)), dma((n, 4)), dma((n, 4)), dma((n, 4)), dma((n,)),
        ],
        compiler_params=pltpu.CompilerParams(
            collective_id=1, has_side_effects=True, vmem_limit_bytes=62 * 2**20),
        name="layer_grads",
    )(queries, kv, mask, rewards, turned, tokens, target, weight)


def per_device(
    tokens, target, rewards, doc_lengths, norm_gain, w_query, w_key, w_value, w_out, gossip_bit
):
    token_rows, target_rows = tokens[0, 0], target[0, 0]
    queries, kv, turned, mask, out_whole = front(
        token_rows, norm_gain, doc_lengths[0], w_query, w_key, w_value, w_out
    )
    results = layer_grads(
        queries, kv, mask, rewards.reshape(ROWS, 1), turned, token_rows, target_rows, out_whole
    )
    own_bit = gossip_bit[0]

    def mean(own, mates):
        partner = mates[0]
        for level in range(1, 4):
            partner = jnp.where(own_bit == level, mates[level], partner)
        return ((own.astype(F32) + partner.astype(F32)) * 0.5)[None]

    return tuple(mean(own, mates) for own, mates in zip(results[:4], results[4:]))


def solution(mesh):
    placed = (
        P("dp", None, "ctx", None),
        P("dp", None, "ctx", None),
        P("dp", None, "ctx"),
        P("dp", None, None),
        P(),
        P(("dp", "ctx"), None),
        P(("dp", "ctx"), None),
        P(("dp", "ctx"), None),
        P(("dp", "ctx"), None),
        P("dp"),
    )
    return jax.shard_map(
        per_device,
        mesh=mesh,
        in_specs=placed,
        out_specs=(
            P("dp", "ctx", None),
            P("dp", "ctx", None),
            P("dp", "ctx", None),
            P("dp", "ctx", None),
        ),
        check_vma=False,
    )
```

time: 214 us -> 203 us (0.949)
  Pallas kernels: 196 us -> 188 us
    pallas_call x2, Pallas kernels: 196 us -> 188 us  [the longest x1 120 us: layer_grads(): pl.pallas_call(layer_kernel, out_shape=tuple((jax.ShapeDtypeStruct(shape,...]
    broadcast_in_dim x1 -> x3, other arithmetic: 1.49 us -> 6.69 us  [mean(): return ((own.astype(F32) + partner.astype(F32)) * 0.5)[None]]
    mul x1 -> x0, other arithmetic: 4.14 us -> none  [per_device(): (grad_inputs.astype(jnp.float32) + partner_inputs.astype(jnp.float32)) * 0.5]
    unnamed x25 -> x16, local copies, waits for them, and re-layouts: 4.74 us -> 1.68 us
    broadcast_in_dim x2 -> x0, local copies, waits for them, and re-layouts: 2.37 us -> none  [the longest x1 1.21 us: per_device(): mean_inputs[None, :, :query_width]]
where the time goes in v3:
time: 203 us
  Pallas kernels  188 us (93%)
  other arithmetic  7.47 us (4%)
  local copies, waits for them, and re-layouts  5.91 us (3%)
    pallas_call x1, Pallas kernels, layer_grads(): pl.pallas_call(layer_kernel, out_shape=tuple((jax.ShapeDtypeStruct(shape,...  120 us
    pallas_call x1, Pallas kernels, front(): pl.pallas_call(functools.partial(front_kernel, rows_in, rows_out), out_sh...  68.2 us
    broadcast_in_dim x3, other arithmetic, mean(): return ((own.astype(F32) + partner.astype(F32)) * 0.5)[None]  6.69 us

profile of v3, /device:TPU:0, one launch (start us, length us, event | category | flops | bytes accessed | tf_op | source)
XLA Modules:
  0.0 203.0 jit_solution(3603625956921389137)
XLA Ops:
  0.6 0.8 pad_maximum_fusion
  1.4 0.0 copy-start.6
  1.5 0.8 copy.18
  2.3 0.7 pad.8.in_ref
  3.0 1.4 pad.9.out_ref
  4.4 1.3 reshape.67.gain_ref
  5.7 68.2 %front.1 = (bf16[4,256,256]{2,1,0:T(8,128)(2,1)}, bf16[6,4,256,256]{3,2,1,0:T(8,128)(2,1)}, bf16[2560,256]{1,0:T(8,128)(2,1)}, f32[256,1280]{1,0:T(8,128)}, bf16[4,4,4,16,2560]{4,3,2,1,0:T(8,128)(2,1)}) custom-call(bf16[8,32,256]{2,1,0:T(8,128)(2,1)} %pad.8.in_ref, bf16[2,16,1280]{2,1,0:T(8,128)(2,1)} %pad.9.out_ref, bf16[256,2560]{1,0:T(8,128)(2,1)} %bitcast.40, ...), custom_call_target="tpu_custom_call" | custom-call | tf_op jit(solution)/shard_map/front/pallas_call | solution.py:328
  73.9 0.0 copy-done.6
  73.9 0.8 copy.16.rewards_ref
  74.7 120.0 %layer_grads.1 = (bf16[320,1024]{1,0:T(8,128)(2,1)}, bf16[320,512]{1,0:T(8,128)(2,1)}, bf16[320,512]{1,0:T(8,128)(2,1)}, bf16[128,2560]{1,0:T(8,128)(2,1)}, bf16...) custom-call(bf16[4,256,256]{2,1,0:T(8,128)(2,1)} %get-tuple-element., ...), custom_call_target="tpu_custom_call" | custom-call | tf_op jit(solution)/shard_map/layer_grads/pallas_call | solution.py:638
  195.4 0.0 copy-start.1
  195.4 0.0 copy-start.2
  195.5 0.0 copy-start.4
  195.5 0.0 copy-start.5
  195.5 3.5 %fusion.1 = f32[1,128,2560]{2,1,0:T(8,128)} fusion(bf16[128,2560]{1,0:T(8,128)(2,1)} %get-tuple-element.28, bf16[4,128,2560]{2,1,0:T(8,128)(2,1)} %get-tuple-element.29, pred[]{:T(512)} %bitcast.10, pred[]{:T(512)} %bitcast.9, pred[]{:T(512)} %bitcast.8), kind=kLoop, calls=%fused_computation.2 | loop fusion | flops 2293760 | bytes 4587523 | tf_op jit(solution)/shard_map/broadcast_in_dim | solution.py:679
  199.0 0.0 copy-done.1
  199.0 0.0 copy-done.2
  199.0 0.0 copy-done.4
  199.0 0.0 copy-done.5
  199.0 0.0 copy-start
  199.0 0.0 copy-start.3
  199.0 1.5 fusion.5
  200.5 0.7 copy-done
  201.2 0.1 copy-done.3
  201.4 1.7 fusion.3
  (6 shorter events, 0.1 us)
Async XLA Ops:
  1.4 72.5 %copy-start.6 = (f32[1,1,256]{2,1,0:T(1,128)S(1)}, f32[1,1,256]{2,1,0:T(1,128)}, u32[]{:S(2)}) copy-start(f32[1,1,256]{2,1,0:T(1,128)} %param.12) | copy-start | bytes 3076
  195.4 3.6 %copy-start.1 = (bf16[4,320,512]{2,1,0:T(8,128)(2,1)S(1)}, bf16[4,320,512]{2,1,0:T(8,128)(2,1)}, u32[]{:S(2)}) copy-start(bf16[4,320,512]{2,1,0:T(8,128)(2,1)} %get-tuple-element.25) | copy-start | bytes 3932164
  195.4 3.6 %copy-start.2 = (bf16[4,320,512]{2,1,0:T(8,128)(2,1)S(1)}, bf16[4,320,512]{2,1,0:T(8,128)(2,1)}, u32[]{:S(2)}) copy-start(bf16[4,320,512]{2,1,0:T(8,128)(2,1)} %get-tuple-element.27) | copy-start | bytes 3932164
  195.5 3.5 %copy-start.4 = (bf16[320,512]{1,0:T(8,128)(2,1)S(1)}, bf16[320,512]{1,0:T(8,128)(2,1)}, u32[]{:S(2)}) copy-start(bf16[320,512]{1,0:T(8,128)(2,1)} %get-tuple-element.24) | copy-start | bytes 983044
  195.5 3.5 %copy-start.5 = (bf16[320,512]{1,0:T(8,128)(2,1)S(1)}, bf16[320,512]{1,0:T(8,128)(2,1)}, u32[]{:S(2)}) copy-start(bf16[320,512]{1,0:T(8,128)(2,1)} %get-tuple-element.26) | copy-start | bytes 983044
  199.0 2.2 %copy-start = (bf16[4,320,1024]{2,1,0:T(8,128)(2,1)S(1)}, bf16[4,320,1024]{2,1,0:T(8,128)(2,1)}, u32[]{:S(2)}) copy-start(bf16[4,320,1024]{2,1,0:T(8,128)(2,1)} %get-tuple-element.23) | copy-start | bytes 7864324
  199.0 2.3 %copy-start.3 = (bf16[320,1024]{1,0:T(8,128)(2,1)S(1)}, bf16[320,1024]{1,0:T(8,128)(2,1)}, u32[]{:S(2)}) copy-start(bf16[320,1024]{1,0:T(8,128)(2,1)} %get-tuple-element.22) | copy-start | bytes 1966084

commit v4 on v3

--- a/solution.py
+++ b/solution.py
@@ -46,7 +46,8 @@
 NEAR_MID = 160
 FAR_DOWN = 80
 FAR_MID = 160
-CHUNKS = ((1, 0, 0, 1280), (1, 1, 0, 1280), (0, 0, 0, 512), (0, 1, 0, 512), (0, 2, 0, 512), (0, 3, 0, 256), (0, 3, 256, 256))
+CHUNKS = ((1, 0, 0, 1280), (1, 1, 0, 1280), (0, 0, 0, 512), (0, 1, 0, 512), (0, 2, 0, 512), (0, 3, 0, 256), (0, 3, 256, 128),
+          (0, 3, 384, 128))
 
 
 def dot(a, b, contract=((1,), (0,))):
@@ -61,17 +62,18 @@
 
 
 PARTS = (
-    ("kv", 0, 64, "xyz"), ("kv", 64, 48, "yzx"), ("kv", 112, 48, "zxy"),
-    ("query", 0, 80, "yxz"), ("query", 80, 80, "yzx"),
-    ("out", 0, 640, "yxz"), ("out", 640, 640, "yzx"),
+    ("kv", 0, 80, "xz"), ("kv", 80, 80, "zx"),
+    ("query", 0, 80, "xz"), ("query", 80, 80, "zx"),
+    ("out", 0, 32, "xz"), ("out", 32, 32, "zx"),
 )
-KV_PARTS, QUERY_PARTS, OUT_PARTS = range(3), range(3, 5), range(5, 7)
-
-
-def front_kernel(rows_in, rows_out, in_ref, out_ref, tokens_ref, gain_ref, lengths_ref,
+KV_PARTS, QUERY_PARTS, OUT_PARTS = (0, 1), (2, 3), (4, 5)
+
+
+def front_kernel(rows_in, rows_out, kv_ref, query_ref, out_ref, tokens_ref, gain_ref, lengths_ref,
                  queries_out, kv_out, turned_out, mask_out, w_out, *scratch):
-    (w_kv, w_query, slots_in, slots_out, wide, block_out, x_ref, queries, kv, kv_relay, turned, mask,
-     swap_send, swap_recv, pair_sem, local_sem, ring_send, ring_recv, twin_send, twin_recv, kv_send, kv_recv, keep_sem) = scratch
+    (w_kv, w_query, slots_kv, slots_query, slots_out, wide, block_out, x_ref, queries, kv, kv_relay, turned, mask,
+     swap_send, swap_recv, local_sem, line_send, line_recv, ring_send, ring_recv, twin_send, twin_recv,
+     kv_send, kv_recv, keep_sem) = scratch
     at = place()
     c = at["c"]
     ctx = at["y"] * 2 + c
@@ -79,7 +81,7 @@
     up, down = beside(at, "y", 1), beside(at, "y", -1)
     others = [lax.rem(ctx + k, 8) for k in range(1, 8)]
     group = [{**at, "y": lax.div(j, 2), "c": lax.rem(j, 2)} for j in others]
-    greet([beside(at, "x", 1), beside(at, "x", -1), beside(at, "z", 1), beside(at, "z", -1)] + group)
+    greet([beside(at, a, step) for a in "xz" for step in (1, -1)] + group)
     sent = []
 
     def remote(src, dst, send, recv, to):
@@ -88,152 +90,143 @@
         sent.append(copy)
         return copy
 
-    copies = [remote(in_ref.at[others[k]], slots_in.at[ctx], swap_send.at[k], swap_recv.at[k], group[k]) for k in range(7)]
-    pair = remote(out_ref.at[1 - c], slots_out.at[c], pair_sem.at[0], pair_sem.at[1], twin)
-    slots_in[ctx] = in_ref[ctx]
-    slots_out[c] = out_ref[c]
-
-    def norm(r):
+    def spread(n, ref, slots):
+        return [remote(ref.at[group[k]["c"]], slots.at[ctx], swap_send.at[n, k], swap_recv.at[n, k], group[k]) for k in range(7)]
+
+    def norm(i, carry):
+        r = pl.ds(pl.multiple_of(i * 32, 32), 32)
         values = tokens_ref[r, :].astype(F32)
         power = jnp.mean(values * values, axis=1, keepdims=True)
         x_ref[r, :] = (values * lax.rsqrt(power + epsilon) * gain_ref[...]).astype(BF16)
-
-    lane = pl.ds(pl.multiple_of(c * 128, 128), 128)
-    for k, copy in enumerate(copies):
-        copy.wait_recv()
-    for j in range(8):
-        wide[rows_in * j:rows_in * (j + 1)] = slots_in[j].astype(F32)[:rows_in]
-    w_kv[at["y"], at["z"], at["x"], :, lane] = wide[:, :128].astype(BF16)
-    w_query[at["y"], at["z"], at["x"], :, lane] = wide[:, 128:].astype(BF16)
-
-    one = {a: pl.ds(at[a], 1) for a in "xyz"}
+        return carry
+
+    def merged(slots, rows, copies):
+        for copy in copies:
+            copy.wait_recv()
+        width = slots.shape[2]
+        for j in range(8):
+            wide[rows * j:rows * (j + 1), :width] = slots[j].astype(F32)[:rows]
+        return wide[:8 * rows, :width].astype(BF16)
+
+    half = pl.ds(pl.multiple_of(c * 512, 128), 512)
+    spread_kv = spread(0, kv_ref, slots_kv)
+    slots_kv[ctx] = kv_ref[c]
+    slots_query[ctx] = query_ref[c]
+    slots_out[ctx] = out_ref[c]
+    w_kv[at["z"], at["x"], :, half] = merged(slots_kv, rows_in, spread_kv)
+
+    one = {a: pl.ds(at[a], 1) for a in "xz"}
     whole = pl.ds(0, SIDE)
 
-    def view(part, where):
+    def view(part, where, piece=None):
         name, start, size, _ = PARTS[part]
+        cut = size // 32 * 16 if size % 32 == 0 else 48
+        rows = pl.ds(*((start, size) if piece is None else ((start, cut), (start + cut, size - cut))[piece]))
         if name == "out":
-            cols = pl.ds(pl.multiple_of(c * 1280 + start, 128), size)
-            return w_out.at[where["z"], where["x"], where["y"], :, cols]
-        ref = w_kv if name == "kv" else w_query
-        return ref.at[where["y"], where["z"], where["x"], pl.ds(start, size), lane]
-
-    first, last, twins = {}, {}, {}
-
-    def known(part, phase, shift, half):
+            return w_out.at[where["z"], where["x"], rows, pl.ds(pl.multiple_of(c * 1280, 128), 1280)]
+        return (w_kv if name == "kv" else w_query).at[where["z"], where["x"], rows, half]
+
+    lines, first, last, twins = {}, {}, {}, {}
+
+    def beside_line(part, step):
+        axis = PARTS[part][3][0]
+        return {**one, axis: pl.ds(beside(at, axis, step)[axis], 1)}
+
+    def hop(part, n, where, step, piece=None):
+        lines.setdefault(part, []).append(
+            remote(view(part, where, piece), view(part, where, piece), line_send.at[part, n], line_recv.at[part, n],
+                   beside(at, PARTS[part][3][0], step)))
+
+    def line(part):
+        hop(part, 0, one, 1)
+        hop(part, 1, one, -1)
+
+    def pass_on(parts):
+        for part in parts:
+            lines[part][0].wait_recv()
+            hop(part, 2, beside_line(part, -1), 1, 0)
+            lines[part][1].wait_recv()
+            hop(part, 3, beside_line(part, 1), -1, 1)
+
+    def lined(parts):
+        for part in parts:
+            for copy in lines[part][2:]:
+                copy.wait_recv()
+
+    def known(part, shift, which):
         order = PARTS[part][3]
-        where = dict(one)
-        for a in order[:phase]:
-            where[a] = whole
-        if phase:
-            where[order[0]] = pl.ds(2 * half, 2)
-        if half is None and phase:
-            where[order[0]] = whole
-        axis = order[phase]
-        where[axis] = pl.ds(lax.rem(at[axis] + shift + SIDE, SIDE), 1)
-        return where
-
-    def ring(part, phase, slot, where, step):
-        return remote(view(part, where), view(part, where), ring_send.at[part, phase, slot],
-                      ring_recv.at[part, phase, slot], beside(at, PARTS[part][3][phase], step))
+        axis = order[1]
+        return {order[0]: pl.ds(2 * which, 2), axis: pl.ds(lax.rem(at[axis] + shift + SIDE, SIDE), 1)}
+
+    def ring(part, slot, where, step):
+        return remote(view(part, where), view(part, where), ring_send.at[part, slot], ring_recv.at[part, slot],
+                      beside(at, PARTS[part][3][1], step))
 
     def to_twin(part, where, slot):
         twins.setdefault(part, []).append(
             remote(view(part, where), view(part, where), twin_send.at[part, slot], twin_recv.at[part, slot], twin))
 
-    def begin(part, phase):
-        if phase:
-            first[part] = (ring(part, phase, 0, known(part, phase, 0, 0), 1), ring(part, phase, 1, known(part, phase, 0, 1), -1))
-            last[part] = [ring(part, phase, 2, known(part, phase, 0, 1), 1), ring(part, phase, 3, known(part, phase, 0, 0), -1)]
-        else:
-            first[part] = (ring(part, 0, 0, known(part, 0, 0, None), 1),)
-            last[part] = [ring(part, 0, 1, known(part, 0, 0, None), -1)]
-
-    def share(part):
-        where = dict(one)
-        for a in PARTS[part][3][:2]:
-            where[a] = whole
-        to_twin(part, where, 0)
-
-    def relay(part, phase):
-        first[part][0].wait_recv()
-        if not phase:
-            last[part].append(ring(part, 0, 4, known(part, 0, -1, None), 1))
-            return
-        last[part].append(ring(part, phase, 4, known(part, phase, -1, 0), 1))
-        first[part][1].wait_recv()
-        last[part].append(ring(part, phase, 5, known(part, phase, 1, 1), -1))
-        if phase == 2:
-            to_twin(part, known(part, phase, -1, 0), 1)
-            to_twin(part, known(part, phase, 1, 1), 2)
-
-    def finish(parts, phase):
+    def begin(parts):
+        for part in parts:
+            first[part] = (ring(part, 0, known(part, 0, 0), 1), ring(part, 1, known(part, 0, 1), -1))
+        for part in parts:
+            last[part] = [ring(part, 2, known(part, 0, 1), 1), ring(part, 3, known(part, 0, 0), -1)]
+        for part in parts:
+            to_twin(part, {**one, PARTS[part][3][0]: whole}, 0)
+
+    def relay(parts):
+        for part in parts:
+            first[part][0].wait_recv()
+            last[part].append(ring(part, 4, known(part, -1, 0), 1))
+        for part in parts:
+            first[part][1].wait_recv()
+            last[part].append(ring(part, 5, known(part, 1, 1), -1))
+        for part in parts:
+            to_twin(part, known(part, -1, 0), 1)
+            to_twin(part, known(part, 1, 1), 2)
+
+    def finish(parts):
         for n in range(4):
             for part in parts:
-                if n < len(last[part]):
-                    last[part][n].wait_recv()
-                    if phase == 2:
-                        shift, half = ((-1, 1), (1, 0), (-2, 0), (2, 1))[n]
-                        to_twin(part, known(part, phase, shift, half), 3 + n)
+                last[part][n].wait_recv()
+                shift, which = ((-1, 1), (1, 0), (-2, 0), (2, 1))[n]
+                to_twin(part, known(part, shift, which), 3 + n)
 
     def arrived(parts):
         for part in parts:
             for copy in twins[part]:
                 copy.wait_recv()
 
-    later = list(QUERY_PARTS) + list(OUT_PARTS)
     for part in KV_PARTS:
-        begin(part, 0)
+        line(part)
+    spread_query = spread(1, query_ref, slots_query)
+    spread_out = spread(2, out_ref, slots_out)
+    lax.fori_loop(0, 2, norm, 0)
+    pass_on(KV_PARTS)
+    lax.fori_loop(2, 4, norm, 0)
+    lined(KV_PARTS)
+    begin(KV_PARTS)
+    w_query[at["z"], at["x"], :, half] = merged(slots_query, rows_in, spread_query)
     for part in QUERY_PARTS:
-        begin(part, 0)
-    pair.wait_recv()
-    block_out[0, 0, 0] = jnp.concatenate(
-        [slots_out[0].astype(F32)[:rows_out], slots_out[1].astype(F32)[:rows_out]], axis=0).astype(BF16)
-    own_cols = pl.ds(pl.multiple_of(c * 1280, 128), 1280)
-    store = pltpu.make_async_copy(block_out, w_out.at[one["z"], one["x"], one["y"], :, own_cols], local_sem)
+        line(part)
+    block_out[0, 0] = merged(slots_out, rows_out, spread_out)
+    store = pltpu.make_async_copy(
+        block_out, w_out.at[one["z"], one["x"], :, pl.ds(pl.multiple_of(c * 1280, 128), 1280)], local_sem)
     store.start()
-    for part in KV_PARTS:
-        relay(part, 0)
+    relay(KV_PARTS)
     store.wait()
     for part in OUT_PARTS:
-        begin(part, 0)
-    finish(KV_PARTS, 0)
-    for part in KV_PARTS:
-        begin(part, 1)
-    add_rows(ROWS // 2, 32, norm)
-    for part in later:
-        relay(part, 0)
-    for part in KV_PARTS:
-        relay(part, 1)
-    finish(later, 0)
-    for part in later:
-        begin(part, 1)
-    finish(KV_PARTS, 1)
-    for part in KV_PARTS:
-        begin(part, 2)
-        share(part)
-
-    def norm_more(i, carry):
-        norm(pl.ds(pl.multiple_of(i * 32, 32), 32))
-        return carry
-    lax.fori_loop(4, ROWS // 32, norm_more, 0)
-    for part in later:
-        relay(part, 1)
-    finish(later, 1)
-    for part in KV_PARTS:
-        relay(part, 2)
-    for part in QUERY_PARTS:
-        begin(part, 2)
-    finish(KV_PARTS, 2)
-    for part in QUERY_PARTS:
-        share(part)
+        line(part)
+    pass_on(QUERY_PARTS)
+    lax.fori_loop(4, ROWS // 32, norm, 0)
+    finish(KV_PARTS)
+    lined(QUERY_PARTS)
+    begin(QUERY_PARTS)
     arrived(KV_PARTS)
 
     here, before, old = 4 + c, 2 + c, c
-
-    def project_kv(n, carry):
-        kv[here, n] = dot(x_ref[...], w_kv[n].reshape(128 * rows_in, 256)).astype(BF16)
-        return carry
-    lax.fori_loop(0, 4, project_kv, 0)
+    for n in range(4):
+        kv[here, n] = dot(x_ref[...], w_kv[:, :, :, 256 * n:256 * n + 256].reshape(128 * rows_in, 256)).astype(BF16)
 
     def rows_of(slot, low, high):
         return kv.at[slot, :, pl.ds(low, high - low), :]
@@ -247,10 +240,10 @@
     a1 = kv_move(rows_of(here, NEAR_UP, ROWS), rows_of(before, NEAR_UP, ROWS), 2, up)
     b1 = kv_move(rows_of(here, NEAR_MID, ROWS), kv_relay.at[:, pl.ds(mid, ROWS - NEAR_MID), :], 3, down)
     t0 = kv_move(kv.at[here], kv.at[here], 4, twin)
-    for part in QUERY_PARTS:
-        relay(part, 2)
-    for part in OUT_PARTS:
-        begin(part, 2)
+    pass_on(OUT_PARTS)
+    relay(QUERY_PARTS)
+    lined(OUT_PARTS)
+    begin(OUT_PARTS)
 
     def turn(i, carry):
         cols = pl.ds(pl.multiple_of(i * 128, 128), 128)
@@ -261,16 +254,13 @@
     lax.fori_loop(0, 10, turn, 0)
     b0.wait_recv()
     b2 = kv_move(kv_relay.at[:, pl.ds(0, mid), :], rows_of(old, NEAR_UP, NEAR_MID), 6, down)
-    finish(QUERY_PARTS, 2)
-    for part in OUT_PARTS:
-        share(part)
+    finish(QUERY_PARTS)
+    b1.wait_recv()
+    b3 = kv_move(kv_relay.at[:, pl.ds(mid, ROWS - NEAR_MID), :], rows_of(old, NEAR_MID, ROWS), 7, down)
+    relay(OUT_PARTS)
     lax.fori_loop(10, WIDE // 128, turn, 0)
     keep_turned = pltpu.make_async_copy(turned, turned_out, keep_sem.at[0])
     keep_turned.start()
-    b1.wait_recv()
-    b3 = kv_move(kv_relay.at[:, pl.ds(mid, ROWS - NEAR_MID), :], rows_of(old, NEAR_MID, ROWS), 7, down)
-    for part in OUT_PARTS:
-        relay(part, 2)
 
     query_pos = ctx * ROWS + lax.broadcasted_iota(jnp.int32, (ROWS, 1), 0)
     key_pos = (ctx - 4) * ROWS + lax.broadcasted_iota(jnp.int32, (1, 5 * ROWS), 1)
@@ -285,22 +275,19 @@
     keep_mask = pltpu.make_async_copy(mask, mask_out, keep_sem.at[1])
     keep_mask.start()
 
+    a1.wait_recv()
+    t1 = kv_move(kv.at[before], kv.at[before], 8, twin)
     arrived(QUERY_PARTS)
-
-    def project_query(n, carry):
-        queries[n] = dot(x_ref[...], w_query[n].reshape(128 * rows_in, 256)).astype(BF16)
-        return carry
-    lax.fori_loop(0, 4, project_query, 0)
+    for n in range(4):
+        queries[n] = dot(x_ref[...], w_query[:, :, :, 256 * n:256 * n + 256].reshape(128 * rows_in, 256)).astype(BF16)
     keep_queries = pltpu.make_async_copy(queries, queries_out, keep_sem.at[2])
     keep_queries.start()
-    a1.wait_recv()
-    t1 = kv_move(kv.at[before], kv.at[before], 8, twin)
     a2.wait_recv()
     b2.wait_recv()
     t2 = kv_move(rows_of(old, 0, NEAR_MID), rows_of(old, 0, NEAR_MID), 9, twin)
-    finish(OUT_PARTS, 2)
     b3.wait_recv()
     t3 = kv_move(rows_of(old, NEAR_MID, ROWS), rows_of(old, NEAR_MID, ROWS), 10, twin)
+    finish(OUT_PARTS)
     for copy in (t0, t1, t2, t3):
         copy.wait_recv()
     keep_kv = pltpu.make_async_copy(kv, kv_out, keep_sem.at[3])
@@ -314,9 +301,10 @@
 
 def front(tokens, norm_gain, lengths, w_query, w_key, w_value, w_out):
     rows_in, rows_out = w_query.shape[0], w_out.shape[0]
-    cut = [w.reshape(rows_in, 8, 128) for w in (jnp.concatenate([w_key, w_value], axis=1), w_query)]
-    pieces_in = jnp.pad(jnp.concatenate(cut, axis=2).transpose(1, 0, 2), ((0, 0), (0, 32 - rows_in), (0, 0)))
-    pieces_out = jnp.pad(w_out.reshape(rows_out, 2, 1280).transpose(1, 0, 2), ((0, 0), (0, 16 - rows_out), (0, 0)))
+    pad_in, pad_out = (0, 32 - rows_in), (0, 16 - rows_out)
+    kv_pieces = jnp.pad(jnp.stack([w_key, w_value]), ((0, 0), pad_in, (0, 0)))
+    query_pieces = jnp.pad(jnp.stack([w_query[:, :512], w_query[:, 512:]]), ((0, 0), pad_in, (0, 0)))
+    out_pieces = jnp.pad(jnp.stack([w_out[:, :1280], w_out[:, 1280:]]), ((0, 0), pad_out, (0, 0)))
     vmem = pl.BlockSpec(memory_space=pltpu.VMEM)
     hbm = pl.BlockSpec(memory_space=pl.ANY)
     smem = pl.BlockSpec(memory_space=pltpu.SMEM)
@@ -332,22 +320,23 @@
             jax.ShapeDtypeStruct((6, 4, ROWS, 256), BF16),
             jax.ShapeDtypeStruct((WIDE, ROWS), BF16),
             jax.ShapeDtypeStruct((ROWS, 5 * ROWS), F32),
-            jax.ShapeDtypeStruct((SIDE, SIDE, SIDE, 2 * rows_out, WIDE), BF16),
+            jax.ShapeDtypeStruct((SIDE, SIDE, 8 * rows_out, WIDE), BF16),
         ),
-        in_specs=[vmem, vmem, vmem, vmem, smem],
+        in_specs=[vmem, vmem, vmem, vmem, vmem, smem],
         out_specs=(hbm,) * 5,
         scratch_shapes=[
-            held(SIDE, SIDE, SIDE, 8 * rows_in, 256), held(SIDE, SIDE, SIDE, 8 * rows_in, 256),
-            held(8, 32, 256), held(2, 16, 1280), pltpu.VMEM((8 * rows_in, 256), F32), held(1, 1, 1, 2 * rows_out, 1280),
+            held(SIDE, SIDE, 8 * rows_in, 1024), held(SIDE, SIDE, 8 * rows_in, 1024),
+            held(8, 32, 512), held(8, 32, 512), held(8, 16, 1280), pltpu.VMEM((8 * rows_in, 1280), F32),
+            held(1, 1, 8 * rows_out, 1280),
             held(ROWS, WIDE), held(HEADS, ROWS, 256), held(6, 4, ROWS, 256), held(4, ROWS - NEAR_UP, 256),
             held(WIDE, ROWS), pltpu.VMEM((ROWS, 5 * ROWS), F32),
-            dma((7,)), dma((7,)), dma((2,)), dma,
-            dma((7, 3, 6)), dma((7, 3, 6)), dma((7, 7)), dma((7, 7)), dma((11,)), dma((11,)), dma((4,)),
+            dma((3, 7)), dma((3, 7)), dma, dma((6, 4)), dma((6, 4)),
+            dma((6, 6)), dma((6, 6)), dma((6, 7)), dma((6, 7)), dma((11,)), dma((11,)), dma((4,)),
         ],
         compiler_params=pltpu.CompilerParams(
             collective_id=0, has_side_effects=True, vmem_limit_bytes=62 * 2**20),
         name="front",
-    )(pieces_in, pieces_out, tokens, norm_gain.reshape(1, -1), lengths)
+    )(kv_pieces, query_pieces, out_pieces, tokens, norm_gain.reshape(1, -1), lengths)
     return (*rest, whole_out.reshape(128 * rows_out, WIDE))
 
 
@@ -382,7 +371,7 @@
     read_weight = read(weight_ref, weight, 1)
     read_tokens = read(tokens_ref, x_two, 2)
     read_target = read(target_ref, x_one, 3)
-    read_turned = read(turned_ref, turned, 0)
+    read_turned = [read(turned_ref.at[:, core], turned.at[core], (0, 4)[core]) for core in range(2)]
     greet([twin, up, down, x_flip, x_turn, z_flip, z_turn])
 
     def tile(n):
@@ -399,8 +388,8 @@
         out = dot(prob, tile(2 + g))
         mixed[h] = out.astype(BF16)
         rounded = out.astype(BF16).astype(F32).T.astype(BF16)
-        mixed_turned[2 * h] = rounded[:128]
-        mixed_turned[2 * h + 1] = rounded[128:]
+        mixed_turned[0, h] = rounded[:128]
+        mixed_turned[1, h] = rounded[128:]
         return carry
     lax.fori_loop(0, HEADS, attend, 0)
 
@@ -431,15 +420,14 @@
     def term(k, dst, core):
         kind, n, start, width = CHUNKS[k]
 
-        def body(i, carry):
-            j = 2 * i + core
+        for m in range(2):
             if kind:
-                dst[i] = dot(mixed_turned[j], delta[:, 1280 * n:1280 * n + 1280]).astype(BF16)
+                cols = slice(1280 * n + 640 * m, 1280 * n + 640 * m + 640)
+                part = dot(mixed_turned[core].reshape(512, ROWS), delta[:, cols])
+                dst[:, :, 640 * m:640 * m + 640] = part.astype(BF16).reshape(4, 128, 640)
             else:
-                rows = pl.ds(pl.multiple_of(j * 320, 64), 320)
-                dst[i] = dot(turned[rows, :], joined[n, :, start:start + width]).astype(BF16)
-            return carry
-        lax.fori_loop(0, 4, body, 0)
+                part = dot(turned[core, 2 * m:2 * m + 2].reshape(640, ROWS), joined[n, :, start:start + width])
+                dst[2 * m:2 * m + 2] = part.astype(BF16).reshape(2, 320, width)
 
     def stage_1(k):
         kind, n, start, width = CHUNKS[k]
@@ -461,8 +449,8 @@
 
         def add(block):
             def body(r):
-                sums[block, r, :] = (sums[block, r, :].astype(F32) + extra[block, r, :].astype(F32)).astype(BF16)
-            add_rows(rows, 32, body)
+                sums[block, r, :] = sums[block, r, :] + extra[block, r, :]
+            add_rows(rows, rows // 2, body)
         add(y_far)
         far[k] = (remote(sums.at[y_far, h0], fars.at[0], far_send.at[k, 0], far_recv.at[k, 0], up),
                   remote(sums.at[y_far, h1], fars.at[1], far_send.at[k, 1], far_recv.at[k, 1], down))
@@ -480,18 +468,11 @@
         h0, h1 = pl.ds(0, half), pl.ds(half, half)
         far[k][0].wait_recv()
 
-        def low(r):
-            sums[y_up, r, :] = (sums[y_up, r, :].astype(F32) + fars[0, r, :].astype(F32)).astype(BF16)
-        add_rows(half, 32, low)
+        sums[y_up, h0, :] = sums[y_up, h0, :] + fars[0]
         one = remote(sums.at[y_up, h0], nears.at[0, h0], near_send.at[k, 2], near_recv.at[k, 2], up)
         far[k][1].wait_recv()
 
-        def high(i, carry):
-            r = pl.ds(pl.multiple_of(i * 32, 32), 32)
-            s = pl.ds(pl.multiple_of(i * 32 + half, 32), 32)
-            sums[y_down, s, :] = (sums[y_down, s, :].astype(F32) + fars[1, r, :].astype(F32)).astype(BF16)
-            return carry
-        lax.fori_loop(0, half // 32, high, 0)
+        sums[y_down, h1, :] = sums[y_down, h1, :] + fars[1]
         near_sum[k] = (one, remote(sums.at[y_down, h1], nears.at[1, h1], near_send.at[k, 3], near_recv.at[k, 3], down))
 
     def result(k, query, key, value, out):
@@ -512,7 +493,7 @@
 
         def body(r):
             done[r, :] = (sums[y, r, :].astype(F32) + nears[0, r, :].astype(F32) + nears[1, r, :].astype(F32)).astype(BF16)
-        add_rows(height[kind], 32, body)
+        add_rows(height[kind], height[kind] // 4 if kind else 80, body)
         flips[k] = (remote(done, mates(k, 0), mate_send.at[k, 0], mate_recv.at[k, 0], x_flip),
                     remote(done, mates(k, 2), mate_send.at[k, 2], mate_recv.at[k, 2], z_flip))
         own, cols = result(k, own_query, own_key, own_value, own_out)
@@ -526,15 +507,13 @@
         turns[k] = (one, remote(mates(k, 2), mates(k, 3), mate_send.at[k, 3], mate_recv.at[k, 3], z_turn))
 
     stage_1(0)
-    stage_1(1)
-    stage_2(0)
 
     def spread(h, carry):
         rows = pl.ds(pl.multiple_of(h * 256, 256), 256)
         mixed_grad[h] = dot(delta[...], weight[rows, :], ((1,), (1,))).astype(BF16)
         return carry
     lax.fori_loop(0, HEADS, spread, 0)
-    stage_2(1)
+    stage_2(0)
 
     terms[5 * (1 - c)] = jnp.zeros((4, ROWS, 256), BF16)
 
@@ -556,23 +535,17 @@
     back(0)
     stage_3(0)
     back(1)
-    stage_3(1)
 
     def move(src, dst, n, to):
         return remote(src, dst, term_send.at[n], term_recv.at[n], to)
 
     to_mate = [move(terms.at[2 * n + 1 - c], term_mate.at[n], n, twin) for n in range(3)]
-    stage_4(0)
-    read_turned.wait()
-    stage_1(2)
+    stage_1(1)
 
     def fold(n):
         to_mate[n].wait_recv()
         for q in range(4):
-            def body(r):
-                terms[2 * n + c, q, r, :] = (
-                    terms[2 * n + c, q, r, :].astype(F32) + term_mate[n, q, r, :].astype(F32)).astype(BF16)
-            add_rows(ROWS, 64, body)
+            terms[2 * n + c, q] = terms[2 * n + c, q] + term_mate[n, q]
 
     def part(ref, low, high, start=0):
         return ref.at[:, pl.ds(low - start, high - low), :]
@@ -585,22 +558,23 @@
     fold(1)
     s1 = terms.at[2 + c]
     e1 = move(part(s1, FAR_DOWN, ROWS), part(term_next, FAR_DOWN, ROWS), 6, down)
-    fold(2)
-    stage_1(3)
-    stage_2(2)
+    stage_2(1)
+    for copy in read_turned:
+        copy.wait()
+    stage_1(2)
     e0.wait_recv()
     for q in range(4):
-        def join(r):
-            terms[2 + c, q, r, :] = (terms[2 + c, q, r, :].astype(F32) + term_far[q, r, :].astype(F32)).astype(BF16)
-        add_rows(FAR_DOWN, 16, join)
+        terms[2 + c, q, 0:FAR_DOWN, :] = terms[2 + c, q, 0:FAR_DOWN, :] + term_far[q]
     e2 = move(part(s1, 0, FAR_DOWN), part(term_next, 0, FAR_DOWN), 7, down)
     f0.wait_recv()
     f2 = move(part(term_relay, FAR_DOWN, FAR_MID, FAR_DOWN), part(term_end, FAR_DOWN, FAR_MID, FAR_DOWN), 8, up)
+    fold(2)
     f1.wait_recv()
     f3 = move(part(term_relay, FAR_MID, ROWS, FAR_DOWN), part(term_end, FAR_MID, ROWS, FAR_DOWN), 9, up)
-    stage_4(1)
-    stage_2(3)
-    stage_5(0)
+    stage_2(2)
+    stage_4(0)
+    stage_3(1)
+    stage_1(3)
     stage_3(2)
     for copy in (e1, e2, f2, f3):
         copy.wait_recv()
@@ -611,15 +585,15 @@
         joined[n, FAR_DOWN:ROWS, 256 * g:256 * g + 256] = (
             terms[4 + c, q, FAR_DOWN:ROWS, :].astype(F32) + term_next[q, FAR_DOWN:ROWS, :].astype(F32)
             + term_end[q].astype(F32)).astype(BF16)
-    order = ((1, 4), (1, 5), (2, 4), (1, 6), (3, 3), (2, 5), (4, 2), (5, 1), (2, 6), (3, 4), (4, 3), (5, 2), (3, 5),
-             (3, 6), (4, 4), (5, 3), (4, 5), (5, 4), (4, 6), (5, 5), (5, 6))
+    order = ((2, 3), (1, 4), (4, 1), (5, 0), (2, 4), (3, 3), (1, 5), (4, 2), (5, 1), (2, 5), (3, 4), (1, 6), (4, 3), (5, 2),
+             (2, 6), (3, 5), (1, 7), (4, 4), (5, 3), (2, 7), (3, 6), (4, 5), (5, 4), (3, 7), (4, 6), (5, 5), (4, 7), (5, 6), (5, 7))
     for stage, k in order:
         (stage_1, stage_2, stage_3, stage_4, stage_5)[stage - 1](k)
     for k in range(len(CHUNKS)):
         turns[k][0].wait_recv()
         turns[k][1].wait_recv()
         keeps[k].wait()
-    for k in (0, 1, 4, 5, 6):
+    for k in (0, 1, 4, 5, 6, 7):
         swaps[k].wait_send()
     for copy in sent:
         copy.wait_send()
@@ -645,19 +619,19 @@
             held(HEADS, ROWS, 5 * ROWS), held(2, ROWS, 5 * ROWS),
             held(6, 4, ROWS, 256), held(3, 4, ROWS, 256), held(4, ROWS, 256), held(4, FAR_DOWN, 256),
             held(4, ROWS - FAR_DOWN, 256), held(4, ROWS - FAR_DOWN, 256),
-            held(ROWS, WIDE), held(ROWS, WIDE), held(HEADS * 256, WIDE), held(WIDE, ROWS),
-            held(HEADS, ROWS, 256), held(8, 128, ROWS), held(HEADS, ROWS, 256), held(4, ROWS, 512),
+            held(ROWS, WIDE), held(ROWS, WIDE), held(HEADS * 256, WIDE), held(2, 4, WIDE // 8, ROWS),
+            held(HEADS, ROWS, 256), held(2, 4, 128, ROWS), held(HEADS, ROWS, 256), held(4, ROWS, 512),
             held(2, 4, ri, 512), held(2, 4, ro, 1280),
             held(4, 4, ri, 512), held(2, 4, ro, 1280), held(4, 4, ri, 512), held(2, 4, ro, 1280),
             held(4, 2, ri // 2, 512), held(2, 2, ro // 2, 1280), held(4, 2, ri, 512), held(2, 2, ro, 1280),
             held(4, ri, 512), held(2, ro, 1280),
-            dma((4,)), dma((10,)), dma((10,)), dma((n,)), dma((n,)),
+            dma((5,)), dma((10,)), dma((10,)), dma((n,)), dma((n,)),
             dma((n, 2)), dma((n, 2)), dma((n, 4)), dma((n, 4)), dma((n, 4)), dma((n, 4)), dma((n,)),
         ],
         compiler_params=pltpu.CompilerParams(
             collective_id=1, has_side_effects=True, vmem_limit_bytes=62 * 2**20),
         name="layer_grads",
-    )(queries, kv, mask, rewards, turned, tokens, target, weight)
+    )(queries, kv, mask, rewards, turned.reshape(4, 2, WIDE // 8, ROWS), tokens, target, weight)
 
 
 def per_device(

time: 203 us -> 197 us (0.970)
  Pallas kernels: 188 us -> 182 us
    pallas_call x1, Pallas kernels: 120 us -> 117 us  [layer_grads(): pl.pallas_call(layer_kernel, out_shape=tuple((jax.ShapeDtypeStruct(shape,...]
    pallas_call x1, Pallas kernels: 68.2 us -> 65.4 us  [front(): pl.pallas_call(functools.partial(front_kernel, rows_in, rows_out), out_sh...]
    pad x2 -> x0, local copies, waits for them, and re-layouts: 2.09 us -> none  [the longest x1 1.42 us: front(): jnp.pad(w_out.reshape(rows_out, 2, 1280).transpose(1, 0, 2), ((0, 0), (0,...]
    another operation x0 -> x2, other arithmetic: none -> 2.06 us  [the longest x1 1.42 us: front(): kv_pieces = jnp.pad(jnp.stack([w_key, w_value]), ((0, 0), pad_in, (0, 0)))]
    broadcast_in_dim x3 -> x4, other arithmetic: 6.69 us -> 7.29 us  [mean(): return ((own.astype(F32) + partner.astype(F32)) * 0.5)[None]]
where the time goes in v4:
time: 197 us
  Pallas kernels  182 us (92%)
  other arithmetic  9.35 us (5%)
  local copies, waits for them, and re-layouts  4.21 us (2%)
    pallas_call x1, Pallas kernels, layer_grads(): pl.pallas_call(layer_kernel, out_shape=tuple((jax.ShapeDtypeStruct(shape,...  117 us
    pallas_call x1, Pallas kernels, front(): pl.pallas_call(functools.partial(front_kernel, rows_in, rows_out), out_sh...  65.4 us
    broadcast_in_dim x4, other arithmetic, mean(): return ((own.astype(F32) + partner.astype(F32)) * 0.5)[None]  7.29 us

profile of v4, /device:TPU:0, one launch (start us, length us, event | category | flops | bytes accessed | tf_op | source)
XLA Modules:
  0.0 197.1 jit_solution(8948641022770048535)
XLA Ops:
  0.6 0.0 copy-start.6
  0.6 0.8 slice_bitcast_fusion.1
  1.4 1.4 fusion.15
  2.8 0.7 slice_bitcast_fusion.3
  3.6 0.6 fusion.14.out_ref
  4.2 1.3 reshape.58.gain_ref
  5.5 65.4 %front.1 = (bf16[4,256,256]{2,1,0:T(8,128)(2,1)}, bf16[6,4,256,256]{3,2,1,0:T(8,128)(2,1)}, bf16[2560,256]{1,0:T(8,128)(2,1)}, f32[256,1280]{1,0:T(8,128)}, bf16[4,4,64,2560]{3,2,1,0:T(8,128)(2,1)}) custom-call(bf16[2,32,512]{2,1,0:T(8,128)(2,1)} %get-tuple-element.34.kv_ref, bf16[2,32,512]{2,1,0:T(8,128)(2,1)} %get-tuple-element.35.query_ref, ...), custom_call_target="tpu_custom_call" | custom-call | tf_op jit(solution)/shard_map/front/pallas_call | solution.py:316
  71.0 0.0 copy-done.6
  71.0 0.8 copy.14.rewards_ref
  71.8 116.7 %layer_grads.1 = (bf16[320,1024]{1,0:T(8,128)(2,1)}, bf16[320,512]{1,0:T(8,128)(2,1)}, bf16[320,512]{1,0:T(8,128)(2,1)}, bf16[128,2560]{1,0:T(8,128)(2,1)}, bf16...) custom-call(bf16[4,256,256]{2,1,0:T(8,128)(2,1)} %get-tuple-element., ...), custom_call_target="tpu_custom_call" | custom-call | tf_op jit(solution)/shard_map/layer_grads/pallas_call | solution.py:612
  189.1 0.0 copy-start.2
  189.2 0.0 copy-start.5
  189.2 0.0 copy-start.4
  189.2 3.5 %fusion.1 = f32[1,128,2560]{2,1,0:T(8,128)} fusion(bf16[128,2560]{1,0:T(8,128)(2,1)} %get-tuple-element.28, bf16[4,128,2560]{2,1,0:T(8,128)(2,1)} %get-tuple-element.29, pred[]{:T(512)} %bitcast.14, pred[]{:T(512)} %bitcast.13, pred[]{:T(512)} %bitcast.12), kind=kLoop, calls=%fused_computation.2 | loop fusion | flops 2293760 | bytes 4587523 | tf_op jit(solution)/shard_map/broadcast_in_dim | solution.py:653
  192.7 0.0 copy-start.1
  192.7 0.0 copy-done.2
  192.7 0.0 copy-done.5
  192.7 0.0 copy-start
  192.7 1.1 fusion.5
  193.8 0.0 copy-start.3
  193.8 0.0 copy-done.4
  193.8 0.5 copy-done.1
  194.2 1.1 fusion.7
  195.3 0.0 copy-done
  195.3 0.1 copy-done.3
  195.4 1.7 fusion.3
Async XLA Ops:
  0.6 70.4 %copy-start.6 = (f32[1,1,256]{2,1,0:T(1,128)S(1)}, f32[1,1,256]{2,1,0:T(1,128)}, u32[]{:S(2)}) copy-start(f32[1,1,256]{2,1,0:T(1,128)} %param.12) | copy-start | bytes 3076
  189.1 3.5 %copy-start.2 = (bf16[4,320,512]{2,1,0:T(8,128)(2,1)S(1)}, bf16[4,320,512]{2,1,0:T(8,128)(2,1)}, u32[]{:S(2)}) copy-start(bf16[4,320,512]{2,1,0:T(8,128)(2,1)} %get-tuple-element.27) | copy-start | bytes 3932164
  189.2 3.5 %copy-start.5 = (bf16[320,512]{1,0:T(8,128)(2,1)S(1)}, bf16[320,512]{1,0:T(8,128)(2,1)}, u32[]{:S(2)}) copy-start(bf16[320,512]{1,0:T(8,128)(2,1)} %get-tuple-element.26) | copy-start | bytes 983044
  189.2 4.6 %copy-start.4 = (bf16[320,512]{1,0:T(8,128)(2,1)S(1)}, bf16[320,512]{1,0:T(8,128)(2,1)}, u32[]{:S(2)}) copy-start(bf16[320,512]{1,0:T(8,128)(2,1)} %get-tuple-element.24) | copy-start | bytes 983044
  192.7 1.6 copy-start.1
  192.7 2.6 %copy-start = (bf16[4,320,1024]{2,1,0:T(8,128)(2,1)S(1)}, bf16[4,320,1024]{2,1,0:T(8,128)(2,1)}, u32[]{:S(2)}) copy-start(bf16[4,320,1024]{2,1,0:T(8,128)(2,1)} %get-tuple-element.23) | copy-start | bytes 7864324
  193.8 1.6 copy-start.3

commit v5 on v4

--- a/solution.py
+++ b/solution.py
@@ -340,9 +340,9 @@
     return (*rest, whole_out.reshape(128 * rows_out, WIDE))
 
 
-def layer_kernel(queries, kv, mask_ref, rewards_ref, turned_ref, tokens_ref, target_ref, weight_ref,
+def layer_kernel(queries_in, kv_in, mask_in, rewards_ref, turned_ref, tokens_ref, target_ref, weight_ref,
                  own_query, own_key, own_value, own_out, mate_query, mate_key, mate_value, mate_out, *scratch):
-    (probs, scores, terms, term_mate, term_next, term_far, term_relay, term_end, x_one, x_two,
+    (queries, kv, mask_ref, probs, scores, terms, term_mate, term_next, term_far, term_relay, term_end, x_one, x_two,
      weight, turned, mixed, mixed_turned, mixed_grad, joined,
      give_in, give_out, sum_in, sum_out, twin_in, twin_out, far_in, far_out, near_in, near_out, done_in, done_out,
      read_sem, term_send, term_recv, twin_send, twin_recv,
@@ -368,11 +368,15 @@
         copy.start()
         return copy
 
+    read_operands = [read(queries_in, queries, 5), read(kv_in, kv, 6), read(mask_in, mask_ref, 7)]
     read_weight = read(weight_ref, weight, 1)
     read_tokens = read(tokens_ref, x_two, 2)
     read_target = read(target_ref, x_one, 3)
     read_turned = [read(turned_ref.at[:, core], turned.at[core], (0, 4)[core]) for core in range(2)]
     greet([twin, up, down, x_flip, x_turn, z_flip, z_turn])
+
+    for copy in read_operands:
+        copy.wait()
 
     def tile(n):
         return kv[pl.ds(c, 5), n].reshape(5 * ROWS, 256)
@@ -613,9 +617,10 @@
         layer_kernel,
         out_shape=tuple(jax.ShapeDtypeStruct(shape, BF16) for shape in results)
         + tuple(jax.ShapeDtypeStruct((4, *shape), BF16) for shape in results),
-        in_specs=[vmem, vmem, vmem, vmem, hbm, hbm, hbm, hbm],
+        in_specs=[hbm, hbm, hbm, vmem, hbm, hbm, hbm, hbm],
         out_specs=(hbm,) * 8,
         scratch_shapes=[
+            held(HEADS, ROWS, 256), held(6, 4, ROWS, 256), pltpu.VMEM((ROWS, 5 * ROWS), F32),
             held(HEADS, ROWS, 5 * ROWS), held(2, ROWS, 5 * ROWS),
             held(6, 4, ROWS, 256), held(3, 4, ROWS, 256), held(4, ROWS, 256), held(4, FAR_DOWN, 256),
             held(4, ROWS - FAR_DOWN, 256), held(4, ROWS - FAR_DOWN, 256),
@@ -625,7 +630,7 @@
             held(4, 4, ri, 512), held(2, 4, ro, 1280), held(4, 4, ri, 512), held(2, 4, ro, 1280),
             held(4, 2, ri // 2, 512), held(2, 2, ro // 2, 1280), held(4, 2, ri, 512), held(2, 2, ro, 1280),
             held(4, ri, 512), held(2, ro, 1280),
-            dma((5,)), dma((10,)), dma((10,)), dma((n,)), dma((n,)),
+            dma((8,)), dma((10,)), dma((10,)), dma((n,)), dma((n,)),
             dma((n, 2)), dma((n, 2)), dma((n, 4)), dma((n, 4)), dma((n, 4)), dma((n, 4)), dma((n,)),
         ],
         compiler_params=pltpu.CompilerParams(

time: 197 us -> 197 us (level)
  no operation moved by 1% of the time
where the time goes in v5:
time: 197 us
  Pallas kernels  182 us (92%)
  other arithmetic  9.35 us (5%)
  local copies, waits for them, and re-layouts  4.21 us (2%)
    pallas_call x1, Pallas kernels, layer_grads(): pl.pallas_call(layer_kernel, out_shape=tuple((jax.ShapeDtypeStruct(shape,...  116 us
    pallas_call x1, Pallas kernels, front(): pl.pallas_call(functools.partial(front_kernel, rows_in, rows_out), out_sh...  65.4 us
    broadcast_in_dim x4, other arithmetic, mean(): return ((own.astype(F32) + partner.astype(F32)) * 0.5)[None]  7.29 us

profile of v5, /device:TPU:0, one launch (start us, length us, event | category | flops | bytes accessed | tf_op | source)
XLA Modules:
  0.0 196.6 jit_solution(12658123972388767894)
XLA Ops:
  0.6 0.0 copy-start.6
  0.6 0.8 slice_bitcast_fusion.1
  1.4 1.4 fusion.15
  2.8 0.7 slice_bitcast_fusion.3
  3.6 0.6 fusion.14.out_ref
  4.2 1.3 reshape.58.gain_ref
  5.5 65.4 %front.1 = (bf16[4,256,256]{2,1,0:T(8,128)(2,1)}, bf16[6,4,256,256]{3,2,1,0:T(8,128)(2,1)}, bf16[2560,256]{1,0:T(8,128)(2,1)}, f32[256,1280]{1,0:T(8,128)}, bf16[4,4,64,2560]{3,2,1,0:T(8,128)(2,1)}) custom-call(bf16[2,32,512]{2,1,0:T(8,128)(2,1)} %get-tuple-element.34.kv_ref, bf16[2,32,512]{2,1,0:T(8,128)(2,1)} %get-tuple-element.35.query_ref, ...), custom_call_target="tpu_custom_call" | custom-call | tf_op jit(solution)/shard_map/front/pallas_call | solution.py:316
  71.0 0.0 copy-done.6
  71.0 0.8 copy.14.rewards_ref
  71.8 116.2 %layer_grads.1 = (bf16[320,1024]{1,0:T(8,128)(2,1)}, bf16[320,512]{1,0:T(8,128)(2,1)}, bf16[320,512]{1,0:T(8,128)(2,1)}, bf16[128,2560]{1,0:T(8,128)(2,1)}, bf16...) custom-call(bf16[4,256,256]{2,1,0:T(8,128)(2,1)} %get-tuple-element., ...), custom_call_target="tpu_custom_call" | custom-call | tf_op jit(solution)/shard_map/layer_grads/pallas_call | solution.py:616
  188.7 0.0 copy-start.2
  188.7 0.0 copy-start.5
  188.7 0.0 copy-start.4
  188.7 3.5 %fusion.1 = f32[1,128,2560]{2,1,0:T(8,128)} fusion(bf16[128,2560]{1,0:T(8,128)(2,1)} %get-tuple-element.28, bf16[4,128,2560]{2,1,0:T(8,128)(2,1)} %get-tuple-element.29, pred[]{:T(512)} %bitcast.14, pred[]{:T(512)} %bitcast.13, pred[]{:T(512)} %bitcast.12), kind=kLoop, calls=%fused_computation.2 | loop fusion | flops 2293760 | bytes 4587523 | tf_op jit(solution)/shard_map/broadcast_in_dim | solution.py:658
  192.2 0.0 copy-start.1
  192.2 0.0 copy-done.2
  192.2 0.0 copy-done.5
  192.2 0.0 copy-start
  192.2 1.1 fusion.5
  193.3 0.0 copy-start.3
  193.3 0.0 copy-done.4
  193.3 0.5 copy-done.1
  193.8 1.1 fusion.7
  194.8 0.0 copy-done
  194.8 0.1 copy-done.3
  194.9 1.7 fusion.3
Async XLA Ops:
  0.6 70.4 %copy-start.6 = (f32[1,1,256]{2,1,0:T(1,128)S(1)}, f32[1,1,256]{2,1,0:T(1,128)}, u32[]{:S(2)}) copy-start(f32[1,1,256]{2,1,0:T(1,128)} %param.12) | copy-start | bytes 3076
  188.7 3.5 %copy-start.2 = (bf16[4,320,512]{2,1,0:T(8,128)(2,1)S(1)}, bf16[4,320,512]{2,1,0:T(8,128)(2,1)}, u32[]{:S(2)}) copy-start(bf16[4,320,512]{2,1,0:T(8,128)(2,1)} %get-tuple-element.27) | copy-start | bytes 3932164
  188.7 3.5 %copy-start.5 = (bf16[320,512]{1,0:T(8,128)(2,1)S(1)}, bf16[320,512]{1,0:T(8,128)(2,1)}, u32[]{:S(2)}) copy-start(bf16[320,512]{1,0:T(8,128)(2,1)} %get-tuple-element.26) | copy-start | bytes 983044
  188.7 4.6 %copy-start.4 = (bf16[320,512]{1,0:T(8,128)(2,1)S(1)}, bf16[320,512]{1,0:T(8,128)(2,1)}, u32[]{:S(2)}) copy-start(bf16[320,512]{1,0:T(8,128)(2,1)} %get-tuple-element.24) | copy-start | bytes 983044
  192.2 1.6 copy-start.1
  192.2 2.6 %copy-start = (bf16[4,320,1024]{2,1,0:T(8,128)(2,1)S(1)}, bf16[4,320,1024]{2,1,0:T(8,128)(2,1)}, u32[]{:S(2)}) copy-start(bf16[4,320,1024]{2,1,0:T(8,128)(2,1)} %get-tuple-element.23) | copy-start | bytes 7864324
  193.3 1.6 copy-start.3

commit v6 on v5

--- a/solution.py
+++ b/solution.py
@@ -97,7 +97,7 @@
         r = pl.ds(pl.multiple_of(i * 32, 32), 32)
         values = tokens_ref[r, :].astype(F32)
         power = jnp.mean(values * values, axis=1, keepdims=True)
-        x_ref[r, :] = (values * lax.rsqrt(power + epsilon) * gain_ref[...]).astype(BF16)
+        x_ref[r, :] = (values * lax.rsqrt(power + epsilon) * gain_ref[...].reshape(1, WIDE)).astype(BF16)
         return carry
 
     def merged(slots, rows, copies):
@@ -336,7 +336,7 @@
         compiler_params=pltpu.CompilerParams(
             collective_id=0, has_side_effects=True, vmem_limit_bytes=62 * 2**20),
         name="front",
-    )(kv_pieces, query_pieces, out_pieces, tokens, norm_gain.reshape(1, -1), lengths)
+    )(kv_pieces, query_pieces, out_pieces, tokens, norm_gain, lengths)
     return (*rest, whole_out.reshape(128 * rows_out, WIDE))
 
 
@@ -400,11 +400,13 @@
     for copy in (read_weight, read_tokens, read_target):
         copy.wait()
 
+    reward = jnp.broadcast_to(rewards_ref[...], (128, ROWS)).T[:, :1]
+
     def error(i, carry):
         cols = pl.ds(pl.multiple_of(i * 512, 512), 512)
         update = sum(dot(mixed[h], weight[256 * h:256 * h + 256, cols]) for h in range(HEADS))
         result = x_two[:, cols].astype(F32) + update
-        x_two[:, cols] = (rewards_ref[...] * (result - x_one[:, cols].astype(F32))).astype(BF16)
+        x_two[:, cols] = (reward * (result - x_one[:, cols].astype(F32))).astype(BF16)
         return carry
     lax.fori_loop(0, WIDE // 512, error, 0)
     delta = x_two
@@ -647,7 +649,7 @@
         token_rows, norm_gain, doc_lengths[0], w_query, w_key, w_value, w_out
     )
     results = layer_grads(
-        queries, kv, mask, rewards.reshape(ROWS, 1), turned, token_rows, target_rows, out_whole
+        queries, kv, mask, rewards.reshape(1, ROWS), turned, token_rows, target_rows, out_whole
     )
     own_bit = gossip_bit[0]
 

time: 197 us -> 195 us (0.990)
  local copies, waits for them, and re-layouts: 4.21 us -> 2.09 us
    reshape x2 -> x0, local copies, waits for them, and re-layouts: 2.11 us -> none  [the longest x1 1.31 us: front(): norm_gain.reshape(1, -1)]
where the time goes in v6:
time: 195 us
  Pallas kernels  182 us (93%)
  other arithmetic  9.35 us (5%)
  local copies, waits for them, and re-layouts  2.09 us (1%)
    pallas_call x1, Pallas kernels, layer_grads(): pl.pallas_call(layer_kernel, out_shape=tuple((jax.ShapeDtypeStruct(shape,...  116 us
    pallas_call x1, Pallas kernels, front(): pl.pallas_call(functools.partial(front_kernel, rows_in, rows_out), out_sh...  65.4 us
    broadcast_in_dim x4, other arithmetic, mean(): return ((own.astype(F32) + partner.astype(F32)) * 0.5)[None]  7.29 us

profile of v6, /device:TPU:0, one launch (start us, length us, event | category | flops | bytes accessed | tf_op | source)
XLA Modules:
  0.0 194.6 jit_solution(9886548881599920619)
XLA Ops:
  0.6 0.8 slice_bitcast_fusion.1
  1.4 1.4 fusion.15
  2.8 0.7 slice_bitcast_fusion.3
  3.6 0.6 fusion.14.out_ref
  4.2 65.4 %front.1 = (bf16[4,256,256]{2,1,0:T(8,128)(2,1)}, bf16[6,4,256,256]{3,2,1,0:T(8,128)(2,1)}, bf16[2560,256]{1,0:T(8,128)(2,1)}, f32[256,1280]{1,0:T(8,128)}, bf16[4,4,64,2560]{3,2,1,0:T(8,128)(2,1)}) custom-call(bf16[2,32,512]{2,1,0:T(8,128)(2,1)} %get-tuple-element.34.kv_ref, bf16[2,32,512]{2,1,0:T(8,128)(2,1)} %get-tuple-element.35.query_ref, ...), custom_call_target="tpu_custom_call" | custom-call | tf_op jit(solution)/shard_map/front/pallas_call | solution.py:316
  69.7 116.4 %layer_grads.1 = (bf16[320,1024]{1,0:T(8,128)(2,1)}, bf16[320,512]{1,0:T(8,128)(2,1)}, bf16[320,512]{1,0:T(8,128)(2,1)}, bf16[128,2560]{1,0:T(8,128)(2,1)}, bf16...) custom-call(bf16[4,256,256]{2,1,0:T(8,128)(2,1)} %get-tuple-element., ...), custom_call_target="tpu_custom_call" | custom-call | tf_op jit(solution)/shard_map/layer_grads/pallas_call | solution.py:618
  186.7 0.0 copy-start.2
  186.7 0.0 copy-start.5
  186.7 0.0 copy-start.4
  186.8 3.5 %fusion.1 = f32[1,128,2560]{2,1,0:T(8,128)} fusion(bf16[128,2560]{1,0:T(8,128)(2,1)} %get-tuple-element.28, bf16[4,128,2560]{2,1,0:T(8,128)(2,1)} %get-tuple-element.29, pred[]{:T(512)} %bitcast.14, pred[]{:T(512)} %bitcast.13, pred[]{:T(512)} %bitcast.12), kind=kLoop, calls=%fused_computation.2 | loop fusion | flops 2293760 | bytes 4587523 | tf_op jit(solution)/shard_map/broadcast_in_dim | solution.py:660
  190.3 0.0 copy-start.1
  190.3 0.0 copy-done.2
  190.3 0.0 copy-done.5
  190.3 0.0 copy-start
  190.3 1.1 fusion.5
  191.3 0.0 copy-start.3
  191.3 0.0 copy-done.4
  191.3 0.5 copy-done.1
  191.8 1.1 fusion.7
  192.9 0.0 copy-done
  192.9 0.1 copy-done.3
  193.0 1.7 fusion.3
Async XLA Ops:
  186.7 3.5 %copy-start.2 = (bf16[4,320,512]{2,1,0:T(8,128)(2,1)S(1)}, bf16[4,320,512]{2,1,0:T(8,128)(2,1)}, u32[]{:S(2)}) copy-start(bf16[4,320,512]{2,1,0:T(8,128)(2,1)} %get-tuple-element.27) | copy-start | bytes 3932164
  186.7 3.5 %copy-start.5 = (bf16[320,512]{1,0:T(8,128)(2,1)S(1)}, bf16[320,512]{1,0:T(8,128)(2,1)}, u32[]{:S(2)}) copy-start(bf16[320,512]{1,0:T(8,128)(2,1)} %get-tuple-element.26) | copy-start | bytes 983044
  186.7 4.6 %copy-start.4 = (bf16[320,512]{1,0:T(8,128)(2,1)S(1)}, bf16[320,512]{1,0:T(8,128)(2,1)}, u32[]{:S(2)}) copy-start(bf16[320,512]{1,0:T(8,128)(2,1)} %get-tuple-element.24) | copy-start | bytes 983044
  190.3 1.6 copy-start.1
  190.3 2.6 %copy-start = (bf16[4,320,1024]{2,1,0:T(8,128)(2,1)S(1)}, bf16[4,320,1024]{2,1,0:T(8,128)(2,1)}, u32[]{:S(2)}) copy-start(bf16[4,320,1024]{2,1,0:T(8,128)(2,1)} %get-tuple-element.23) | copy-start | bytes 7864324
  191.3 1.6 copy-start.3
